TPU v7x, 128 devices: a whole 4x4x4 slice. The times are simulated.
128 devices in a mesh: blk: 8 (over x, core), feat: 16 (over y, z).
Axes of the slice: x: 4, y: 4, z: 4, core: 2. Of those that a mesh axis runs over, the one named last changes fastest.
Arguments:
- features: bfloat16 [128, 131072], P(('blk', 'feat')), may hold values from -24 to 24
- w_self: bfloat16 [128, 256], replicated, may hold values from -0.5 to 0.5
- w_neigh: bfloat16 [128, 256], replicated, may hold values from -0.5 to 0.5
- adjacency_tiles: bfloat16 [1024, 8, 128, 128], P(('blk', 'feat')), as said below
- tile_columns: int32 [1024, 8], P(('blk', 'feat')), may hold values from 0 to 127, as said below
- tile_count: int32 [1024], P(('blk', 'feat')), may hold values from 1 to 8
- cotangent: bfloat16 [131072, 256], P(('blk', 'feat')), may hold values from -0.08984375 to 0.08984375
Outputs:
- hidden_out: bfloat16 [131072, 256], P(('blk', 'feat'))
- grad_self: float32 [128, 256], replicated
- grad_neigh: float32 [128, 256], replicated
Inputs may be any that keep to these rules, and one draw needn't show every extreme that they name: `adjacency_tiles`: nonnegative adjacency weights; slots at or beyond tile_count are not used. `tile_columns`: the 8 column blocks of a row block are distinct.
All inputs are finite; a program needn't handle non-finite values.
Results may differ from a plain program's by a relative error of at most 0.0055.
Values may be sent and summed in bfloat16 or wider, within the bound.
No kernel may reach another device: no remote copies, remote signals or barrier semaphores. Data moves between devices by JAX's collectives and lax.ppermute only.
A program may use at most 128 MiB of HBM per device.

v0:
```python
import math

import jax
import jax.numpy as jnp
from jax import lax
from jax.sharding import PartitionSpec as P


def column_match(adjacency_tiles, tile_columns, tile_count, first_row, piece_width):
    block_count, tile_slots, block_size, _ = adjacency_tiles.shape
    piece_blocks = piece_width // block_size
    column_ids = first_row // block_size + jnp.arange(piece_blocks, dtype=jnp.int32)
    live_slot = jnp.arange(tile_slots, dtype=jnp.int32)[None, :] < tile_count[:, None]
    matches = (tile_columns[:, :, None] == column_ids[None, None, :]) & live_slot[:, :, None]
    matches = matches.astype(jnp.bfloat16)
    table = jnp.einsum(
        "btc,btij->bicj", matches, adjacency_tiles, preferred_element_type=jnp.float32
    )
    return table.reshape(block_count * block_size, piece_width).astype(jnp.bfloat16)


def column_table(adjacency_tiles, tile_columns, tile_count, first_row, piece_width):
    return column_match(adjacency_tiles, tile_columns, tile_count, first_row, piece_width)


def blocked_fold(running, shard_rows, node_rows, step_fn):
    width = shard_rows.shape[0]
    step = math.gcd(width, node_rows)

    def one_step(k, carry):
        start = k * step
        rows_here = lax.dynamic_slice_in_dim(shard_rows, start, step, 0)
        return step_fn(carry, rows_here, start, step)

    return lax.fori_loop(0, width // step, one_step, running)


def per_device(features, w_self, w_neigh, adjacency_tiles, tile_columns, tile_count, cotangent):
    hidden = w_self.shape[1]
    node_rows = cotangent.shape[0]
    w_both = jnp.concatenate([w_self, w_neigh], axis=1)
    contract_first = (((0,), (0,)), ((), ()))
    node_features = lax.all_to_all(
        features, ("blk", "feat"), split_axis=1, concat_axis=0, tiled=True
    )
    projected = lax.dot_general(
        node_features, w_both, contract_first, preferred_element_type=jnp.float32
    ).astype(jnp.bfloat16)
    z_self = projected[:, :hidden]
    z_neigh = projected[:, hidden:]

    def add_neighbours(running, rows_here, first_row, width):
        table = column_table(adjacency_tiles, tile_columns, tile_count, first_row, width)
        return running + jnp.dot(table, rows_here, preferred_element_type=jnp.float32)

    aggregated = blocked_fold(
        jnp.zeros((node_rows, hidden), jnp.float32),
        lax.all_gather(z_neigh, "feat", axis=0, tiled=True),
        node_rows,
        add_neighbours,
    )
    pre_act = z_self.astype(jnp.float32) + aggregated
    hidden_out = jax.nn.silu(pre_act).astype(jnp.bfloat16)
    sigmoid_pre = jax.nn.sigmoid(pre_act)
    grad_pre = (
        cotangent.astype(jnp.float32) * sigmoid_pre * (1.0 + pre_act * (1.0 - sigmoid_pre))
    ).astype(jnp.bfloat16)
    partial_self = jnp.dot(node_features, grad_pre, preferred_element_type=jnp.float32)
    pieces = node_rows * lax.axis_size("feat") // node_rows

    def one_piece(index):
        table = column_table(
            adjacency_tiles, tile_columns, tile_count, index * node_rows, node_rows
        )
        return lax.dot_general(table, grad_pre, contract_first, preferred_element_type=jnp.float32)

    stacked = lax.map(one_piece, jnp.arange(pieces, dtype=jnp.int32))
    grad_zn = lax.psum_scatter(
        stacked.reshape(node_rows * lax.axis_size("feat"), hidden),
        "feat",
        scatter_dimension=0,
        tiled=True,
    )
    partial_neigh = jnp.dot(
        node_features.astype(jnp.float32),
        grad_zn,
        precision=lax.Precision.HIGHEST,
        preferred_element_type=jnp.float32,
    )
    grad_self, grad_neigh = lax.psum((partial_self, partial_neigh), ("blk", "feat"))
    return (hidden_out, grad_self, grad_neigh)


def solution(mesh):
    return jax.shard_map(
        per_device,
        mesh=mesh,
        in_specs=(
            P(("blk", "feat"), None),
            P(),
            P(),
            P(("blk", "feat"), None, None, None),
            P(("blk", "feat"), None),
            P(("blk", "feat")),
            P(("blk", "feat"), None),
        ),
        out_specs=(P(("blk", "feat"), None), P(), P()),
        check_vma=False,
    )
```

profile of v0, /device:TPU:1, one launch (start us, length us, event | category | flops | bytes accessed | tf_op | source)
XLA Modules:
  0.0 511.7 jit_solution(14051999147701093096)
XLA Ops:
  7.7 3.1 reduce
  11.1 22.5 %all_to_all.16 = bf16[128,2,512]{2,1,0:T(2,128)(2,1)S(1)} all-to-all(bf16[128,2,512]{2,1,0:T(2,128)(2,1)S(1)} %reshape.86), channel_id=1, replica_groups=mesh['blk'=8,'feat'=16] {'blk','feat'}, dimensions={0} | all-to-all | bytes 524288 | tf_op jit(solution)/shard_map/all_to_all | solution.py:43
  36.6 3.0 copy.28
  39.6 62.6 %all-gather.2.cloned.1.call-done = bf16[16384,256]{0,1:T(8,128)(2,1)} async-done(((bf16[1024,256]{0,1:T(8,128)(2,1)}), bf16[16384,256]{0,1:T(8,128)(2,1)}) %all-gather.2.cloned.1.call-update) | async-done | bytes 8388624 | tf_op jit(solution)/shard_map/all_gather | solution.py:58
  102.2 69.8 %while.29 = (s32[]{:T(128)}, f32[1024,256]{1,0:T(8,128)}, s32[8,8]{1,0:T(8,128)S(1)}, s32[8]{0:T(128)S(1)}, bf16[8,8,128,128]{3,1,2,0:T(8,128)(2,1)S(1)}, /*inde...) while((s32[]{:T(128)}, f32[1024,256]{1,0:T(8,128)}, ...), condition=%wide.region_1.2_spmd.clone, body=%wide.region_0.1_spmd.clone.sunk | while | flops 555222080 | bytes 17302376 | solution.py:35
  103.5 2.1 fusion.64
  107.9 2.1 fusion.64
  116.6 2.1 fusion.64
  121.0 2.1 fusion.64
  125.3 2.1 fusion.64
  129.7 2.1 fusion.64
  134.0 2.1 fusion.64
  138.4 2.1 fusion.64
  142.8 2.1 fusion.64
  147.1 2.1 fusion.64
  155.8 2.1 fusion.64
  160.2 2.1 fusion.64
  164.6 2.1 fusion.64
  172.0 2.5 copy.30
  174.5 2.8 multiply_convert_fusion
  178.3 66.2 %while.28 = (s32[]{:T(128)}, f32[16,1024,256]{2,1,0:T(8,128)}, s32[8,8]{1,0:T(8,128)S(1)}, s32[16]{0:T(128)S(1)}, s32[8]{0:T(128)S(1)}, /*index=5*/bf16[8,8,128,...) while((s32[]{:T(128)}, f32[16,1024,256]{2,1,0:T(8,128)}, ...), condition=%wide.region_4.5_spmd, body=%wide.region_3.4_spmd.sunk | while | flops 554697792 | bytes 9962295 | solution.py:77
  245.6 109.2 %reduce-scatter.2.cloned.1.call-done = f32[1024,256]{1,0:T(8,128)} async-done(((f32[16384,256]{1,0:T(8,128)}), f32[1024,256]{1,0:T(8,128)}) %reduce-scatter.2.cloned.1.call-update) | async-done | bytes 1048592 | tf_op jit(solution)/shard_map/reduce_scatter | solution.py:78
  354.8 2.9 convolution_bitcast_fusion.1
  358.7 143.2 %all-reduce.3.cloned.1.call-done = (f32[128,256]{0,1:T(8,128)}, f32[128,256]{0,1:T(8,128)}) async-done(((f32[128,256]{0,1:T(8,128)}, f32[128,256]{0,1:T(8,128)}), (f32[128,256]{0,1:T(8,128)}, f32[128,256]{0,1:T(8,128)})) %all-reduce.3.cloned.1.call-update) | async-done | bytes 262160 | tf_op jit(solution)/shard_map/psum | solution.py:90
  (261 shorter events, 107.6 us)
Async XLA Ops:
  7.2 26.7 %copy-start.7 = (bf16[128,256]{1,0:T(8,128)(2,1)S(1)}, bf16[128,256]{1,0:T(8,128)(2,1)}, u32[]{:S(2)}) copy-start(bf16[128,256]{1,0:T(8,128)(2,1)} %param.13) | copy-start | bytes 196612
  7.2 26.7 %copy-start.8 = (bf16[128,256]{1,0:T(8,128)(2,1)S(1)}, bf16[128,256]{1,0:T(8,128)(2,1)}, u32[]{:S(2)}) copy-start(bf16[128,256]{1,0:T(8,128)(2,1)} %param.12) | copy-start | bytes 196612
  7.2 95.0 %all-gather.2.cloned.1.call-start = ((), (), s32[]{:S(2)}) async-start(), calls=%async_computation.2 | async-start | bytes 8912896 | tf_op jit(solution)/shard_map/all_gather | solution.py:58
  11.1 24.5 %copy-start.4 = (bf16[1024,256]{1,0:T(8,128)(2,1)S(1)}, bf16[1024,256]{1,0:T(8,128)(2,1)}, u32[]{:S(2)}) copy-start(bf16[1024,256]{1,0:T(8,128)(2,1)} %param.17) | copy-start | bytes 1572868
  34.3 1.2 copy-start
  35.3 319.5 %reduce-scatter.2.cloned.1.call-start = ((), (), s32[]{:S(2)}) async-start(), calls=%async_computation.3 | async-start | bytes 17825792 | tf_op jit(solution)/shard_map/reduce_scatter | solution.py:78
  36.6 65.6 %copy-start.6 = (s32[8,8]{1,0:T(8,128)S(1)}, s32[8,8]{1,0:T(8,128)}, u32[]{:S(2)}) copy-start(s32[8,8]{1,0:T(8,128)} %param.15) | copy-start | bytes 772
  36.6 65.6 %copy-start.9 = (s32[8]{0:T(128)S(1)}, s32[8]{0:T(128)}, u32[]{:S(2)}) copy-start(s32[8]{0:T(128)} %param.16) | copy-start | bytes 100
  102.3 1.2 copy-start.2
  106.6 1.2 copy-start.2
  111.0 1.2 copy-start.2
  115.4 1.2 copy-start.2
  119.7 1.2 copy-start.2
  124.1 1.2 copy-start.2
  132.8 1.2 copy-start.2
  137.2 1.2 copy-start.2
  141.5 1.2 copy-start.2
  145.9 1.2 copy-start.2
  150.3 1.2 copy-start.2
  159.0 1.2 copy-start.2
  163.3 1.2 copy-start.2
  167.7 1.2 copy-start.2
  244.6 113.1 %copy-start.1 = (bf16[1024,256]{0,1:T(8,128)(2,1)S(1)}, bf16[1024,256]{0,1:T(8,128)(2,1)}, u32[]{:S(2)}) copy-start(bf16[1024,256]{0,1:T(8,128)(2,1)} %get-tuple-element.348) | copy-start | bytes 1572868
  244.6 257.2 %all-reduce.3.cloned.1.call-start = ((), (), s32[]{:S(2)}) async-start(), calls=%async_computation.4 | async-start | bytes 524288 | tf_op jit(solution)/shard_map/psum | solution.py:90
  (34 other events, 34.6 us)
Sparse Core Ops, SparseCore 0:
  35.4 66.7 all-gather.1
  244.7 110.0 reduce-scatter.1
  360.3 141.5 all-reduce.2
where the time goes:
time: 514 us; the launch traced here: 512 us
  waiting for transfers between devices  315 us (61%)
  matrix products  90 us (18%)
  local copies, waits for them, and re-layouts  50.4 us (10%)
  blocking collectives  22.5 us (4%)
  between operations  13.9 us (3%)
  loops' own time  11.3 us (2%)
  other arithmetic  8.39 us (2%)
    psum x1, waiting for transfers between devices, per_device(): lax.psum((partial_self, partial_neigh), ('blk', 'feat'))  143 us
    reduce_scatter x1, waiting for transfers between devices, per_device(): lax.psum_scatter(stacked.reshape(node_rows * lax.axis_size('feat'), hidde...  109 us
    all_gather x1, waiting for transfers between devices, per_device(): lax.all_gather(z_neigh, 'feat', axis=0, tiled=True)  62.6 us
    dot_general x16, matrix products, add_neighbours(): jnp.dot(table, rows_here, preferred_element_type=jnp.float32)  33.3 us
    dot_general x16, matrix products, one_piece(): lax.dot_general(table, grad_pre, contract_first, preferred_element_type=j...  28.1 us
    while x96, local copies, waits for them, and re-layouts  27.2 us
    dot_general x32, matrix products, column_match(): jnp.einsum('btc,btij->bicj', matches, adjacency_tiles, preferred_element_...  24.3 us
    all_to_all x1, blocking collectives, per_device(): lax.all_to_all(features, ('blk', 'feat'), split_axis=1, concat_axis=0, ti...  22.5 us
  transfers between devices with their start and end apart: 3, of which 3 were waited for; matrix products, arithmetic and copies ran while one was open for 1% of the time, Pallas kernels for 0%

commit v1 on v0

v1 whole, which is shorter than its diff:
```python
import functools

import jax
import jax.numpy as jnp
from jax import lax
from jax.experimental import pallas as pl
from jax.experimental.pallas import tpu as pltpu
from jax.sharding import PartitionSpec as P

ALL = ("blk", "feat")
CONTRACT_FIRST = (((0,), (0,)), ((), ()))
CONTRACT_LAST = (((1,), (1,)), ((), ()))


def layer_kernel(columns, counts, own, x_ref, tiles_ref, w_ref, cot_ref, hidden_ref, grad_ref):
    blocks, slots, size, _ = tiles_ref.shape
    first = own[0] * (blocks * size)
    w = w_ref[...]
    grad = jnp.zeros(grad_ref.shape, jnp.float32)
    for b in range(blocks):
        gathered = jnp.zeros((x_ref.shape[0], size), jnp.float32)
        for t in range(slots):
            start = pl.multiple_of(columns[b * slots + t] * size, size)
            tile = tiles_ref[b, t]
            tile = jnp.where(t < counts[b], tile, jnp.zeros_like(tile))
            gathered += lax.dot_general(
                x_ref[:, pl.ds(start, size)], tile, CONTRACT_LAST,
                preferred_element_type=jnp.float32,
            )
        own_x = x_ref[:, pl.ds(pl.multiple_of(first + b * size, size), size)]
        both = jnp.concatenate([own_x, gathered.astype(jnp.bfloat16)], axis=0)
        pre = lax.dot_general(both, w, CONTRACT_FIRST, preferred_element_type=jnp.float32)
        s = jax.nn.sigmoid(pre)
        rows = pl.ds(b * size, size)
        hidden_ref[rows, :] = (pre * s).astype(jnp.bfloat16)
        cot = cot_ref[rows, :].astype(jnp.float32)
        grad_pre = (cot * s * (1.0 + pre * (1.0 - s))).astype(jnp.bfloat16)
        grad += jnp.dot(both, grad_pre, preferred_element_type=jnp.float32)
    grad_ref[...] = grad


def per_device(features, w_self, w_neigh, adjacency_tiles, tile_columns, tile_count, cotangent):
    nb, nf = lax.axis_size("blk"), lax.axis_size("feat")
    depth, hidden = w_self.shape
    nodes = cotangent.shape[0]

    def regroup(w):
        return w.reshape(nb, nf, hidden).transpose(1, 0, 2).reshape(depth, hidden)

    w = jnp.concatenate([regroup(w_self), regroup(w_neigh)], axis=0)
    rows = lax.all_to_all(features, "blk", split_axis=1, concat_axis=0, tiled=True)
    x = lax.all_gather(rows, "feat", axis=0, tiled=True)
    own = lax.axis_index("feat").astype(jnp.int32).reshape(1)
    vmem = pl.BlockSpec(memory_space=pltpu.VMEM)
    smem = pl.BlockSpec(memory_space=pltpu.SMEM)
    hidden_out, grad = pl.pallas_call(
        layer_kernel,
        out_shape=(
            jax.ShapeDtypeStruct((nodes, hidden), jnp.bfloat16),
            jax.ShapeDtypeStruct((2 * depth, hidden), jnp.float32),
        ),
        in_specs=[smem, smem, smem, vmem, vmem, vmem, vmem],
        out_specs=(vmem, vmem),
        compiler_params=pltpu.CompilerParams(vmem_limit_bytes=24 * 1024 * 1024),
    )(tile_columns.reshape(-1), tile_count, own, x, adjacency_tiles, w, cotangent)
    parts = grad.reshape(2, depth, hidden).transpose(1, 0, 2)
    parts = lax.all_to_all(parts, ALL, split_axis=0, concat_axis=0, tiled=True)
    mine = jnp.sum(parts, axis=0)
    total = lax.all_to_all(
        jnp.broadcast_to(mine[None], (depth, 2, hidden)), ALL, split_axis=0, concat_axis=0, tiled=True
    )
    total = total.reshape(nf, nb, 2, hidden).transpose(2, 1, 0, 3).reshape(2, depth, hidden)
    return hidden_out, total[0], total[1]


def solution(mesh):
    return jax.shard_map(
        per_device,
        mesh=mesh,
        in_specs=(
            P(ALL, None),
            P(),
            P(),
            P(ALL, None, None, None),
            P(ALL, None),
            P(ALL),
            P(ALL, None),
        ),
        out_specs=(P(ALL, None), P(), P()),
        check_vma=False,
    )
```

time: 514 us -> 128 us (0.25)
  waiting for transfers between devices: 315 us -> 51 us
  matrix products: 90 us -> 0 us
  local copies, waits for them, and re-layouts: 50.4 us -> 7.55 us
  blocking collectives: 22.5 us -> 46.3 us
  loops' own time: 11.3 us -> 0 us
  Pallas kernels: 0 us -> 5.43 us
    psum x1 -> x0, waiting for transfers between devices: 143 us -> none  [per_device(): lax.psum((partial_self, partial_neigh), ('blk', 'feat'))]
    reduce_scatter x1 -> x0, waiting for transfers between devices: 109 us -> none  [per_device(): lax.psum_scatter(stacked.reshape(node_rows * lax.axis_size('feat'), hidde...]
    dot_general x67 -> x0, matrix products: 90 us -> none  [the longest x16 33.3 us: add_neighbours(): jnp.dot(table, rows_here, preferred_element_type=jnp.float32)]
    while x98 -> x0, local copies, waits for them, and re-layouts: 30.7 us -> none
    all_to_all x1 -> x3, blocking collectives: 22.5 us -> 46.3 us  [the longest x1 18.9 us: per_device(): parts = lax.all_to_all(parts, ALL, split_axis=0, concat_axis=0, tiled=True)]
    all_gather x1, waiting for transfers between devices: 62.6 us -> 51 us  [per_device(): x = lax.all_gather(rows, 'feat', axis=0, tiled=True)]
    another operation x2 -> x0, loops' own time: 11.3 us -> none  [the longest x1 11 us: per_device(): stacked = lax.map(one_piece, jnp.arange(pieces, dtype=jnp.int32))]
    dynamic_slice x16 -> x0, local copies, waits for them, and re-layouts: 9.32 us -> none  [per_device(): stacked = lax.map(one_piece, jnp.arange(pieces, dtype=jnp.int32))]
  transfers between devices with their start and end apart: 3 -> 1, of which waited for: 3 -> 1; matrix products, arithmetic and copies ran while one was open for 1% -> 1% of each run, Pallas kernels for 0% -> 0%
where the time goes in v1:
time: 128 us
  waiting for transfers between devices  51 us (40%)
  blocking collectives  46.3 us (36%)
  between operations  14.1 us (11%)
  local copies, waits for them, and re-layouts  7.55 us (6%)
  Pallas kernels  5.43 us (4%)
  other arithmetic  3.58 us (3%)
    all_gather x1, waiting for transfers between devices, per_device(): x = lax.all_gather(rows, 'feat', axis=0, tiled=True)  51 us
    all_to_all x1, blocking collectives, per_device(): parts = lax.all_to_all(parts, ALL, split_axis=0, concat_axis=0, tiled=True)  18.9 us
    all_to_all x1, blocking collectives, per_device(): lax.all_to_all(jnp.broadcast_to(mine[None], (depth, 2, hidden)), ALL, spl...  15.2 us
    all_to_all x1, blocking collectives, per_device(): lax.all_to_all(features, 'blk', split_axis=1, concat_axis=0, tiled=True)  12.1 us
    pallas_call x1, Pallas kernels, per_device(): pl.pallas_call(layer_kernel, out_shape=(jax.ShapeDtypeStruct((nodes, hidd...  5.43 us
    unnamed x1, other arithmetic  3.42 us
    unnamed x11, local copies, waits for them, and re-layouts  3.16 us
  transfers between devices with their start and end apart: 1, of which 1 were waited for; matrix products, arithmetic and copies ran while one was open for 1% of the time, Pallas kernels for 0%

profile of v1, /device:TPU:1, one launch (start us, length us, event | category | flops | bytes accessed | tf_op | source)
XLA Modules:
  0.0 128.0 jit_solution(7983632407271605396)
XLA Ops:
  7.2 0.0 copy-start.2
  7.2 0.0 copy-start.3
  7.2 0.0 copy-start.1
  7.2 0.0 all-gather.3.cloned.1.call-start
  7.2 0.5 broadcast.1
  7.8 3.4 %reduce = bf16[8,16384]{1,0:T(8,128)(2,1)S(1)} reduce(bf16[8,1,16384]{2,1,0:T(2,128)(2,1)} %bitcast.31, bf16[]{:T(256)} %broadcast.1), dimensions={1}, to_apply=%bitcast.22.reduce_sub_computation | reduce | bytes 524290
  11.2 0.2 reshape.51
  11.4 12.1 %all_to_all.26 = bf16[8,2,8192]{2,1,0:T(2,128)(2,1)S(1)} all-to-all(bf16[8,2,8192]{2,1,0:T(2,128)(2,1)S(1)} %reshape.51), channel_id=1, replica_groups=mesh['blk'=8,'feat'=16] {'blk'}, dimensions={0} | all-to-all | bytes 524288 | tf_op jit(solution)/shard_map/all_to_all | solution.py:51
  23.5 0.3 reshape.52
  23.7 1.0 copy.18
  24.7 0.0 all-gather.3.cloned.1.call-update
  24.8 0.8 reshape.42.columns
  25.5 0.9 copy_bitcast_fusion.2
  26.5 51.0 %all-gather.3.cloned.1.call-done = bf16[1,128,16384]{2,1,0:T(8,128)(2,1)} async-done(((bf16[1,8,16384]{2,1,0:T(8,128)(2,1)}), bf16[1,128,16384]{2,1,0:T(8,128)(2,1)}) %all-gather.3.cloned.1.call-update) | async-done | bytes 4194320 | tf_op jit(solution)/shard_map/all_gather | solution.py:52
  77.5 0.0 copy-done.2
  77.5 2.2 %copy-done = bf16[1,128,16384]{2,1,0:T(8,128)(2,1)S(1)} copy-done((bf16[1,128,16384]{2,1,0:T(8,128)(2,1)S(1)}, bf16[1,128,16384]{2,1,0:T(8,128)(2,1)}, u32[]{:S(2)}) %copy-start) | copy-done | bytes 4194328
  79.7 5.4 %shard_map.94 = (bf16[1024,256]{1,0:T(8,128)(2,1)}, f32[256,256]{1,0:T(8,128)S(1)}) custom-call(s32[64]{0:T(128)S(1)} %reshape.42.columns, s32[8]{0:T(128)S(1)} %copy-done.3, s32[1]{0:T(128)} %bitcast.own, bf16[128,16384]{1,0:T(8,128)(2,1)S(1)} %bitcast.26, bf16[8,8,128,128]{3,2,1,0:T(8,128)(2,1)S(1)} %copy-done.1, ...), custom_call_target="tpu_custom_call" | custom-call | tf_op jit(solution)/shard_map/pallas_call | solution.py:56
  85.1 0.2 copy.30
  85.3 18.9 %all_to_all.27 = f32[128,2,256]{2,1,0:T(2,128)S(1)} all-to-all(f32[128,2,256]{2,1,0:T(2,128)S(1)} %bitcast.30), channel_id=1, replica_groups=mesh['blk'=8,'feat'=16] {'blk','feat'}, dimensions={0} | all-to-all | bytes 524288 | tf_op jit(solution)/shard_map/all_to_all | solution.py:67
  104.2 0.1 reduce_sum.9
  104.4 0.1 broadcast_in_dim.2
  104.5 15.2 %all_to_all.28 = f32[128,2,256]{2,1,0:T(2,128)S(1)} all-to-all(f32[128,2,256]{2,1,0:T(2,128)S(1)} %broadcast_in_dim.2), channel_id=1, replica_groups=mesh['blk'=8,'feat'=16] {'blk','feat'}, dimensions={0} | all-to-all | bytes 524288 | tf_op jit(solution)/shard_map/all_to_all | solution.py:69
  119.8 0.7 copy.24
  120.5 0.7 copy.23
  (6 shorter events, 0.1 us)
Async XLA Ops:
  7.2 70.3 %copy-start.2 = (bf16[1024,256]{1,0:T(8,128)(2,1)S(1)}, bf16[1024,256]{1,0:T(8,128)(2,1)}, u32[]{:S(2)}) copy-start(bf16[1024,256]{1,0:T(8,128)(2,1)} %cot_ref.1) | copy-start | bytes 1572868
  7.2 70.3 %copy-start.3 = (s32[8]{0:T(128)S(1)}, s32[8]{0:T(128)}, u32[]{:S(2)}) copy-start(s32[8]{0:T(128)} %counts.1) | copy-start | bytes 100
  7.2 70.3 %copy-start.1 = (bf16[8,8,128,128]{3,2,1,0:T(8,128)(2,1)S(1)}, bf16[8,8,128,128]{3,2,1,0:T(8,128)(2,1)}, u32[]{:S(2)}) copy-start(bf16[8,8,128,128]{3,2,1,0:T(8,128)(2,1)} %tiles_ref.1) | copy-start | bytes 6291460
  7.2 70.3 %all-gather.3.cloned.1.call-start = ((), (), s32[]{:S(2)}) async-start(), calls=%async_computation.3 | async-start | bytes 4456448 | tf_op jit(solution)/shard_map/all_gather | solution.py:52
  77.5 2.2 %copy-start = (bf16[1,128,16384]{2,1,0:T(8,128)(2,1)S(1)}, bf16[1,128,16384]{2,1,0:T(8,128)(2,1)}, u32[]{:S(2)}) copy-start(bf16[1,128,16384]{2,1,0:T(8,128)(2,1)} %all-gather.3.cloned.1.call-done) | copy-start | bytes 12582916
Sparse Core Ops, SparseCore 0:
  24.9 52.5 all-gather.2

commit v2 on v1

v2 whole, which is shorter than its diff:
```python
import jax
import jax.numpy as jnp
from jax import lax
from jax.experimental import pallas as pl
from jax.experimental.pallas import tpu as pltpu
from jax.sharding import PartitionSpec as P

ALL = ("blk", "feat")
CONTRACT_FIRST = (((0,), (0,)), ((), ()))
CONTRACT_LAST = (((1,), (1,)), ((), ()))
RANGE = range(4)


def device(x, c, y, z):
    return (x * 2 + c) * 16 + y * 4 + z


PLANES = [[device(x, 0, y, z) for x in RANGE for z in RANGE] for y in RANGE]
PLANES += [[device(x, 1, y, z) for x in RANGE for y in RANGE] for z in RANGE]


def ring(step):
    pairs = []
    for x in RANGE:
        for y in RANGE:
            for z in RANGE:
                pairs.append((device(x, 0, y, z), device(x, 0, (y + step) % 4, z)))
                pairs.append((device(x, 1, y, z), device(x, 1, y, (z + step) % 4)))
    return pairs


RIGHT, LEFT = ring(1), ring(-1)
OTHER_CORE = [(d, d ^ 16) for d in range(128)]


def interleave_kernel(core, in_ref, own_ref, other_ref):
    half = own_ref.shape[0]
    step = 16
    for part, out_ref in enumerate((own_ref, other_ref)):
        first = ((core[0] + part) % 2) * half
        for k in range(half // step):
            start = pl.multiple_of(first + k * step, step)
            out_ref[pl.ds(k * step, step)] = jnp.swapaxes(in_ref[:, pl.ds(start, step), :], 0, 1)


def layer_kernel(columns, counts, place, *refs):
    pieces = refs[:8]
    tiles_ref, w_ref, cot_ref, hidden_ref, grad_ref = refs[8:]
    blocks, slots, size, _ = tiles_ref.shape
    chunk = w_ref.shape[2]
    w = jnp.concatenate([w_ref[s, place[1 + k]] for s in range(2) for k in range(8)], axis=0)
    grad = jnp.zeros((16 * chunk, w.shape[1]), jnp.float32)

    def features_of(block):
        return jnp.concatenate([piece[block] for piece in pieces], axis=0)

    for b in range(blocks):
        gathered = jnp.zeros((8 * chunk, size), jnp.float32)
        for t in range(slots):
            tile = tiles_ref[b, t]
            tile = jnp.where(t < counts[b], tile, jnp.zeros_like(tile))
            gathered += lax.dot_general(
                features_of(columns[b * slots + t]), tile, CONTRACT_LAST,
                preferred_element_type=jnp.float32,
            )
        own_x = features_of(place[0] * blocks + b)
        both = jnp.concatenate([own_x, gathered.astype(jnp.bfloat16)], axis=0)
        pre = lax.dot_general(both, w, CONTRACT_FIRST, preferred_element_type=jnp.float32)
        s = jax.nn.sigmoid(pre)
        rows = pl.ds(b * size, size)
        hidden_ref[rows, :] = (pre * s).astype(jnp.bfloat16)
        cot = cot_ref[rows, :].astype(jnp.float32)
        grad_pre = (cot * s * (1.0 + pre * (1.0 - s))).astype(jnp.bfloat16)
        grad += jnp.dot(both, grad_pre, preferred_element_type=jnp.float32)
    for s in range(2):
        for k in range(8):
            start = (s * 8 + k) * chunk
            grad_ref[s, place[1 + k]] = grad[start : start + chunk]


VMEM = pl.BlockSpec(memory_space=pltpu.VMEM)
SMEM = pl.BlockSpec(memory_space=pltpu.SMEM)
PARAMS = pltpu.CompilerParams(vmem_limit_bytes=24 * 1024 * 1024)


def send(array, pairs):
    return lax.ppermute(array, ALL, pairs)


def by_chunk(w):
    w = w.reshape(4, 2, 4, 4, -1)
    w = jnp.stack([w[:, 0].transpose(1, 0, 2, 3), w[:, 1].transpose(2, 0, 1, 3)])
    return w.reshape(8, 16, -1)


def by_row(g):
    g = g.reshape(2, 4, 4, 4, -1)
    g = jnp.stack([g[0].transpose(1, 0, 2, 3), g[1].transpose(1, 2, 0, 3)], axis=1)
    return g.reshape(128, -1)


def per_device(features, w_self, w_neigh, adjacency_tiles, tile_columns, tile_count, cotangent):
    depth, hidden = w_self.shape
    nodes = cotangent.shape[0]
    blocks, slots, size, _ = adjacency_tiles.shape
    core = lax.axis_index("blk") % 2
    feat = lax.axis_index("feat")
    y, z = feat // 4, feat % 4

    out = features.reshape(4, 1, 256, size)
    out = jnp.broadcast_to(out, (4, 4, 256, size)).reshape(16, 256, size)
    rows = lax.all_to_all(
        out, ALL, split_axis=0, concat_axis=0, tiled=True, axis_index_groups=PLANES
    )
    piece = jax.ShapeDtypeStruct((128, 16, size), jnp.bfloat16)
    own, other = pl.pallas_call(
        interleave_kernel,
        out_shape=(piece, piece),
        in_specs=[SMEM, VMEM],
        out_specs=(VMEM, VMEM),
        compiler_params=PARAMS,
    )(core.astype(jnp.int32).reshape(1), rows)

    own_left, other_right = send(own, RIGHT), send(other, LEFT)
    other_left, own_right = send(other, RIGHT), send(own, LEFT)
    own_far, other_far = send(own_left, RIGHT), send(other_right, LEFT)
    swapped = [send(v, OTHER_CORE) for v in (other, other_left, other_right, other_far)]
    pieces = [own, own_left, own_right, own_far, *swapped]

    at = jnp.where(core == 0, y, z)
    partner_at = jnp.where(core == 0, z, y)
    steps = jnp.array([0, 3, 1, 2], jnp.int32)
    place = jnp.concatenate(
        [feat[None], core * 4 + (at + steps) % 4, (1 - core) * 4 + (partner_at + steps) % 4]
    ).astype(jnp.int32)
    w = jnp.stack([by_chunk(w_self), by_chunk(w_neigh)])
    hidden_out, grad = pl.pallas_call(
        layer_kernel,
        out_shape=(
            jax.ShapeDtypeStruct((nodes, hidden), jnp.bfloat16),
            jax.ShapeDtypeStruct((2, 8, 16, hidden), jnp.float32),
        ),
        in_specs=[SMEM, SMEM, SMEM] + [VMEM] * 11,
        out_specs=(VMEM, VMEM),
        compiler_params=PARAMS,
    )(tile_columns.reshape(-1), tile_count, place, *pieces, adjacency_tiles, w, cotangent)
    parts = grad.reshape(2, depth, hidden).transpose(1, 0, 2)
    parts = lax.all_to_all(parts, ALL, split_axis=0, concat_axis=0, tiled=True)
    mine = jnp.sum(parts, axis=0)
    total = lax.all_to_all(
        jnp.broadcast_to(mine[None], (depth, 2, hidden)), ALL, split_axis=0, concat_axis=0, tiled=True
    )
    return hidden_out, by_row(total[:, 0]), by_row(total[:, 1])


def solution(mesh):
    return jax.shard_map(
        per_device,
        mesh=mesh,
        in_specs=(
            P(ALL, None),
            P(),
            P(),
            P(ALL, None, None, None),
            P(ALL, None),
            P(ALL),
            P(ALL, None),
        ),
        out_specs=(P(ALL, None), P(), P()),
        check_vma=False,
    )
```

time: 128 us -> 102 us (0.80)
  starting transfers between devices: 0.04 us -> 27.8 us
  waiting for transfers between devices: 51 us -> 23.4 us
  blocking collectives: 46.3 us -> 32.3 us
  between operations: 14.1 us -> 0.89 us
  Pallas kernels: 5.43 us -> 7.61 us
    all_gather x1 -> x0, waiting for transfers between devices: 51 us -> none  [per_device(): x = lax.all_gather(rows, 'feat', axis=0, tiled=True)]
    ppermute x0 -> x10, starting transfers between devices: none -> 20.1 us  [send(): return lax.ppermute(array, ALL, pairs)]
    all_to_all x0 -> x1, waiting for transfers between devices: none -> 14.8 us  [per_device(): lax.all_to_all(out, ALL, split_axis=0, concat_axis=0, tiled=True, axis_in...]
    all_to_all x1 -> x0, blocking collectives: 12.1 us -> none  [per_device(): lax.all_to_all(features, 'blk', split_axis=1, concat_axis=0, tiled=True)]
    ppermute x0 -> x10, waiting for transfers between devices: none -> 8.6 us  [send(): return lax.ppermute(array, ALL, pairs)]
    all_to_all x0 -> x1, starting transfers between devices: none -> 7.73 us  [per_device(): lax.all_to_all(out, ALL, split_axis=0, concat_axis=0, tiled=True, axis_in...]
    all_to_all x1, blocking collectives: 18.9 us -> 17.1 us  [per_device(): parts = lax.all_to_all(parts, ALL, split_axis=0, concat_axis=0, tiled=True)]
    unnamed x11 -> x22, local copies, waits for them, and re-layouts: 3.16 us -> 2.96 us
  transfers between devices with their start and end apart: 1 -> 11, of which waited for: 1 -> 3; matrix products, arithmetic and copies ran while one was open for 1% -> 0% of each run, Pallas kernels for 0% -> 0%
where the time goes in v2:
time: 102 us
  blocking collectives  32.3 us (32%)
  starting transfers between devices  27.8 us (27%)
  waiting for transfers between devices  23.4 us (23%)
  Pallas kernels  7.61 us (7%)
  local copies, waits for them, and re-layouts  6.89 us (7%)
  other arithmetic  2.91 us (3%)
    ppermute x10, starting transfers between devices, send(): return lax.ppermute(array, ALL, pairs)  20.1 us
    all_to_all x1, blocking collectives, per_device(): parts = lax.all_to_all(parts, ALL, split_axis=0, concat_axis=0, tiled=True)  17.1 us
    all_to_all x1, blocking collectives, per_device(): lax.all_to_all(jnp.broadcast_to(mine[None], (depth, 2, hidden)), ALL, spl...  15.2 us
    all_to_all x1, waiting for transfers between devices, per_device(): lax.all_to_all(out, ALL, split_axis=0, concat_axis=0, tiled=True, axis_in...  14.8 us
    ppermute x10, waiting for transfers between devices, send(): return lax.ppermute(array, ALL, pairs)  8.6 us
    all_to_all x1, starting transfers between devices, per_device(): lax.all_to_all(out, ALL, split_axis=0, concat_axis=0, tiled=True, axis_in...  7.73 us
    pallas_call x1, Pallas kernels, per_device(): pl.pallas_call(layer_kernel, out_shape=(jax.ShapeDtypeStruct((nodes, hidd...  6.56 us
    unnamed x22, local copies, waits for them, and re-layouts  2.96 us
  transfers between devices with their start and end apart: 11, of which 3 were waited for; matrix products, arithmetic and copies ran while one was open for 0% of the time, Pallas kernels for 0%

profile of v2, /device:TPU:1, one launch (start us, length us, event | category | flops | bytes accessed | tf_op | source)
XLA Modules:
  0.0 101.8 jit_solution(3563205045023037996)
XLA Ops:
  0.6 2.5 %reduce = bf16[131072]{0:T(1024)(128)(2,1)S(1)} reduce(bf16[1,131072]{1,0:T(2,128)(2,1)} %param.8, bf16[]{:T(256)} %constant.67), dimensions={0}, to_apply=%param.8.reduce_sub_computation | reduce | bytes 524290 | tf_op args[0]
  3.1 1.2 %broadcast_in_dim.18 = bf16[4,4,256,128]{3,2,1,0:T(8,128)(2,1)} broadcast(bf16[4,256,128]{2,1,0:T(8,128)(2,1)S(1)} %bitcast.54), dimensions={0,2,3} | broadcast | bytes 1310720 | tf_op jit(solution)/shard_map/broadcast_in_dim | solution.py:111
  4.3 7.7 %all-to-all-start = ((bf16[16,256,128]{2,1,0:T(8,128)(2,1)}), bf16[16,256,128]{2,1,0:T(8,128)(2,1)S(1)}, u32[]{:S(2)}, u32[]{:S(2)}) async-start(bf16[16,256,128]{2,1,0:T(8,128)(2,1)} %bitcast.53), calls=%async_computation | async-start | bytes 2097152 | tf_op jit(solution)/shard_map/all_to_all | solution.py:112
  12.1 14.8 %all-to-all-done.in_ref = bf16[16,256,128]{2,1,0:T(8,128)(2,1)S(1)} async-done(((bf16[16,256,128]{2,1,0:T(8,128)(2,1)}), bf16[16,256,128]{2,1,0:T(8,128)(2,1)S(1)}, u32[]{:S(2)}, u32[]{:S(2)}) %all-to-all-start) | async-done | bytes 1048608 | tf_op jit(solution)/shard_map/all_to_all | solution.py:112
  26.9 1.0 %shard_map.103 = (bf16[128,16,128]{2,1,0:T(8,128)(2,1)S(1)}, bf16[128,16,128]{2,1,0:T(8,128)(2,1)}) custom-call(s32[1]{0:T(128)} %bitcast.1.core, bf16[16,256,128]{2,1,0:T(8,128)(2,1)S(1)} %all-to-all-done.in_ref), custom_call_target="tpu_custom_call" | custom-call | tf_op jit(solution)/shard_map/pallas_call | solution.py:116
  27.9 0.8 copy-done.2
  28.7 3.7 %collective-permute-start.6 = (bf16[128,16,128]{2,1,0:T(8,128)(2,1)}, bf16[128,16,128]{2,1,0:T(8,128)(2,1)}, u32[]{:S(2)}, u32[]{:S(2)}) collective-permute-start(bf16[128,16,128]{2,1,0:T(8,128)(2,1)} %get-tuple-element.8), channel_id=1, source_target_pairs={{0,12},{16,19},{1,13},{17,16},{2,14},{18,17},{3,15},{19,18},{4,0},... | collective-permute-start | bytes 1572872 | tf_op jit(solution)/shard_map/ppermute | solution.py:87
  33.0 1.1 %collective-permute-start = (bf16[128,16,128]{2,1,0:T(8,128)(2,1)}, bf16[128,16,128]{2,1,0:T(8,128)(2,1)S(1)}, u32[]{:S(2)}, u32[]{:S(2)}) collective-permute-start(bf16[128,16,128]{2,1,0:T(8,128)(2,1)} %copy-done.2), channel_id=1, source_target_pairs={{0,4},{16,17},{1,5},{17,18},{2,6},{18,19},{3,7},{19,16},{4,8},{20,... | collective-permute-start | bytes 1572872 | tf_op jit(solution)/shard_map/ppermute | solution.py:87
  34.1 4.8 %collective-permute-done.6 = bf16[128,16,128]{2,1,0:T(8,128)(2,1)} collective-permute-done((bf16[128,16,128]{2,1,0:T(8,128)(2,1)}, bf16[128,16,128]{2,1,0:T(8,128)(2,1)}, u32[]{:S(2)}, u32[]{:S(2)}) %collective-permute-start.6) | collective-permute-done | bytes 524320 | tf_op jit(solution)/shard_map/ppermute | solution.py:87
  38.9 3.3 %collective-permute-start.8 = (bf16[128,16,128]{2,1,0:T(8,128)(2,1)}, bf16[128,16,128]{2,1,0:T(8,128)(2,1)}, u32[]{:S(2)}, u32[]{:S(2)}) collective-permute-start(bf16[128,16,128]{2,1,0:T(8,128)(2,1)} %collective-permute-done.6), channel_id=1, source_target_pairs={{0,12},{16,19},{1,13},{17,16},{2,14},{18,17},{3,15},{19,18},{4,0},... | collective-permute-start | bytes 1572872 | tf_op jit(solution)/shard_map/ppermute | solution.py:87
  42.5 4.3 %collective-permute-start.3 = (bf16[128,16,128]{2,1,0:T(8,128)(2,1)}, bf16[128,16,128]{2,1,0:T(8,128)(2,1)}, u32[]{:S(2)}, u32[]{:S(2)}) collective-permute-start(bf16[128,16,128]{2,1,0:T(8,128)(2,1)} %get-tuple-element.8), channel_id=1, source_target_pairs={{0,16},{1,17},{2,18},{3,19},{4,20},{5,21},{6,22},{7,23},{8,24},{9,... | collective-permute-start | bytes 1572872 | tf_op jit(solution)/shard_map/ppermute | solution.py:87
  46.7 1.6 %collective-permute-start.7 = (bf16[128,16,128]{2,1,0:T(8,128)(2,1)}, bf16[128,16,128]{2,1,0:T(8,128)(2,1)}, u32[]{:S(2)}, u32[]{:S(2)}) collective-permute-start(bf16[128,16,128]{2,1,0:T(8,128)(2,1)} %collective-permute-done.6), channel_id=1, source_target_pairs={{0,16},{1,17},{2,18},{3,19},{4,20},{5,21},{6,22},{7,23},{8,24},{9,... | collective-permute-start | bytes 1572872 | tf_op jit(solution)/shard_map/ppermute | solution.py:87
  48.3 1.0 collective-permute-start.2
  49.3 3.8 %collective-permute-start.5 = (bf16[128,16,128]{2,1,0:T(8,128)(2,1)}, bf16[128,16,128]{2,1,0:T(8,128)(2,1)}, u32[]{:S(2)}, u32[]{:S(2)}) collective-permute-start(bf16[128,16,128]{2,1,0:T(8,128)(2,1)} %collective-permute-done.4), channel_id=1, source_target_pairs={{0,16},{1,17},{2,18},{3,19},{4,20},{5,21},{6,22},{7,23},{8,24},{9,... | collective-permute-start | bytes 1572872 | tf_op jit(solution)/shard_map/ppermute | solution.py:87
  53.1 0.8 collective-permute-start.9
  54.2 3.8 %collective-permute-done.2.refs_3_ = bf16[128,16,128]{2,1,0:T(8,128)(2,1)} collective-permute-done((bf16[128,16,128]{2,1,0:T(8,128)(2,1)S(1)}, bf16[128,16,128]{2,1,0:T(8,128)(2,1)}, u32[]{:S(2)}, u32[]{:S(2)}) %collective-permute-start.2) | collective-permute-done | bytes 524320 | tf_op jit(solution)/shard_map/ppermute | solution.py:87
  58.0 1.0 %copy-done.1 = bf16[1024,256]{1,0:T(8,128)(2,1)S(1)} copy-done((bf16[1024,256]{1,0:T(8,128)(2,1)S(1)}, bf16[1024,256]{1,0:T(8,128)(2,1)}, u32[]{:S(2)}) %copy-start.1) | copy-done | bytes 524312
  59.1 1.0 %copy-done.3 = bf16[128,16,128]{2,1,0:T(8,128)(2,1)S(1)} copy-done((bf16[128,16,128]{2,1,0:T(8,128)(2,1)S(1)}, bf16[128,16,128]{2,1,0:T(8,128)(2,1)}, u32[]{:S(2)}) %copy-start.3) | copy-done | bytes 524312
  60.1 6.6 %shard_map.104 = (bf16[1024,256]{1,0:T(8,128)(2,1)}, f32[2,8,16,256]{3,2,1,0:T(8,128)S(1)}) custom-call(s32[64]{0:T(128)S(1)} %reshape.41.columns, s32[8]{0:T(128)S(1)} %copy-done.4, s32[9]{0:T(128)S(1)} %pad_add_fusion.place, bf16[128,16,128]{2,1,0:T(8,128)(2,1)S(1)} %copy-done.3, bf16[128,16,128]{2,1,0:T(8,128)(2,1)S(1)} %collective-permute-done.refs_1_, ...), custom_call_target="tpu_custom_call" | custom-call | tf_op jit(solution)/shard_map/pallas_call | solution.py:137
  66.9 17.1 %all_to_all.15 = f32[128,2,256]{2,1,0:T(2,128)S(1)} all-to-all(f32[128,2,256]{2,1,0:T(2,128)S(1)} %bitcast.55), channel_id=1, replica_groups=mesh['blk'=8,'feat'=16] {'blk','feat'}, dimensions={0} | all-to-all | bytes 524288 | tf_op jit(solution)/shard_map/all_to_all | solution.py:148
  84.1 15.2 %all_to_all.16 = f32[128,2,256]{2,1,0:T(2,128)S(1)} all-to-all(f32[128,2,256]{2,1,0:T(2,128)S(1)} %broadcast_in_dim.19), channel_id=1, replica_groups=mesh['blk'=8,'feat'=16] {'blk','feat'}, dimensions={0} | all-to-all | bytes 524288 | tf_op jit(solution)/shard_map/all_to_all | solution.py:150
  99.4 0.7 slice_reduce_fusion.1
  100.2 0.7 reshape.48
  101.1 0.7 reshape.47
  (54 shorter events, 1.7 us)
Async XLA Ops:
  3.1 29.3 %copy-start.7 = (s32[8,8]{1,0:T(8,128)S(1)}, s32[8,8]{1,0:T(8,128)}, u32[]{:S(2)}) copy-start(s32[8,8]{1,0:T(8,128)} %param.12) | copy-start | bytes 772
  3.1 29.4 %copy-start.5 = (bf16[128,256]{1,0:T(8,128)(2,1)S(1)}, bf16[128,256]{1,0:T(8,128)(2,1)}, u32[]{:S(2)}) copy-start(bf16[128,256]{1,0:T(8,128)(2,1)} %param.9) | copy-start | bytes 196612
  4.3 38.1 %copy-start.6 = (bf16[128,256]{1,0:T(8,128)(2,1)S(1)}, bf16[128,256]{1,0:T(8,128)(2,1)}, u32[]{:S(2)}) copy-start(bf16[128,256]{1,0:T(8,128)(2,1)} %param.10) | copy-start | bytes 196612
  4.3 49.7 %copy-start.8 = (s32[4]{0:T(128)S(1)}, s32[4]{0:T(128)}, u32[]{:S(2)}) copy-start(s32[4]{0:T(128)} %constant.62.clone) | copy-start | bytes 52
  4.3 53.7 %copy-start = (bf16[8,8,128,128]{3,2,1,0:T(8,128)(2,1)S(1)}, bf16[8,8,128,128]{3,2,1,0:T(8,128)(2,1)}, u32[]{:S(2)}) copy-start(bf16[8,8,128,128]{3,2,1,0:T(8,128)(2,1)} %refs_8_.1) | copy-start | bytes 6291460
  4.3 53.7 %copy-start.4 = (s32[8]{0:T(128)S(1)}, s32[8]{0:T(128)}, u32[]{:S(2)}) copy-start(s32[8]{0:T(128)} %counts.1) | copy-start | bytes 100
  4.3 22.5 %all-to-all-start = ((bf16[16,256,128]{2,1,0:T(8,128)(2,1)}), bf16[16,256,128]{2,1,0:T(8,128)(2,1)S(1)}, u32[]{:S(2)}, u32[]{:S(2)}) async-start(bf16[16,256,128]{2,1,0:T(8,128)(2,1)} %bitcast.53), calls=%async_computation | async-start | bytes 2097152 | tf_op jit(solution)/shard_map/all_to_all | solution.py:112
  27.9 0.8 copy-start.2
  28.7 10.2 %collective-permute-start.6 = (bf16[128,16,128]{2,1,0:T(8,128)(2,1)}, bf16[128,16,128]{2,1,0:T(8,128)(2,1)}, u32[]{:S(2)}, u32[]{:S(2)}) collective-permute-start(bf16[128,16,128]{2,1,0:T(8,128)(2,1)} %get-tuple-element.8), channel_id=1, source_target_pairs={{0,12},{16,19},{1,13},{17,16},{2,14},{18,17},{3,15},{19,18},{4,0},... | collective-permute-start | bytes 1572872 | tf_op jit(solution)/shard_map/ppermute | solution.py:87
  32.6 14.2 %collective-permute-start.1 = (bf16[128,16,128]{2,1,0:T(8,128)(2,1)}, bf16[128,16,128]{2,1,0:T(8,128)(2,1)S(1)}, u32[]{:S(2)}, u32[]{:S(2)}) collective-permute-start(bf16[128,16,128]{2,1,0:T(8,128)(2,1)} %copy-done.2), channel_id=1, source_target_pairs={{0,12},{16,19},{1,13},{17,16},{2,14},{18,17},{3,15},{19,18},{4,0},... | collective-permute-start | bytes 1572872 | tf_op jit(solution)/shard_map/ppermute | solution.py:87
  33.0 15.3 %collective-permute-start = (bf16[128,16,128]{2,1,0:T(8,128)(2,1)}, bf16[128,16,128]{2,1,0:T(8,128)(2,1)S(1)}, u32[]{:S(2)}, u32[]{:S(2)}) collective-permute-start(bf16[128,16,128]{2,1,0:T(8,128)(2,1)} %copy-done.2), channel_id=1, source_target_pairs={{0,4},{16,17},{1,5},{17,18},{2,6},{18,19},{3,7},{19,16},{4,8},{20,... | collective-permute-start | bytes 1572872 | tf_op jit(solution)/shard_map/ppermute | solution.py:87
  34.1 15.2 %collective-permute-start.4 = (bf16[128,16,128]{2,1,0:T(8,128)(2,1)}, bf16[128,16,128]{2,1,0:T(8,128)(2,1)}, u32[]{:S(2)}, u32[]{:S(2)}) collective-permute-start(bf16[128,16,128]{2,1,0:T(8,128)(2,1)} %get-tuple-element.8), channel_id=1, source_target_pairs={{0,4},{16,17},{1,5},{17,18},{2,6},{18,19},{3,7},{19,16},{4,8},{20,... | collective-permute-start | bytes 1572872 | tf_op jit(solution)/shard_map/ppermute | solution.py:87
  38.9 14.2 %collective-permute-start.8 = (bf16[128,16,128]{2,1,0:T(8,128)(2,1)}, bf16[128,16,128]{2,1,0:T(8,128)(2,1)}, u32[]{:S(2)}, u32[]{:S(2)}) collective-permute-start(bf16[128,16,128]{2,1,0:T(8,128)(2,1)} %collective-permute-done.6), channel_id=1, source_target_pairs={{0,12},{16,19},{1,13},{17,16},{2,14},{18,17},{3,15},{19,18},{4,0},... | collective-permute-start | bytes 1572872 | tf_op jit(solution)/shard_map/ppermute | solution.py:87
  42.5 11.7 %collective-permute-start.3 = (bf16[128,16,128]{2,1,0:T(8,128)(2,1)}, bf16[128,16,128]{2,1,0:T(8,128)(2,1)}, u32[]{:S(2)}, u32[]{:S(2)}) collective-permute-start(bf16[128,16,128]{2,1,0:T(8,128)(2,1)} %get-tuple-element.8), channel_id=1, source_target_pairs={{0,16},{1,17},{2,18},{3,19},{4,20},{5,21},{6,22},{7,23},{8,24},{9,... | collective-permute-start | bytes 1572872 | tf_op jit(solution)/shard_map/ppermute | solution.py:87
  46.7 11.2 %collective-permute-start.7 = (bf16[128,16,128]{2,1,0:T(8,128)(2,1)}, bf16[128,16,128]{2,1,0:T(8,128)(2,1)}, u32[]{:S(2)}, u32[]{:S(2)}) collective-permute-start(bf16[128,16,128]{2,1,0:T(8,128)(2,1)} %collective-permute-done.6), channel_id=1, source_target_pairs={{0,16},{1,17},{2,18},{3,19},{4,20},{5,21},{6,22},{7,23},{8,24},{9,... | collective-permute-start | bytes 1572872 | tf_op jit(solution)/shard_map/ppermute | solution.py:87
  48.3 9.6 %collective-permute-start.2 = (bf16[128,16,128]{2,1,0:T(8,128)(2,1)S(1)}, bf16[128,16,128]{2,1,0:T(8,128)(2,1)}, u32[]{:S(2)}, u32[]{:S(2)}) collective-permute-start(bf16[128,16,128]{2,1,0:T(8,128)(2,1)S(1)} %collective-permute-done.refs_1_), channel_id=1, source_target_pairs={{0,4},{16,17},{1,5},{17,18},{2,6},{18,19},{3,7},{19,16},{4,8},{20,... | collective-permute-start | bytes 1572872 | tf_op jit(solution)/shard_map/ppermute | solution.py:87
  49.3 8.7 %collective-permute-start.5 = (bf16[128,16,128]{2,1,0:T(8,128)(2,1)}, bf16[128,16,128]{2,1,0:T(8,128)(2,1)}, u32[]{:S(2)}, u32[]{:S(2)}) collective-permute-start(bf16[128,16,128]{2,1,0:T(8,128)(2,1)} %collective-permute-done.4), channel_id=1, source_target_pairs={{0,16},{1,17},{2,18},{3,19},{4,20},{5,21},{6,22},{7,23},{8,24},{9,... | collective-permute-start | bytes 1572872 | tf_op jit(solution)/shard_map/ppermute | solution.py:87
  53.1 4.9 %collective-permute-start.9 = (bf16[128,16,128]{2,1,0:T(8,128)(2,1)}, bf16[128,16,128]{2,1,0:T(8,128)(2,1)}, u32[]{:S(2)}, u32[]{:S(2)}) collective-permute-start(bf16[128,16,128]{2,1,0:T(8,128)(2,1)} %collective-permute-done.8), channel_id=1, source_target_pairs={{0,16},{1,17},{2,18},{3,19},{4,20},{5,21},{6,22},{7,23},{8,24},{9,... | collective-permute-start | bytes 1572872 | tf_op jit(solution)/shard_map/ppermute | solution.py:87
  58.0 1.0 %copy-start.1 = (bf16[1024,256]{1,0:T(8,128)(2,1)S(1)}, bf16[1024,256]{1,0:T(8,128)(2,1)}, u32[]{:S(2)}) copy-start(bf16[1024,256]{1,0:T(8,128)(2,1)} %refs_10_.1) | copy-start | bytes 1572868
  59.0 1.0 %copy-start.3 = (bf16[128,16,128]{2,1,0:T(8,128)(2,1)S(1)}, bf16[128,16,128]{2,1,0:T(8,128)(2,1)}, u32[]{:S(2)}) copy-start(bf16[128,16,128]{2,1,0:T(8,128)(2,1)} %copy-done.2) | copy-start | bytes 1572868

commit v3 on v2

v3 whole, which is shorter than its diff:
```python
import jax
import jax.numpy as jnp
from jax import lax
from jax.experimental import pallas as pl
from jax.experimental.pallas import tpu as pltpu
from jax.sharding import PartitionSpec as P

ALL = ("blk", "feat")
CONTRACT_FIRST = (((0,), (0,)), ((), ()))
CONTRACT_LAST = (((1,), (1,)), ((), ()))
RANGE = range(4)


def device(x, c, y, z):
    return (x * 2 + c) * 16 + y * 4 + z


PLANES = [[device(x, 0, y, z) for x in RANGE for z in RANGE] for y in RANGE]
PLANES += [[device(x, 1, y, z) for x in RANGE for y in RANGE] for z in RANGE]


def ring(step, to_other_core=0, other_axis=0):
    pairs = []
    for x in RANGE:
        for c in range(2):
            for y in RANGE:
                for z in RANGE:
                    along_z = c ^ other_axis
                    to_y, to_z = (y, (z + step) % 4) if along_z else ((y + step) % 4, z)
                    pairs.append((device(x, c, y, z), device(x, c ^ to_other_core, to_y, to_z)))
    return pairs


RIGHT, LEFT = ring(1), ring(-1)
RIGHT_ACROSS, LEFT_ACROSS = ring(1, to_other_core=1), ring(-1, to_other_core=1)
LEFT_ON = ring(-1, other_axis=1)
OTHER_CORE = [(d, d ^ 16) for d in range(128)]


def spread_kernel(in_ref, out_ref):
    copies, rows, size = out_ref.shape[1:]
    step = 16
    for k in range(in_ref.shape[1] // (step * size)):
        flat = in_ref[0:1, k * step * size : (k + 1) * step * size]
        block = flat.astype(jnp.float32).reshape(step, size).astype(jnp.bfloat16)
        x, first = divmod(k * step, rows)
        for copy in range(copies):
            out_ref[x, copy, first : first + step] = block


def interleave_kernel(core, in_ref, own_ref, other_ref):
    half = own_ref.shape[0]
    step = 16
    for part, out_ref in enumerate((own_ref, other_ref)):
        first = ((core[0] + part) % 2) * half
        for k in range(half // step):
            start = pl.multiple_of(first + k * step, step)
            out_ref[pl.ds(k * step, step)] = jnp.swapaxes(in_ref[:, pl.ds(start, step), :], 0, 1)


def layer_kernel(columns, counts, place, *refs):
    pieces = refs[:8]
    tiles_ref, w_ref, cot_ref, hidden_ref, grad_ref, both_ref = refs[8:]
    blocks, slots, size, _ = tiles_ref.shape
    chunk = w_ref.shape[2]
    depth = 8 * chunk

    def features_of(block):
        return jnp.concatenate([piece[block] for piece in pieces], axis=0)

    for b in range(blocks):
        nodes = slice(b * size, (b + 1) * size)
        both_ref[:depth, nodes] = features_of(place[0] * blocks + b)
        x = jnp.concatenate([features_of(columns[b * slots + t]) for t in range(slots)], axis=1)
        tiles = []
        for t in range(slots):
            tile = tiles_ref[b, t]
            tiles.append(jnp.where(t < counts[b], tile, jnp.zeros_like(tile)))
        gathered = lax.dot_general(
            x, jnp.concatenate(tiles, axis=1), CONTRACT_LAST, preferred_element_type=jnp.float32
        )
        both_ref[depth:, nodes] = gathered.astype(jnp.bfloat16)
    w = jnp.concatenate([w_ref[s, place[1 + k]] for s in range(2) for k in range(8)], axis=0)
    both = both_ref[...]
    pre = lax.dot_general(both, w, CONTRACT_FIRST, preferred_element_type=jnp.float32)
    s = jax.nn.sigmoid(pre)
    hidden = pre * s
    hidden_ref[...] = hidden.astype(jnp.bfloat16)
    grad_pre = (cot_ref[...].astype(jnp.float32) * (s + hidden * (1.0 - s))).astype(jnp.bfloat16)
    grad = jnp.dot(both, grad_pre, preferred_element_type=jnp.float32)
    for k in range(8):
        first, stride = place[9 + k], place[17 + k // 4]
        for i in range(chunk):
            row = first + (i // 4) * 32 + (i % 4) * stride
            for s in range(2):
                at = s * depth + k * chunk + i
                grad_ref[row, s : s + 1] = grad[at : at + 1]


VMEM = pl.BlockSpec(memory_space=pltpu.VMEM)
SMEM = pl.BlockSpec(memory_space=pltpu.SMEM)
PARAMS = pltpu.CompilerParams(vmem_limit_bytes=24 * 1024 * 1024)


def send(array, pairs):
    return lax.ppermute(array, ALL, pairs)


def by_chunk(w):
    w = w.reshape(4, 2, 4, 4, -1)
    w = jnp.stack([w[:, 0].transpose(1, 0, 2, 3), w[:, 1].transpose(2, 0, 1, 3)])
    return w.reshape(8, 16, -1)


def per_device(features, w_self, w_neigh, adjacency_tiles, tile_columns, tile_count, cotangent):
    depth, hidden = w_self.shape
    nodes = cotangent.shape[0]
    blocks, slots, size, _ = adjacency_tiles.shape
    core = lax.axis_index("blk") % 2
    feat = lax.axis_index("feat")
    y, z = feat // 4, feat % 4

    out = pl.pallas_call(
        spread_kernel,
        out_shape=jax.ShapeDtypeStruct((4, 4, 256, size), jnp.bfloat16),
        in_specs=[VMEM],
        out_specs=VMEM,
        compiler_params=PARAMS,
    )(features).reshape(16, 256, size)
    rows = lax.all_to_all(
        out, ALL, split_axis=0, concat_axis=0, tiled=True, axis_index_groups=PLANES
    )
    piece = jax.ShapeDtypeStruct((128, 16, size), jnp.bfloat16)
    own, other = pl.pallas_call(
        interleave_kernel,
        out_shape=(piece, piece),
        in_specs=[SMEM, VMEM],
        out_specs=(VMEM, VMEM),
        compiler_params=PARAMS,
    )(core.astype(jnp.int32).reshape(1), rows)

    own_left, across_right = send(own, RIGHT), send(other, LEFT_ACROSS)
    across_left, own_right = send(other, RIGHT_ACROSS), send(own, LEFT)
    own_far, across_far = send(own_left, RIGHT), send(across_right, LEFT_ON)
    across = send(other, OTHER_CORE)
    pieces = [own, own_left, own_right, own_far, across, across_left, across_right, across_far]

    steps = jnp.array([0, 3, 1, 2], jnp.int32)
    at = (jnp.where(core == 0, y, z) + steps) % 4
    partner_at = (jnp.where(core == 0, z, y) + steps) % 4
    cores = jnp.stack([core, 1 - core])
    chunks = (cores[:, None] * 4 + jnp.stack([at, partner_at])).reshape(-1)
    strides = jnp.where(cores == 0, 1, 4)
    first_rows = cores[:, None] * 16 + jnp.stack([at, partner_at]) * (4 // strides)[:, None]
    place = jnp.concatenate([feat[None], chunks, first_rows.reshape(-1), strides]).astype(jnp.int32)
    w = jnp.stack([by_chunk(w_self), by_chunk(w_neigh)])
    hidden_out, grad = pl.pallas_call(
        layer_kernel,
        out_shape=(
            jax.ShapeDtypeStruct((nodes, hidden), jnp.bfloat16),
            jax.ShapeDtypeStruct((depth, 2, hidden), jnp.float32),
        ),
        in_specs=[SMEM, SMEM, SMEM] + [VMEM] * 11,
        out_specs=(VMEM, VMEM),
        scratch_shapes=[pltpu.VMEM((2 * depth, nodes), jnp.bfloat16)],
        compiler_params=PARAMS,
    )(tile_columns.reshape(-1), tile_count, place, *pieces, adjacency_tiles, w, cotangent)
    parts = lax.all_to_all(grad, ALL, split_axis=0, concat_axis=0, tiled=True)
    mine = jnp.sum(parts, axis=0)
    total = lax.all_to_all(
        jnp.broadcast_to(mine[None], (depth, 2, hidden)), ALL, split_axis=0, concat_axis=0, tiled=True
    )
    return hidden_out, total[:, 0], total[:, 1]


def solution(mesh):
    return jax.shard_map(
        per_device,
        mesh=mesh,
        in_specs=(
            P(ALL, None),
            P(),
            P(),
            P(ALL, None, None, None),
            P(ALL, None),
            P(ALL),
            P(ALL, None),
        ),
        out_specs=(P(ALL, None), P(), P()),
        check_vma=False,
    )
```

time: 102 us -> 90.7 us (0.89)
  starting transfers between devices: 27.8 us -> 17.9 us
  waiting for transfers between devices: 23.4 us -> 29.2 us
  local copies, waits for them, and re-layouts: 6.89 us -> 3.54 us
  other arithmetic: 2.91 us -> 0.62 us
  Pallas kernels: 7.61 us -> 6.13 us
    ppermute x10 -> x7, starting transfers between devices: 20.1 us -> 10.1 us  [send(): return lax.ppermute(array, ALL, pairs)]
    ppermute x10 -> x7, waiting for transfers between devices: 8.6 us -> 14.7 us  [send(): return lax.ppermute(array, ALL, pairs)]
    pallas_call x1, Pallas kernels: 6.56 us -> 3.82 us  [per_device(): pl.pallas_call(layer_kernel, out_shape=(jax.ShapeDtypeStruct((nodes, hidd...]
    unnamed x1 -> x0, other arithmetic: 2.49 us -> none
    reshape x3 -> x0, local copies, waits for them, and re-layouts: 1.61 us -> none  [the longest x2 1.4 us: by_row(): return g.reshape(128, -1)]
    broadcast_in_dim x1 -> x0, local copies, waits for them, and re-layouts: 1.17 us -> none  [per_device(): out = jnp.broadcast_to(out, (4, 4, 256, size)).reshape(16, 256, size)]
    pallas_call x0 -> x1, Pallas kernels: none -> 1.09 us  [per_device(): pl.pallas_call(spread_kernel, out_shape=jax.ShapeDtypeStruct((4, 4, 256,...]
    unnamed x22 -> x21, local copies, waits for them, and re-layouts: 2.96 us -> 2.88 us
  transfers between devices with their start and end apart: 11 -> 8, of which waited for: 3 -> 6; matrix products, arithmetic and copies ran while one was open for 0% -> 1% of each run, Pallas kernels for 0% -> 0%
where the time goes in v3:
time: 90.7 us; the launch traced here: 90.4 us
  blocking collectives  32.2 us (36%)
  waiting for transfers between devices  29.2 us (32%)
  starting transfers between devices  17.9 us (20%)
  Pallas kernels  6.13 us (7%)
  local copies, waits for them, and re-layouts  3.54 us (4%)
    all_to_all x1, blocking collectives, per_device(): parts = lax.all_to_all(grad, ALL, split_axis=0, concat_axis=0, tiled=True)  17 us
    all_to_all x1, blocking collectives, per_device(): lax.all_to_all(jnp.broadcast_to(mine[None], (depth, 2, hidden)), ALL, spl...  15.2 us
    ppermute x7, waiting for transfers between devices, send(): return lax.ppermute(array, ALL, pairs)  14.7 us
    all_to_all x1, waiting for transfers between devices, per_device(): lax.all_to_all(out, ALL, split_axis=0, concat_axis=0, tiled=True, axis_in...  14.5 us
    ppermute x7, starting transfers between devices, send(): return lax.ppermute(array, ALL, pairs)  10.1 us
    all_to_all x1, starting transfers between devices, per_device(): lax.all_to_all(out, ALL, split_axis=0, concat_axis=0, tiled=True, axis_in...  7.72 us
    pallas_call x1, Pallas kernels, per_device(): pl.pallas_call(layer_kernel, out_shape=(jax.ShapeDtypeStruct((nodes, hidd...  3.82 us
    unnamed x21, local copies, waits for them, and re-layouts  2.88 us
  transfers between devices with their start and end apart: 8, of which 6 were waited for; matrix products, arithmetic and copies ran while one was open for 1% of the time, Pallas kernels for 0%

profile of v3, /device:TPU:1, one launch (start us, length us, event | category | flops | bytes accessed | tf_op | source)
XLA Modules:
  0.0 90.4 jit_solution(16514935730858986640)
XLA Ops:
  0.7 1.0 %copy-done.1 = bf16[1,131072]{1,0:T(2,128)(2,1)S(1)} copy-done((bf16[1,131072]{1,0:T(2,128)(2,1)S(1)}, bf16[1,131072]{1,0:T(2,128)(2,1)}, u32[]{:S(2)}) %copy-start.1) | copy-done | bytes 262168
  1.7 1.1 %shard_map.103 = bf16[4,4,256,128]{3,2,1,0:T(8,128)(2,1)} custom-call(bf16[1,131072]{1,0:T(2,128)(2,1)S(1)} %copy-done.1), custom_call_target="tpu_custom_call" | custom-call | tf_op jit(solution)/shard_map/pallas_call | solution.py:123
  2.8 7.7 %all-to-all-start = ((bf16[16,256,128]{2,1,0:T(8,128)(2,1)}), bf16[16,256,128]{2,1,0:T(8,128)(2,1)S(1)}, u32[]{:S(2)}, u32[]{:S(2)}) async-start(bf16[16,256,128]{2,1,0:T(8,128)(2,1)} %bitcast.5), calls=%async_computation | async-start | bytes 2097152 | tf_op jit(solution)/shard_map/all_to_all | solution.py:130
  10.7 0.1 broadcast_multiply_fusion
  10.9 14.5 %all-to-all-done.in_ref = bf16[16,256,128]{2,1,0:T(8,128)(2,1)S(1)} async-done(((bf16[16,256,128]{2,1,0:T(8,128)(2,1)}), bf16[16,256,128]{2,1,0:T(8,128)(2,1)S(1)}, u32[]{:S(2)}, u32[]{:S(2)}) %all-to-all-start) | async-done | bytes 1048608 | tf_op jit(solution)/shard_map/all_to_all | solution.py:130
  25.3 1.2 %shard_map.104 = (bf16[128,16,128]{2,1,0:T(8,128)(2,1)}, bf16[128,16,128]{2,1,0:T(8,128)(2,1)}) custom-call(s32[1]{0:T(128)} %bitcast.1.core, bf16[16,256,128]{2,1,0:T(8,128)(2,1)S(1)} %all-to-all-done.in_ref), custom_call_target="tpu_custom_call" | custom-call | tf_op jit(solution)/shard_map/pallas_call | solution.py:134
  26.5 1.6 %collective-permute-start = (bf16[128,16,128]{2,1,0:T(8,128)(2,1)}, bf16[128,16,128]{2,1,0:T(8,128)(2,1)S(1)}, u32[]{:S(2)}, u32[]{:S(2)}) collective-permute-start(bf16[128,16,128]{2,1,0:T(8,128)(2,1)} %get-tuple-element.7.refs_0_), channel_id=1, source_target_pairs={{0,4},{1,5},{2,6},{3,7},{4,8},{5,9},{6,10},{7,11},{8,12},{9,13},{1... | collective-permute-start | bytes 1572872 | tf_op jit(solution)/shard_map/ppermute | solution.py:106
  28.2 3.9 %collective-permute-start.5 = (bf16[128,16,128]{2,1,0:T(8,128)(2,1)}, bf16[128,16,128]{2,1,0:T(8,128)(2,1)S(1)}, u32[]{:S(2)}, u32[]{:S(2)}) collective-permute-start(bf16[128,16,128]{2,1,0:T(8,128)(2,1)} %get-tuple-element.8), channel_id=1, source_target_pairs={{0,28},{1,29},{2,30},{3,31},{4,16},{5,17},{6,18},{7,19},{8,20},{9,... | collective-permute-start | bytes 1572872 | tf_op jit(solution)/shard_map/ppermute | solution.py:106
  32.5 1.5 %collective-permute-start.1 = (bf16[128,16,128]{2,1,0:T(8,128)(2,1)}, bf16[128,16,128]{2,1,0:T(8,128)(2,1)}, u32[]{:S(2)}, u32[]{:S(2)}) collective-permute-start(bf16[128,16,128]{2,1,0:T(8,128)(2,1)} %get-tuple-element.7.refs_0_), channel_id=1, source_target_pairs={{0,12},{1,13},{2,14},{3,15},{4,0},{5,1},{6,2},{7,3},{8,4},{9,5},{1... | collective-permute-start | bytes 1572872 | tf_op jit(solution)/shard_map/ppermute | solution.py:106
  33.9 1.2 %collective-permute-start.4 = (bf16[128,16,128]{2,1,0:T(8,128)(2,1)}, bf16[128,16,128]{2,1,0:T(8,128)(2,1)}, u32[]{:S(2)}, u32[]{:S(2)}) collective-permute-start(bf16[128,16,128]{2,1,0:T(8,128)(2,1)} %get-tuple-element.8), channel_id=1, source_target_pairs={{0,20},{1,21},{2,22},{3,23},{4,24},{5,25},{6,26},{7,27},{8,28},{9,... | collective-permute-start | bytes 1572872 | tf_op jit(solution)/shard_map/ppermute | solution.py:106
  35.1 0.7 collective-permute-start.3
  35.8 1.5 %collective-permute-done.refs_1_ = bf16[128,16,128]{2,1,0:T(8,128)(2,1)S(1)} collective-permute-done((bf16[128,16,128]{2,1,0:T(8,128)(2,1)}, bf16[128,16,128]{2,1,0:T(8,128)(2,1)S(1)}, u32[]{:S(2)}, u32[]{:S(2)}) %collective-permute-start) | collective-permute-done | bytes 524320 | tf_op jit(solution)/shard_map/ppermute | solution.py:106
  37.4 3.5 %collective-permute-done.5.refs_6_ = bf16[128,16,128]{2,1,0:T(8,128)(2,1)S(1)} collective-permute-done((bf16[128,16,128]{2,1,0:T(8,128)(2,1)}, bf16[128,16,128]{2,1,0:T(8,128)(2,1)S(1)}, u32[]{:S(2)}, u32[]{:S(2)}) %collective-permute-start.5) | collective-permute-done | bytes 524320 | tf_op jit(solution)/shard_map/ppermute | solution.py:106
  40.9 1.3 %collective-permute-start.6 = (bf16[128,16,128]{2,1,0:T(8,128)(2,1)S(1)}, bf16[128,16,128]{2,1,0:T(8,128)(2,1)}, u32[]{:S(2)}, u32[]{:S(2)}) collective-permute-start(bf16[128,16,128]{2,1,0:T(8,128)(2,1)S(1)} %collective-permute-done.5.refs_6_), channel_id=1, source_target_pairs={{0,3},{1,0},{2,1},{3,2},{4,7},{5,4},{6,5},{7,6},{8,11},{9,8},{10,9... | collective-permute-start | bytes 1572872 | tf_op jit(solution)/shard_map/ppermute | solution.py:106
  42.5 5.3 %collective-permute-done.1.refs_2_ = bf16[128,16,128]{2,1,0:T(8,128)(2,1)} collective-permute-done((bf16[128,16,128]{2,1,0:T(8,128)(2,1)}, bf16[128,16,128]{2,1,0:T(8,128)(2,1)}, u32[]{:S(2)}, u32[]{:S(2)}) %collective-permute-start.1) | collective-permute-done | bytes 524320 | tf_op jit(solution)/shard_map/ppermute | solution.py:106
  47.7 2.1 %collective-permute-done.2.refs_3_ = bf16[128,16,128]{2,1,0:T(8,128)(2,1)} collective-permute-done((bf16[128,16,128]{2,1,0:T(8,128)(2,1)S(1)}, bf16[128,16,128]{2,1,0:T(8,128)(2,1)}, u32[]{:S(2)}, u32[]{:S(2)}) %collective-permute-start.2) | collective-permute-done | bytes 524320 | tf_op jit(solution)/shard_map/ppermute | solution.py:106
  49.8 2.3 %collective-permute-done.6.refs_7_ = bf16[128,16,128]{2,1,0:T(8,128)(2,1)} collective-permute-done((bf16[128,16,128]{2,1,0:T(8,128)(2,1)S(1)}, bf16[128,16,128]{2,1,0:T(8,128)(2,1)}, u32[]{:S(2)}, u32[]{:S(2)}) %collective-permute-start.6) | collective-permute-done | bytes 524320 | tf_op jit(solution)/shard_map/ppermute | solution.py:106
  52.1 1.0 %copy-done.2 = bf16[1024,256]{1,0:T(8,128)(2,1)S(1)} copy-done((bf16[1024,256]{1,0:T(8,128)(2,1)S(1)}, bf16[1024,256]{1,0:T(8,128)(2,1)}, u32[]{:S(2)}) %copy-start.2) | copy-done | bytes 524312
  53.2 3.8 %shard_map.105 = (bf16[1024,256]{1,0:T(8,128)(2,1)}, f32[128,2,256]{2,1,0:T(2,128)S(1)}) custom-call(s32[64]{0:T(128)S(1)} %reshape.92.columns, s32[8]{0:T(128)S(1)} %copy-done.3, s32[19]{0:T(128)S(1)} %pad_add_fusion.2.place, bf16[128,16,128]{2,1,0:T(8,128)(2,1)} %get-tuple-element.7.refs_0_, bf16[128,16,128]{2,1,0:T(8,128)(2,1)S(1)} %collective-permute-done.refs_1_, ...), custom_call_target="tpu_custom_call" | custom-call | tf_op jit(solution)/shard_map/pallas_call | solution.py:157
  57.0 17.0 %all_to_all.15 = f32[128,2,256]{2,1,0:T(2,128)S(1)} all-to-all(f32[128,2,256]{2,1,0:T(2,128)S(1)} %get-tuple-element.10), channel_id=1, replica_groups=mesh['blk'=8,'feat'=16] {'blk','feat'}, dimensions={0} | all-to-all | bytes 524288 | tf_op jit(solution)/shard_map/all_to_all | solution.py:168
  74.0 0.1 reduce_sum.9
  74.2 15.2 %all_to_all.16 = f32[128,2,256]{2,1,0:T(2,128)S(1)} all-to-all(f32[128,2,256]{2,1,0:T(2,128)S(1)} %broadcast_in_dim.9), channel_id=1, replica_groups=mesh['blk'=8,'feat'=16] {'blk','feat'}, dimensions={0} | all-to-all | bytes 524288 | tf_op jit(solution)/shard_map/all_to_all | solution.py:170
  89.4 0.2 fusion.4
  89.6 0.7 copy_bitcast_fusion
  (38 shorter events, 0.9 us)
Async XLA Ops:
  0.6 10.1 %copy-start.7 = (s32[4]{0:T(128)S(1)}, s32[4]{0:T(128)}, u32[]{:S(2)}) copy-start(s32[4]{0:T(128)} %constant.71.clone) | copy-start | bytes 52
  0.6 1.0 %copy-start.1 = (bf16[1,131072]{1,0:T(2,128)(2,1)S(1)}, bf16[1,131072]{1,0:T(2,128)(2,1)}, u32[]{:S(2)}) copy-start(bf16[1,131072]{1,0:T(2,128)(2,1)} %in_ref.1) | copy-start | bytes 786436
  1.7 8.9 %copy-start.6 = (s32[8,8]{1,0:T(8,128)S(1)}, s32[8,8]{1,0:T(8,128)}, u32[]{:S(2)}) copy-start(s32[8,8]{1,0:T(8,128)} %param.12) | copy-start | bytes 772
  1.7 30.6 %copy-start.4 = (bf16[128,256]{1,0:T(8,128)(2,1)S(1)}, bf16[128,256]{1,0:T(8,128)(2,1)}, u32[]{:S(2)}) copy-start(bf16[128,256]{1,0:T(8,128)(2,1)} %param.9) | copy-start | bytes 196612
  2.8 29.7 %copy-start.5 = (bf16[128,256]{1,0:T(8,128)(2,1)S(1)}, bf16[128,256]{1,0:T(8,128)(2,1)}, u32[]{:S(2)}) copy-start(bf16[128,256]{1,0:T(8,128)(2,1)} %param.10) | copy-start | bytes 196612
  2.8 49.4 %copy-start = (bf16[8,8,128,128]{3,2,1,0:T(8,128)(2,1)S(1)}, bf16[8,8,128,128]{3,2,1,0:T(8,128)(2,1)}, u32[]{:S(2)}) copy-start(bf16[8,8,128,128]{3,2,1,0:T(8,128)(2,1)} %refs_8_.1) | copy-start | bytes 6291460
  2.8 49.4 %copy-start.3 = (s32[8]{0:T(128)S(1)}, s32[8]{0:T(128)}, u32[]{:S(2)}) copy-start(s32[8]{0:T(128)} %counts.1) | copy-start | bytes 100
  2.8 22.5 %all-to-all-start = ((bf16[16,256,128]{2,1,0:T(8,128)(2,1)}), bf16[16,256,128]{2,1,0:T(8,128)(2,1)S(1)}, u32[]{:S(2)}, u32[]{:S(2)}) async-start(bf16[16,256,128]{2,1,0:T(8,128)(2,1)} %bitcast.5), calls=%async_computation | async-start | bytes 2097152 | tf_op jit(solution)/shard_map/all_to_all | solution.py:130
  26.5 10.8 %collective-permute-start = (bf16[128,16,128]{2,1,0:T(8,128)(2,1)}, bf16[128,16,128]{2,1,0:T(8,128)(2,1)S(1)}, u32[]{:S(2)}, u32[]{:S(2)}) collective-permute-start(bf16[128,16,128]{2,1,0:T(8,128)(2,1)} %get-tuple-element.7.refs_0_), channel_id=1, source_target_pairs={{0,4},{1,5},{2,6},{3,7},{4,8},{5,9},{6,10},{7,11},{8,12},{9,13},{1... | collective-permute-start | bytes 1572872 | tf_op jit(solution)/shard_map/ppermute | solution.py:106
  28.2 12.7 %collective-permute-start.5 = (bf16[128,16,128]{2,1,0:T(8,128)(2,1)}, bf16[128,16,128]{2,1,0:T(8,128)(2,1)S(1)}, u32[]{:S(2)}, u32[]{:S(2)}) collective-permute-start(bf16[128,16,128]{2,1,0:T(8,128)(2,1)} %get-tuple-element.8), channel_id=1, source_target_pairs={{0,28},{1,29},{2,30},{3,31},{4,16},{5,17},{6,18},{7,19},{8,20},{9,... | collective-permute-start | bytes 1572872 | tf_op jit(solution)/shard_map/ppermute | solution.py:106
  32.5 15.2 %collective-permute-start.1 = (bf16[128,16,128]{2,1,0:T(8,128)(2,1)}, bf16[128,16,128]{2,1,0:T(8,128)(2,1)}, u32[]{:S(2)}, u32[]{:S(2)}) collective-permute-start(bf16[128,16,128]{2,1,0:T(8,128)(2,1)} %get-tuple-element.7.refs_0_), channel_id=1, source_target_pairs={{0,12},{1,13},{2,14},{3,15},{4,0},{5,1},{6,2},{7,3},{8,4},{9,5},{1... | collective-permute-start | bytes 1572872 | tf_op jit(solution)/shard_map/ppermute | solution.py:106
  33.9 13.8 %collective-permute-start.4 = (bf16[128,16,128]{2,1,0:T(8,128)(2,1)}, bf16[128,16,128]{2,1,0:T(8,128)(2,1)}, u32[]{:S(2)}, u32[]{:S(2)}) collective-permute-start(bf16[128,16,128]{2,1,0:T(8,128)(2,1)} %get-tuple-element.8), channel_id=1, source_target_pairs={{0,20},{1,21},{2,22},{3,23},{4,24},{5,25},{6,26},{7,27},{8,28},{9,... | collective-permute-start | bytes 1572872 | tf_op jit(solution)/shard_map/ppermute | solution.py:106
  35.1 12.6 %collective-permute-start.3 = (bf16[128,16,128]{2,1,0:T(8,128)(2,1)}, bf16[128,16,128]{2,1,0:T(8,128)(2,1)}, u32[]{:S(2)}, u32[]{:S(2)}) collective-permute-start(bf16[128,16,128]{2,1,0:T(8,128)(2,1)} %get-tuple-element.8), channel_id=1, source_target_pairs={{0,16},{1,17},{2,18},{3,19},{4,20},{5,21},{6,22},{7,23},{8,24},{9,... | collective-permute-start | bytes 1572872 | tf_op jit(solution)/shard_map/ppermute | solution.py:106
  37.4 12.5 %collective-permute-start.2 = (bf16[128,16,128]{2,1,0:T(8,128)(2,1)S(1)}, bf16[128,16,128]{2,1,0:T(8,128)(2,1)}, u32[]{:S(2)}, u32[]{:S(2)}) collective-permute-start(bf16[128,16,128]{2,1,0:T(8,128)(2,1)S(1)} %collective-permute-done.refs_1_), channel_id=1, source_target_pairs={{0,4},{1,5},{2,6},{3,7},{4,8},{5,9},{6,10},{7,11},{8,12},{9,13},{1... | collective-permute-start | bytes 1572872 | tf_op jit(solution)/shard_map/ppermute | solution.py:106
  40.9 11.2 %collective-permute-start.6 = (bf16[128,16,128]{2,1,0:T(8,128)(2,1)S(1)}, bf16[128,16,128]{2,1,0:T(8,128)(2,1)}, u32[]{:S(2)}, u32[]{:S(2)}) collective-permute-start(bf16[128,16,128]{2,1,0:T(8,128)(2,1)S(1)} %collective-permute-done.5.refs_6_), channel_id=1, source_target_pairs={{0,3},{1,0},{2,1},{3,2},{4,7},{5,4},{6,5},{7,6},{8,11},{9,8},{10,9... | collective-permute-start | bytes 1572872 | tf_op jit(solution)/shard_map/ppermute | solution.py:106
  52.1 1.0 %copy-start.2 = (bf16[1024,256]{1,0:T(8,128)(2,1)S(1)}, bf16[1024,256]{1,0:T(8,128)(2,1)}, u32[]{:S(2)}) copy-start(bf16[1024,256]{1,0:T(8,128)(2,1)} %refs_10_.1) | copy-start | bytes 1572868

commit v4 on v3

v4 whole, which is shorter than its diff:
```python
import jax
import jax.numpy as jnp
from jax import lax
from jax.experimental import pallas as pl
from jax.experimental.pallas import tpu as pltpu
from jax.sharding import PartitionSpec as P

ALL = ("blk", "feat")
CONTRACT_FIRST = (((0,), (0,)), ((), ()))
CONTRACT_LAST = (((1,), (1,)), ((), ()))
RANGE = range(4)


def device(x, c, y, z):
    return (x * 2 + c) * 16 + y * 4 + z


PLANES = [[device(x, 0, y, z) for x in RANGE for z in RANGE] for y in RANGE]
PLANES += [[device(x, 1, y, z) for x in RANGE for y in RANGE] for z in RANGE]


def ring(step, to_other_core=0):
    pairs = []
    for x in RANGE:
        for y in RANGE:
            for z in RANGE:
                pairs.append((device(x, 0, y, z), device(x, to_other_core, (y + step) % 4, z)))
                pairs.append((device(x, 1, y, z), device(x, 1 - to_other_core, y, (z + step) % 4)))
    return pairs


RIGHT, LEFT, FAR = ring(1), ring(-1), ring(2)
RIGHT_ACROSS, LEFT_ACROSS, FAR_ACROSS = ring(1, 1), ring(-1, 1), ring(2, 1)
OTHER_CORE = [(d, d ^ 16) for d in range(128)]


def spread_kernel(in_ref, out_ref):
    copies, rows, size = out_ref.shape[1:]
    step = 16
    for k in range(in_ref.shape[1] // (step * size)):
        flat = in_ref[0:1, k * step * size : (k + 1) * step * size]
        block = flat.astype(jnp.float32).reshape(step, size).astype(jnp.bfloat16)
        x, first = divmod(k * step, rows)
        for copy in range(copies):
            out_ref[x, copy, first : first + step] = block


def arrange_kernel(place, w_self_ref, w_neigh_ref, out_ref, wide_ref, placed_ref):
    depth = w_self_ref.shape[0]
    wide_ref[:depth] = w_self_ref[...].astype(jnp.float32)
    wide_ref[depth:] = w_neigh_ref[...].astype(jnp.float32)
    for at, row in feature_rows(place):
        for s in range(2):
            placed_ref[s * depth + at : s * depth + at + 1] = wide_ref[pl.ds(s * depth + row, 1)]
    out_ref[...] = placed_ref[...].astype(jnp.bfloat16)


def feature_rows(place):
    for k in range(8):
        first, stride = place[k], place[8 + k // 4]
        for i in range(16):
            yield k * 16 + i, first + (i // 4) * 32 + (i % 4) * stride


def select_kernel(meta, lists, in_ref, w_ref, *refs):
    out_refs, rows_ref, built_ref, sems = refs[:8], *refs[8:]
    half = rows_ref.shape[0] // 2
    step = 16
    blocks, slots = lists.shape[2:]
    copies = []
    for part in range(2):
        first = ((meta[0] + part) % 2) * half
        for k in range(half // step):
            start = pl.multiple_of(first + k * step, step)
            rows_ref[pl.ds(part * half + k * step, step)] = jnp.swapaxes(
                in_ref[:, pl.ds(start, step), :], 0, 1
            )
    for place in (3, 1, 2, 0):
        for part in range(2):
            m = 2 * place + part
            for b in range(blocks):
                for t in range(slots):
                    block = lists[place, part, b, t]
                    built_ref[m, b * slots + t] = rows_ref[part * half + block]
                own = meta[1 + place] * blocks + b
                built_ref[m, blocks * slots + b] = rows_ref[part * half + own]
            copy = pltpu.make_async_copy(built_ref.at[m], out_refs[m], sems.at[m])
            copy.start()
            copies.append(copy)
    for copy in copies:
        copy.wait()


def aggregate_kernel(counts, *refs):
    pieces = refs[:8]
    tiles_ref, both_ref = refs[8:]
    blocks, slots, size, _ = tiles_ref.shape
    depth = both_ref.shape[0] // 2

    def features_of(k):
        return jnp.concatenate([piece[k] for piece in pieces], axis=0)

    for b in range(blocks):
        nodes = slice(b * size, (b + 1) * size)
        both_ref[:depth, nodes] = features_of(blocks * slots + b)
        x = jnp.concatenate([features_of(b * slots + t) for t in range(slots)], axis=1)
        tiles = []
        for t in range(slots):
            tile = tiles_ref[b, t]
            tiles.append(jnp.where(t < counts[b], tile, jnp.zeros_like(tile)))
        gathered = lax.dot_general(
            x, jnp.concatenate(tiles, axis=1), CONTRACT_LAST, preferred_element_type=jnp.float32
        )
        both_ref[depth:, nodes] = gathered.astype(jnp.bfloat16)


def layer_kernel(place, both_ref, w_ref, cot_ref, hidden_ref, grad_ref):
    depth = both_ref.shape[0] // 2
    both = both_ref[...]
    pre = lax.dot_general(both, w_ref[...], CONTRACT_FIRST, preferred_element_type=jnp.float32)
    s = jax.nn.sigmoid(pre)
    hidden = pre * s
    hidden_ref[...] = hidden.astype(jnp.bfloat16)
    grad_pre = (cot_ref[...].astype(jnp.float32) * (s + hidden * (1.0 - s))).astype(jnp.bfloat16)
    grad = jnp.dot(both, grad_pre, preferred_element_type=jnp.float32)
    for at, row in feature_rows(place):
        for s in range(2):
            grad_ref[row, s : s + 1] = grad[s * depth + at : s * depth + at + 1]


VMEM = pl.BlockSpec(memory_space=pltpu.VMEM)
SMEM = pl.BlockSpec(memory_space=pltpu.SMEM)
HBM = pl.BlockSpec(memory_space=pltpu.HBM)
ANY = pl.BlockSpec(memory_space=pl.ANY)
PARAMS = pltpu.CompilerParams(vmem_limit_bytes=24 * 1024 * 1024)


def send(array, pairs):
    return lax.ppermute(array, ALL, pairs)


def per_device(features, w_self, w_neigh, adjacency_tiles, tile_columns, tile_count, cotangent):
    depth, hidden = w_self.shape
    nodes = cotangent.shape[0]
    blocks, slots, size, _ = adjacency_tiles.shape
    core = lax.axis_index("blk") % 2
    feat = lax.axis_index("feat")
    y, z = feat // 4, feat % 4

    out = pl.pallas_call(
        spread_kernel,
        out_shape=jax.ShapeDtypeStruct((4, 4, 256, size), jnp.bfloat16),
        in_specs=[VMEM],
        out_specs=VMEM,
        compiler_params=PARAMS,
    )(features).reshape(16, 256, size)
    rows = lax.all_to_all(
        out, ALL, split_axis=0, concat_axis=0, tiled=True, axis_index_groups=PLANES
    )
    steps = jnp.array([0, 3, 1, 2], jnp.int32)
    at = (jnp.where(core == 0, y, z) + steps) % 4
    partner_at = (jnp.where(core == 0, z, y) + jnp.array([2, 3, 1, 0], jnp.int32)) % 4
    chip = jnp.where(core == 0, at * 4 + z, y * 4 + at)
    meta = jnp.concatenate([core[None], chip]).astype(jnp.int32)
    cores = jnp.stack([core, 1 - core])
    strides = jnp.where(cores == 0, 1, 4)
    first_rows = cores[:, None] * 16 + jnp.stack([at, partner_at]) * (4 // strides)[:, None]
    place = jnp.concatenate([first_rows.reshape(-1), strides]).astype(jnp.int32)
    w = pl.pallas_call(
        arrange_kernel,
        out_shape=jax.ShapeDtypeStruct((2 * depth, hidden), jnp.bfloat16),
        in_specs=[SMEM, VMEM, VMEM],
        out_specs=VMEM,
        scratch_shapes=[pltpu.VMEM((2 * depth, hidden), jnp.float32)] * 2,
        compiler_params=PARAMS,
    )(place, w_self, w_neigh)

    here = jnp.stack([tile_columns, send(tile_columns, OTHER_CORE)])
    lists = jnp.stack([here, send(here, RIGHT), send(here, LEFT), send(here, FAR)])
    listed = blocks * slots + blocks
    piece = jax.ShapeDtypeStruct((listed, 16, size), jnp.bfloat16)
    own, across, own_l, across_l, own_r, across_r, own_f, across_f = pl.pallas_call(
        select_kernel,
        out_shape=(piece,) * 8,
        in_specs=[SMEM, SMEM, VMEM, ANY],
        out_specs=(HBM,) * 8,
        scratch_shapes=[
            pltpu.VMEM((256, 16, size), jnp.bfloat16),
            pltpu.VMEM((8, listed, 16, size), jnp.bfloat16),
            pltpu.SemaphoreType.DMA((8,)),
        ],
        compiler_params=PARAMS,
    )(meta, lists, rows, w)
    pieces = [own, send(own_r, RIGHT), send(own_l, LEFT), send(own_f, FAR)]
    pieces += [send(across_f, FAR_ACROSS), send(across_r, RIGHT_ACROSS), send(across_l, LEFT_ACROSS)]
    pieces += [send(across, OTHER_CORE)]

    both = pl.pallas_call(
        aggregate_kernel,
        out_shape=jax.ShapeDtypeStruct((2 * depth, nodes), jnp.bfloat16),
        in_specs=[SMEM] + [VMEM] * 9,
        out_specs=VMEM,
        compiler_params=PARAMS,
    )(tile_count, *pieces, adjacency_tiles)
    hidden_out, grad = pl.pallas_call(
        layer_kernel,
        out_shape=(
            jax.ShapeDtypeStruct((nodes, hidden), jnp.bfloat16),
            jax.ShapeDtypeStruct((depth, 2, hidden), jnp.float32),
        ),
        in_specs=[SMEM] + [VMEM] * 3,
        out_specs=(VMEM, VMEM),
        compiler_params=PARAMS,
    )(place, both, w, cotangent)
    parts = lax.all_to_all(grad, ALL, split_axis=0, concat_axis=0, tiled=True)
    mine = jnp.sum(parts, axis=0).astype(jnp.bfloat16)
    total = lax.all_to_all(
        jnp.broadcast_to(mine[None], (depth, 2, hidden)), ALL, split_axis=0, concat_axis=0, tiled=True
    )
    total = total.astype(jnp.float32)
    return hidden_out, total[:, 0], total[:, 1]


def solution(mesh):
    return jax.shard_map(
        per_device,
        mesh=mesh,
        in_specs=(
            P(ALL, None),
            P(),
            P(),
            P(ALL, None, None, None),
            P(ALL, None),
            P(ALL),
            P(ALL, None),
        ),
        out_specs=(P(ALL, None), P(), P()),
        check_vma=False,
    )
```

time: 90.7 us -> 86.3 us (0.951)
  waiting for transfers between devices: 29.2 us -> 16.1 us
  starting transfers between devices: 17.9 us -> 27.9 us
  blocking collectives: 32.2 us -> 30.1 us
  Pallas kernels: 6.13 us -> 7.74 us
    ppermute x7 -> x11, starting transfers between devices: 10.1 us -> 20.9 us  [send(): return lax.ppermute(array, ALL, pairs)]
    all_to_all x1, waiting for transfers between devices: 14.5 us -> 6.71 us  [per_device(): lax.all_to_all(out, ALL, split_axis=0, concat_axis=0, tiled=True, axis_in...]
    ppermute x7 -> x11, waiting for transfers between devices: 14.7 us -> 9.43 us  [send(): return lax.ppermute(array, ALL, pairs)]
    pallas_call x1 -> x3, Pallas kernels: 1.22 us -> 4.79 us  [the longest x1 2.48 us: per_device(): pl.pallas_call(select_kernel, out_shape=(piece,) * 8, in_specs=[SMEM, SME...]
    pallas_call x1, Pallas kernels: 3.82 us -> 1.84 us  [per_device(): pl.pallas_call(layer_kernel, out_shape=(jax.ShapeDtypeStruct((nodes, hidd...]
    all_to_all x1, blocking collectives: 17 us -> 15.9 us  [per_device(): parts = lax.all_to_all(grad, ALL, split_axis=0, concat_axis=0, tiled=True)]
    all_to_all x1, blocking collectives: 15.2 us -> 14.2 us  [per_device(): lax.all_to_all(jnp.broadcast_to(mine[None], (depth, 2, hidden)), ALL, spl...]
    unnamed x21 -> x20, local copies, waits for them, and re-layouts: 2.88 us -> 2.41 us
  transfers between devices with their start and end apart: 8 -> 12, of which waited for: 6 -> 6; matrix products, arithmetic and copies ran while one was open for 1% -> 1% of each run, Pallas kernels for 0% -> 2%
where the time goes in v4:
time: 86.3 us; the launch traced here: 86 us
  blocking collectives  30.1 us (35%)
  starting transfers between devices  27.9 us (32%)
  waiting for transfers between devices  16.1 us (19%)
  Pallas kernels  7.74 us (9%)
  local copies, waits for them, and re-layouts  2.74 us (3%)
    ppermute x11, starting transfers between devices, send(): return lax.ppermute(array, ALL, pairs)  20.9 us
    all_to_all x1, blocking collectives, per_device(): parts = lax.all_to_all(grad, ALL, split_axis=0, concat_axis=0, tiled=True)  15.9 us
    all_to_all x1, blocking collectives, per_device(): lax.all_to_all(jnp.broadcast_to(mine[None], (depth, 2, hidden)), ALL, spl...  14.2 us
    ppermute x11, waiting for transfers between devices, send(): return lax.ppermute(array, ALL, pairs)  9.43 us
    all_to_all x1, starting transfers between devices, per_device(): lax.all_to_all(out, ALL, split_axis=0, concat_axis=0, tiled=True, axis_in...  6.97 us
    all_to_all x1, waiting for transfers between devices, per_device(): lax.all_to_all(out, ALL, split_axis=0, concat_axis=0, tiled=True, axis_in...  6.71 us
    pallas_call x1, Pallas kernels, per_device(): pl.pallas_call(select_kernel, out_shape=(piece,) * 8, in_specs=[SMEM, SME...  2.48 us
    unnamed x20, local copies, waits for them, and re-layouts  2.41 us
  transfers between devices with their start and end apart: 12, of which 6 were waited for; matrix products, arithmetic and copies ran while one was open for 1% of the time, Pallas kernels for 2%

profile of v4, /device:TPU:1, one launch (start us, length us, event | category | flops | bytes accessed | tf_op | source)
XLA Modules:
  0.0 86.0 jit_solution(16338668209912723052)
XLA Ops:
  0.7 1.5 %collective-permute-start = (s32[8,8]{1,0:T(8,128)}, s32[8,8]{1,0:T(8,128)S(1)}, u32[]{:S(2)}, u32[]{:S(2)}) collective-permute-start(s32[8,8]{1,0:T(8,128)} %param.13), channel_id=1, source_target_pairs={{0,16},{1,17},{2,18},{3,19},{4,20},{5,21},{6,22},{7,23},{8,24},{9,... | collective-permute-start | bytes 776 | tf_op jit(solution)/shard_map/ppermute | solution.py:139
  2.2 1.0 %copy-done.1 = bf16[1,131072]{1,0:T(2,128)(2,1)S(1)} copy-done((bf16[1,131072]{1,0:T(2,128)(2,1)S(1)}, bf16[1,131072]{1,0:T(2,128)(2,1)}, u32[]{:S(2)}) %copy-start.1) | copy-done | bytes 262168
  3.2 1.1 %shard_map.112 = bf16[4,4,256,128]{3,2,1,0:T(8,128)(2,1)} custom-call(bf16[1,131072]{1,0:T(2,128)(2,1)S(1)} %copy-done.1), custom_call_target="tpu_custom_call" | custom-call | tf_op jit(solution)/shard_map/pallas_call | solution.py:150
  4.3 7.0 %all-to-all-start = ((bf16[16,256,128]{2,1,0:T(8,128)(2,1)}), bf16[16,256,128]{2,1,0:T(8,128)(2,1)S(1)}, u32[]{:S(2)}, u32[]{:S(2)}) async-start(bf16[16,256,128]{2,1,0:T(8,128)(2,1)} %bitcast.10), calls=%async_computation | async-start | bytes 2097152 | tf_op jit(solution)/shard_map/all_to_all | solution.py:157
  11.8 3.8 %collective-permute-start.2 = (s32[2,8,8]{2,1,0:T(8,128)S(1)}, s32[2,8,8]{2,1,0:T(8,128)S(1)}, u32[]{:S(2)}, u32[]{:S(2)}) collective-permute-start(s32[2,8,8]{2,1,0:T(8,128)S(1)} %get-tuple-element.30), channel_id=1, source_target_pairs={{0,12},{16,19},{1,13},{17,16},{2,14},{18,17},{3,15},{19,18},{4,0},... | collective-permute-start | bytes 1544 | tf_op jit(solution)/shard_map/ppermute | solution.py:139
  15.7 1.3 %collective-permute-start.3 = (s32[2,8,8]{2,1,0:T(8,128)S(1)}, s32[2,8,8]{2,1,0:T(8,128)S(1)}, u32[]{:S(2)}, u32[]{:S(2)}) collective-permute-start(s32[2,8,8]{2,1,0:T(8,128)S(1)} %get-tuple-element.30), channel_id=1, source_target_pairs={{0,8},{16,18},{1,9},{17,19},{2,10},{18,16},{3,11},{19,17},{4,12},{... | collective-permute-start | bytes 1544 | tf_op jit(solution)/shard_map/ppermute | solution.py:139
  17.0 1.0 %shard_map.113.w_ref = bf16[256,256]{1,0:T(8,128)(2,1)S(1)} custom-call(s32[10]{0:T(128)S(1)} %pad_add_fusion.3.place, bf16[128,256]{1,0:T(8,128)(2,1)S(1)} %copy-done.3, bf16[128,256]{1,0:T(8,128)(2,1)S(1)} %copy-done.4), custom_call_target="tpu_custom_call" | custom-call | tf_op jit(solution)/shard_map/pallas_call | solution.py:169
  18.0 1.6 %collective-permute-done.1 = s32[2,8,8]{2,1,0:T(8,128)S(1)} collective-permute-done((s32[2,8,8]{2,1,0:T(8,128)S(1)}, s32[2,8,8]{2,1,0:T(8,128)S(1)}, u32[]{:S(2)}, u32[]{:S(2)}) %collective-permute-start.1) | collective-permute-done | bytes 544 | tf_op jit(solution)/shard_map/ppermute | solution.py:139
  19.7 6.7 %all-to-all-done.in_ref = bf16[16,256,128]{2,1,0:T(8,128)(2,1)S(1)} async-done(((bf16[16,256,128]{2,1,0:T(8,128)(2,1)}), bf16[16,256,128]{2,1,0:T(8,128)(2,1)S(1)}, u32[]{:S(2)}, u32[]{:S(2)}) %all-to-all-start) | async-done | bytes 1048608 | tf_op jit(solution)/shard_map/all_to_all | solution.py:157
  26.4 2.5 %shard_map.114 = (bf16[72,16,128]{2,1,0:T(8,128)(2,1)S(1)}, bf16[72,16,128]{2,1,0:T(8,128)(2,1)S(1)}, bf16[72,16,128]{2,1,0:T(8,128)(2,1)S(1)}, bf16[72,16,128]{...) custom-call(s32[5]{0:T(128)S(1)} %pad_add_fusion.4.meta, ...), custom_call_target="tpu_custom_call" | custom-call | tf_op jit(solution)/shard_map/pallas_call | solution.py:182
  28.9 1.7 %collective-permute-start.4 = (bf16[72,16,128]{2,1,0:T(8,128)(2,1)S(1)}, bf16[72,16,128]{2,1,0:T(8,128)(2,1)S(1)}, u32[]{:S(2)}, u32[]{:S(2)}) collective-permute-start(bf16[72,16,128]{2,1,0:T(8,128)(2,1)S(1)} %get-tuple-element.14), channel_id=1, source_target_pairs={{0,4},{16,17},{1,5},{17,18},{2,6},{18,19},{3,7},{19,16},{4,8},{20,... | collective-permute-start | bytes 884744 | tf_op jit(solution)/shard_map/ppermute | solution.py:139
  30.5 4.1 %collective-permute-start.5 = (bf16[72,16,128]{2,1,0:T(8,128)(2,1)S(1)}, bf16[72,16,128]{2,1,0:T(8,128)(2,1)S(1)}, u32[]{:S(2)}, u32[]{:S(2)}) collective-permute-start(bf16[72,16,128]{2,1,0:T(8,128)(2,1)S(1)} %get-tuple-element.15), channel_id=1, source_target_pairs={{0,12},{16,19},{1,13},{17,16},{2,14},{18,17},{3,15},{19,18},{4,0},... | collective-permute-start | bytes 884744 | tf_op jit(solution)/shard_map/ppermute | solution.py:139
  34.7 1.1 %collective-permute-start.6 = (bf16[72,16,128]{2,1,0:T(8,128)(2,1)S(1)}, bf16[72,16,128]{2,1,0:T(8,128)(2,1)S(1)}, u32[]{:S(2)}, u32[]{:S(2)}) collective-permute-start(bf16[72,16,128]{2,1,0:T(8,128)(2,1)S(1)} %get-tuple-element.16), channel_id=1, source_target_pairs={{0,8},{16,18},{1,9},{17,19},{2,10},{18,16},{3,11},{19,17},{4,12},{... | collective-permute-start | bytes 884744 | tf_op jit(solution)/shard_map/ppermute | solution.py:139
  35.8 2.8 %collective-permute-start.7 = (bf16[72,16,128]{2,1,0:T(8,128)(2,1)S(1)}, bf16[72,16,128]{2,1,0:T(8,128)(2,1)S(1)}, u32[]{:S(2)}, u32[]{:S(2)}) collective-permute-start(bf16[72,16,128]{2,1,0:T(8,128)(2,1)S(1)} %get-tuple-element.17), channel_id=1, source_target_pairs={{0,24},{16,2},{1,25},{17,3},{2,26},{18,0},{3,27},{19,1},{4,28},{20... | collective-permute-start | bytes 884744 | tf_op jit(solution)/shard_map/ppermute | solution.py:139
  39.0 2.6 %collective-permute-start.9 = (bf16[72,16,128]{2,1,0:T(8,128)(2,1)S(1)}, bf16[72,16,128]{2,1,0:T(8,128)(2,1)S(1)}, u32[]{:S(2)}, u32[]{:S(2)}) collective-permute-start(bf16[72,16,128]{2,1,0:T(8,128)(2,1)S(1)} %get-tuple-element.19), channel_id=1, source_target_pairs={{0,28},{16,3},{1,29},{17,0},{2,30},{18,1},{3,31},{19,2},{4,16},{20... | collective-permute-start | bytes 884744 | tf_op jit(solution)/shard_map/ppermute | solution.py:139
  41.6 3.1 %collective-permute-done.5.refs_2_ = bf16[72,16,128]{2,1,0:T(8,128)(2,1)S(1)} collective-permute-done((bf16[72,16,128]{2,1,0:T(8,128)(2,1)S(1)}, bf16[72,16,128]{2,1,0:T(8,128)(2,1)S(1)}, u32[]{:S(2)}, u32[]{:S(2)}) %collective-permute-start.5) | collective-permute-done | bytes 294944 | tf_op jit(solution)/shard_map/ppermute | solution.py:139
  44.7 2.0 %collective-permute-start.10 = (bf16[72,16,128]{2,1,0:T(8,128)(2,1)S(1)}, bf16[72,16,128]{2,1,0:T(8,128)(2,1)S(1)}, u32[]{:S(2)}, u32[]{:S(2)}) collective-permute-start(bf16[72,16,128]{2,1,0:T(8,128)(2,1)S(1)} %get-tuple-element.20), channel_id=1, source_target_pairs={{0,16},{1,17},{2,18},{3,19},{4,20},{5,21},{6,22},{7,23},{8,24},{9,... | collective-permute-start | bytes 884744 | tf_op jit(solution)/shard_map/ppermute | solution.py:139
  46.7 1.2 %collective-permute-done.7.refs_4_ = bf16[72,16,128]{2,1,0:T(8,128)(2,1)S(1)} collective-permute-done((bf16[72,16,128]{2,1,0:T(8,128)(2,1)S(1)}, bf16[72,16,128]{2,1,0:T(8,128)(2,1)S(1)}, u32[]{:S(2)}, u32[]{:S(2)}) %collective-permute-start.7) | collective-permute-done | bytes 294944 | tf_op jit(solution)/shard_map/ppermute | solution.py:139
  47.9 3.1 %collective-permute-done.8.refs_5_ = bf16[72,16,128]{2,1,0:T(8,128)(2,1)S(1)} collective-permute-done((bf16[72,16,128]{2,1,0:T(8,128)(2,1)S(1)}, bf16[72,16,128]{2,1,0:T(8,128)(2,1)S(1)}, u32[]{:S(2)}, u32[]{:S(2)}) %collective-permute-start.8) | collective-permute-done | bytes 294944 | tf_op jit(solution)/shard_map/ppermute | solution.py:139
  51.0 1.3 %shard_map.115.both_ref = bf16[256,1024]{1,0:T(8,128)(2,1)S(1)} custom-call(s32[8]{0:T(128)S(1)} %copy-done.5, bf16[72,16,128]{2,1,0:T(8,128)(2,1)S(1)} %get-tuple-element.13.refs_0_, bf16[72,16,128]{2,1,0:T(8,128)(2,1)S(1)} %collective-permute-done.4.refs_1_, bf16[72,16,128]{2,1,0:T(8,128)(2,1)S(1)} %collective-permute-done.5.refs_2_, ...), custom_call_target="tpu_custom_call" | custom-call | tf_op jit(solution)/shard_map/pallas_call | solution.py:198
  52.3 1.8 %shard_map.116 = (bf16[1024,256]{1,0:T(8,128)(2,1)}, f32[128,2,256]{2,1,0:T(2,128)S(1)}) custom-call(s32[10]{0:T(128)S(1)} %pad_add_fusion.3.place, bf16[256,1024]{1,0:T(8,128)(2,1)S(1)} %shard_map.115.both_ref, bf16[256,256]{1,0:T(8,128)(2,1)S(1)} %shard_map.113.w_ref, bf16[1024,256]{1,0:T(8,128)(2,1)S(1)} %copy-done.2), custom_call_target="tpu_custom_call" | custom-call | tf_op jit(solution)/shard_map/pallas_call | solution.py:205
  54.2 15.9 %all_to_all.15 = f32[128,2,256]{2,1,0:T(2,128)S(1)} all-to-all(f32[128,2,256]{2,1,0:T(2,128)S(1)} %get-tuple-element.22), channel_id=1, replica_groups=mesh['blk'=8,'feat'=16] {'blk','feat'}, dimensions={0} | all-to-all | bytes 524288 | tf_op jit(solution)/shard_map/all_to_all | solution.py:215
  70.3 14.2 %all_to_all.16 = bf16[128,2,256]{2,1,0:T(2,128)(2,1)S(1)} all-to-all(bf16[128,2,256]{2,1,0:T(2,128)(2,1)S(1)} %broadcast_in_dim.9), channel_id=1, replica_groups=mesh['blk'=8,'feat'=16] {'blk','feat'}, dimensions={0} | all-to-all | bytes 262144 | tf_op jit(solution)/shard_map/all_to_all | solution.py:217
  84.7 0.7 copy.16
  (39 shorter events, 2.1 us)
Async XLA Ops:
  0.6 10.7 %copy-start.8 = (s32[4]{0:T(128)S(1)}, s32[4]{0:T(128)}, u32[]{:S(2)}) copy-start(s32[4]{0:T(128)} %constant.74.clone) | copy-start | bytes 52
  0.6 10.9 %copy-start.7 = (s32[4]{0:T(128)S(1)}, s32[4]{0:T(128)}, u32[]{:S(2)}) copy-start(s32[4]{0:T(128)} %constant.73.clone) | copy-start | bytes 52
  0.7 11.2 %collective-permute-start = (s32[8,8]{1,0:T(8,128)}, s32[8,8]{1,0:T(8,128)S(1)}, u32[]{:S(2)}, u32[]{:S(2)}) collective-permute-start(s32[8,8]{1,0:T(8,128)} %param.13), channel_id=1, source_target_pairs={{0,16},{1,17},{2,18},{3,19},{4,20},{5,21},{6,22},{7,23},{8,24},{9,... | collective-permute-start | bytes 776 | tf_op jit(solution)/shard_map/ppermute | solution.py:139
  2.2 1.0 %copy-start.1 = (bf16[1,131072]{1,0:T(2,128)(2,1)S(1)}, bf16[1,131072]{1,0:T(2,128)(2,1)}, u32[]{:S(2)}) copy-start(bf16[1,131072]{1,0:T(2,128)(2,1)} %in_ref.1) | copy-start | bytes 786436
  3.2 8.6 %copy-start.6 = (s32[8,8]{1,0:T(8,128)S(1)}, s32[8,8]{1,0:T(8,128)}, u32[]{:S(2)}) copy-start(s32[8,8]{1,0:T(8,128)} %param.13) | copy-start | bytes 772
  3.2 13.8 %copy-start.3 = (bf16[128,256]{1,0:T(8,128)(2,1)S(1)}, bf16[128,256]{1,0:T(8,128)(2,1)}, u32[]{:S(2)}) copy-start(bf16[128,256]{1,0:T(8,128)(2,1)} %w_self_ref.1) | copy-start | bytes 196612
  3.2 13.8 %copy-start.4 = (bf16[128,256]{1,0:T(8,128)(2,1)S(1)}, bf16[128,256]{1,0:T(8,128)(2,1)}, u32[]{:S(2)}) copy-start(bf16[128,256]{1,0:T(8,128)(2,1)} %w_neigh_ref.1) | copy-start | bytes 196612
  4.3 46.7 %copy-start = (bf16[8,8,128,128]{3,2,1,0:T(8,128)(2,1)S(1)}, bf16[8,8,128,128]{3,2,1,0:T(8,128)(2,1)}, u32[]{:S(2)}) copy-start(bf16[8,8,128,128]{3,2,1,0:T(8,128)(2,1)} %refs_8_.1) | copy-start | bytes 6291460
  4.3 46.7 %copy-start.5 = (s32[8]{0:T(128)S(1)}, s32[8]{0:T(128)}, u32[]{:S(2)}) copy-start(s32[8]{0:T(128)} %counts.1) | copy-start | bytes 100
  4.3 22.1 %all-to-all-start = ((bf16[16,256,128]{2,1,0:T(8,128)(2,1)}), bf16[16,256,128]{2,1,0:T(8,128)(2,1)S(1)}, u32[]{:S(2)}, u32[]{:S(2)}) async-start(bf16[16,256,128]{2,1,0:T(8,128)(2,1)} %bitcast.10), calls=%async_computation | async-start | bytes 2097152 | tf_op jit(solution)/shard_map/all_to_all | solution.py:157
  11.8 6.2 %collective-permute-start.2 = (s32[2,8,8]{2,1,0:T(8,128)S(1)}, s32[2,8,8]{2,1,0:T(8,128)S(1)}, u32[]{:S(2)}, u32[]{:S(2)}) collective-permute-start(s32[2,8,8]{2,1,0:T(8,128)S(1)} %get-tuple-element.30), channel_id=1, source_target_pairs={{0,12},{16,19},{1,13},{17,16},{2,14},{18,17},{3,15},{19,18},{4,0},... | collective-permute-start | bytes 1544 | tf_op jit(solution)/shard_map/ppermute | solution.py:139
  15.7 4.0 %collective-permute-start.1 = (s32[2,8,8]{2,1,0:T(8,128)S(1)}, s32[2,8,8]{2,1,0:T(8,128)S(1)}, u32[]{:S(2)}, u32[]{:S(2)}) collective-permute-start(s32[2,8,8]{2,1,0:T(8,128)S(1)} %get-tuple-element.30), channel_id=1, source_target_pairs={{0,4},{16,17},{1,5},{17,18},{2,6},{18,19},{3,7},{19,16},{4,8},{20,... | collective-permute-start | bytes 1544 | tf_op jit(solution)/shard_map/ppermute | solution.py:139
  15.7 4.0 %collective-permute-start.3 = (s32[2,8,8]{2,1,0:T(8,128)S(1)}, s32[2,8,8]{2,1,0:T(8,128)S(1)}, u32[]{:S(2)}, u32[]{:S(2)}) collective-permute-start(s32[2,8,8]{2,1,0:T(8,128)S(1)} %get-tuple-element.30), channel_id=1, source_target_pairs={{0,8},{16,18},{1,9},{17,19},{2,10},{18,16},{3,11},{19,17},{4,12},{... | collective-permute-start | bytes 1544 | tf_op jit(solution)/shard_map/ppermute | solution.py:139
  28.9 10.1 %collective-permute-start.4 = (bf16[72,16,128]{2,1,0:T(8,128)(2,1)S(1)}, bf16[72,16,128]{2,1,0:T(8,128)(2,1)S(1)}, u32[]{:S(2)}, u32[]{:S(2)}) collective-permute-start(bf16[72,16,128]{2,1,0:T(8,128)(2,1)S(1)} %get-tuple-element.14), channel_id=1, source_target_pairs={{0,4},{16,17},{1,5},{17,18},{2,6},{18,19},{3,7},{19,16},{4,8},{20,... | collective-permute-start | bytes 884744 | tf_op jit(solution)/shard_map/ppermute | solution.py:139
  30.5 14.1 %collective-permute-start.5 = (bf16[72,16,128]{2,1,0:T(8,128)(2,1)S(1)}, bf16[72,16,128]{2,1,0:T(8,128)(2,1)S(1)}, u32[]{:S(2)}, u32[]{:S(2)}) collective-permute-start(bf16[72,16,128]{2,1,0:T(8,128)(2,1)S(1)} %get-tuple-element.15), channel_id=1, source_target_pairs={{0,12},{16,19},{1,13},{17,16},{2,14},{18,17},{3,15},{19,18},{4,0},... | collective-permute-start | bytes 884744 | tf_op jit(solution)/shard_map/ppermute | solution.py:139
  34.7 12.0 %collective-permute-start.6 = (bf16[72,16,128]{2,1,0:T(8,128)(2,1)S(1)}, bf16[72,16,128]{2,1,0:T(8,128)(2,1)S(1)}, u32[]{:S(2)}, u32[]{:S(2)}) collective-permute-start(bf16[72,16,128]{2,1,0:T(8,128)(2,1)S(1)} %get-tuple-element.16), channel_id=1, source_target_pairs={{0,8},{16,18},{1,9},{17,19},{2,10},{18,16},{3,11},{19,17},{4,12},{... | collective-permute-start | bytes 884744 | tf_op jit(solution)/shard_map/ppermute | solution.py:139
  35.8 12.1 %collective-permute-start.7 = (bf16[72,16,128]{2,1,0:T(8,128)(2,1)S(1)}, bf16[72,16,128]{2,1,0:T(8,128)(2,1)S(1)}, u32[]{:S(2)}, u32[]{:S(2)}) collective-permute-start(bf16[72,16,128]{2,1,0:T(8,128)(2,1)S(1)} %get-tuple-element.17), channel_id=1, source_target_pairs={{0,24},{16,2},{1,25},{17,3},{2,26},{18,0},{3,27},{19,1},{4,28},{20... | collective-permute-start | bytes 884744 | tf_op jit(solution)/shard_map/ppermute | solution.py:139
  38.5 12.4 %collective-permute-start.8 = (bf16[72,16,128]{2,1,0:T(8,128)(2,1)S(1)}, bf16[72,16,128]{2,1,0:T(8,128)(2,1)S(1)}, u32[]{:S(2)}, u32[]{:S(2)}) collective-permute-start(bf16[72,16,128]{2,1,0:T(8,128)(2,1)S(1)} %get-tuple-element.18), channel_id=1, source_target_pairs={{0,20},{16,1},{1,21},{17,2},{2,22},{18,3},{3,23},{19,0},{4,24},{20... | collective-permute-start | bytes 884744 | tf_op jit(solution)/shard_map/ppermute | solution.py:139
  39.0 12.0 %collective-permute-start.9 = (bf16[72,16,128]{2,1,0:T(8,128)(2,1)S(1)}, bf16[72,16,128]{2,1,0:T(8,128)(2,1)S(1)}, u32[]{:S(2)}, u32[]{:S(2)}) collective-permute-start(bf16[72,16,128]{2,1,0:T(8,128)(2,1)S(1)} %get-tuple-element.19), channel_id=1, source_target_pairs={{0,28},{16,3},{1,29},{17,0},{2,30},{18,1},{3,31},{19,2},{4,16},{20... | collective-permute-start | bytes 884744 | tf_op jit(solution)/shard_map/ppermute | solution.py:139
  44.7 6.3 %collective-permute-start.10 = (bf16[72,16,128]{2,1,0:T(8,128)(2,1)S(1)}, bf16[72,16,128]{2,1,0:T(8,128)(2,1)S(1)}, u32[]{:S(2)}, u32[]{:S(2)}) collective-permute-start(bf16[72,16,128]{2,1,0:T(8,128)(2,1)S(1)} %get-tuple-element.20), channel_id=1, source_target_pairs={{0,16},{1,17},{2,18},{3,19},{4,20},{5,21},{6,22},{7,23},{8,24},{9,... | collective-permute-start | bytes 884744 | tf_op jit(solution)/shard_map/ppermute | solution.py:139
  51.0 1.4 %copy-start.2 = (bf16[1024,256]{1,0:T(8,128)(2,1)S(1)}, bf16[1024,256]{1,0:T(8,128)(2,1)}, u32[]{:S(2)}) copy-start(bf16[1024,256]{1,0:T(8,128)(2,1)} %cot_ref.1) | copy-start | bytes 1572868

commit v5 on v4

v5 whole, which is shorter than its diff:
```python
import jax
import jax.numpy as jnp
from jax import lax
from jax.experimental import pallas as pl
from jax.experimental.pallas import tpu as pltpu
from jax.sharding import PartitionSpec as P

ALL = ("blk", "feat")
CONTRACT_FIRST = (((0,), (0,)), ((), ()))
CONTRACT_LAST = (((1,), (1,)), ((), ()))
RANGE = range(4)


def device(x, c, y, z):
    return (x * 2 + c) * 16 + y * 4 + z


PLANES = [[device(x, 0, y, z) for x in RANGE for z in RANGE] for y in RANGE]
PLANES += [[device(x, 1, y, z) for x in RANGE for y in RANGE] for z in RANGE]


def ring(step, to_other_core=0):
    pairs = []
    for x in RANGE:
        for y in RANGE:
            for z in RANGE:
                pairs.append((device(x, 0, y, z), device(x, to_other_core, (y + step) % 4, z)))
                pairs.append((device(x, 1, y, z), device(x, 1 - to_other_core, y, (z + step) % 4)))
    return pairs


RIGHT, LEFT, FAR = ring(1), ring(-1), ring(2)
RIGHT_ACROSS, LEFT_ACROSS, FAR_ACROSS = ring(1, 1), ring(-1, 1), ring(2, 1)
OTHER_CORE = [(d, d ^ 16) for d in range(128)]


def spread_kernel(in_ref, out_ref):
    copies, rows, size = out_ref.shape[1:]
    step = 16
    for k in range(in_ref.shape[1] // (step * size)):
        flat = in_ref[0:1, k * step * size : (k + 1) * step * size]
        block = flat.astype(jnp.float32).reshape(step, size).astype(jnp.bfloat16)
        x, first = divmod(k * step, rows)
        for copy in range(copies):
            out_ref[x, copy, first : first + step] = block


def arrange_kernel(place, w_self_ref, w_neigh_ref, columns_ref, out_ref, columns_out_ref, wide_ref, placed_ref):
    columns_out_ref[...] = columns_ref[...]
    depth = w_self_ref.shape[0]
    wide_ref[:depth] = w_self_ref[...].astype(jnp.float32)
    wide_ref[depth:] = w_neigh_ref[...].astype(jnp.float32)
    for s, at, row in feature_rows(place):
        placed_ref[at : at + 1] = wide_ref[pl.ds(s * depth + row, 1)]
    out_ref[...] = placed_ref[...].astype(jnp.bfloat16)


def feature_rows(place):
    for k in range(8):
        first, stride = place[k], place[8 + k]
        for i in range(16):
            at = k // 4 * 128 + k % 4 * 16 + i
            row = first + (i // 4) * 32 + (i % 4) * stride
            yield 0, at, row
            yield 1, at + 64, row


def interleave_kernel(meta, lists, in_ref, w_ref, rows_ref, *out_refs):
    half = rows_ref.shape[0] // 2
    step = 16
    for part in range(2):
        first = ((meta[0] + part) % 2) * half
        for k in range(half // step):
            start = pl.multiple_of(first + k * step, step)
            rows_ref[pl.ds(part * half + k * step, step)] = jnp.swapaxes(
                in_ref[:, pl.ds(start, step), :], 0, 1
            )
    select(meta, lists, rows_ref, out_refs, EARLY)


def select_kernel(meta, lists, rows_ref, *out_refs):
    select(meta, lists, rows_ref, out_refs, LATE)


def select(meta, lists, rows_ref, out_refs, messages):
    half = rows_ref.shape[0] // 2
    blocks, slots = lists.shape[2:]
    for (place, part), out_ref in zip(messages, out_refs):
        for b in range(blocks):
            for t in range(slots):
                out_ref[b * slots + t] = rows_ref[part * half + lists[place, part, b, t]]
            out_ref[blocks * slots + b] = rows_ref[part * half + meta[1 + place] * blocks + b]


EARLY = ((2, 0), (1, 0))
LATE = ((0, 1), (3, 0), (3, 1), (2, 1), (1, 1), (0, 0))


def aggregate(counts, pieces, tiles_ref, both_ref):
    blocks, slots, size, _ = tiles_ref.shape
    depth = both_ref.shape[0] // 2

    def features_of(k):
        return jnp.concatenate([piece[k] for piece in pieces], axis=0)

    for b in range(blocks):
        nodes = slice(b * size, (b + 1) * size)
        both_ref[:depth, nodes] = features_of(blocks * slots + b)
        x = jnp.concatenate([features_of(b * slots + t) for t in range(slots)], axis=1)
        tiles = []
        for t in range(slots):
            tile = tiles_ref[b, t]
            tiles.append(jnp.where(t < counts[b], tile, jnp.zeros_like(tile)))
        gathered = lax.dot_general(
            x, jnp.concatenate(tiles, axis=1), CONTRACT_LAST, preferred_element_type=jnp.float32
        )
        both_ref[depth:, nodes] = gathered.astype(jnp.bfloat16)


def first_half_kernel(counts, *refs):
    tiles_ref, w_ref, both_ref, pre_ref = refs[4:]
    aggregate(counts, refs[:4], tiles_ref, both_ref)
    pre_ref[...] = lax.dot_general(
        both_ref[...], w_ref[:128], CONTRACT_FIRST, preferred_element_type=jnp.float32
    )


def second_half_kernel(counts, place, *refs):
    tiles_ref, w_ref, first_ref, pre_ref, cot_ref, hidden_ref, grad_ref, both_ref = refs[4:]
    aggregate(counts, refs[:4], tiles_ref, both_ref)
    pre = pre_ref[...] + lax.dot_general(
        both_ref[...], w_ref[128:], CONTRACT_FIRST, preferred_element_type=jnp.float32
    )
    s = jax.nn.sigmoid(pre)
    hidden = pre * s
    hidden_ref[...] = hidden.astype(jnp.bfloat16)
    grad_pre = (cot_ref[...].astype(jnp.float32) * (s + hidden * (1.0 - s))).astype(jnp.bfloat16)
    both = jnp.concatenate([first_ref[...], both_ref[...]], axis=0)
    grad = jnp.dot(both, grad_pre, preferred_element_type=jnp.float32)
    for s, at, row in feature_rows(place):
        grad_ref[row, s : s + 1] = grad[at : at + 1]


def finish_kernel(total_ref, grad_self_ref, grad_neigh_ref):
    grad_self_ref[...] = total_ref[:, 0, :].astype(jnp.float32)
    grad_neigh_ref[...] = total_ref[:, 1, :].astype(jnp.float32)


VMEM = pl.BlockSpec(memory_space=pltpu.VMEM)
SMEM = pl.BlockSpec(memory_space=pltpu.SMEM)
HBM = pl.BlockSpec(memory_space=pltpu.HBM)
ANY = pl.BlockSpec(memory_space=pl.ANY)
PARAMS = pltpu.CompilerParams(vmem_limit_bytes=24 * 1024 * 1024)


def send(array, pairs):
    return lax.ppermute(array, ALL, pairs)


def per_device(features, w_self, w_neigh, adjacency_tiles, tile_columns, tile_count, cotangent):
    depth, hidden = w_self.shape
    nodes = cotangent.shape[0]
    blocks, slots, size, _ = adjacency_tiles.shape
    core = lax.axis_index("blk") % 2
    feat = lax.axis_index("feat")
    y, z = feat // 4, feat % 4

    out = pl.pallas_call(
        spread_kernel,
        out_shape=jax.ShapeDtypeStruct((4, 4, 256, size), jnp.bfloat16),
        in_specs=[VMEM],
        out_specs=VMEM,
        compiler_params=PARAMS,
    )(features).reshape(16, 256, size)
    rows = lax.all_to_all(
        out, ALL, split_axis=0, concat_axis=0, tiled=True, axis_index_groups=PLANES
    )
    steps = jnp.array([0, 3, 1, 2], jnp.int32)
    ring_at = jnp.where(core == 0, y, z) + steps
    chip = jnp.where(core == 0, ring_at % 4 * 4 + z, y * 4 + ring_at % 4)
    meta = jnp.concatenate([core[None], chip]).astype(jnp.int32)
    piece_core = jnp.array([0, 0, 0, 1, 0, 1, 1, 1], jnp.int32) ^ core
    piece_at = jnp.where(piece_core == 0, y, z) + jnp.array([0, 3, 1, 0, 2, 2, 3, 1], jnp.int32)
    strides = jnp.where(piece_core == 0, 1, 4)
    first_rows = piece_core * 16 + piece_at % 4 * jnp.where(piece_core == 0, 4, 1)
    place = jnp.concatenate([first_rows, strides]).astype(jnp.int32)
    w, columns = pl.pallas_call(
        arrange_kernel,
        out_shape=(
            jax.ShapeDtypeStruct((2 * depth, hidden), jnp.bfloat16),
            jax.ShapeDtypeStruct(tile_columns.shape, tile_columns.dtype),
        ),
        in_specs=[SMEM, VMEM, VMEM, VMEM],
        out_specs=(VMEM, VMEM),
        scratch_shapes=[pltpu.VMEM((2 * depth, hidden), jnp.float32)] * 2,
        compiler_params=PARAMS,
    )(place, w_self, w_neigh, tile_columns)

    here = jnp.stack([columns, send(columns, OTHER_CORE)])
    lists = jnp.stack([here, send(here, RIGHT), send(here, LEFT), send(here, FAR)])
    listed = blocks * slots + blocks
    piece = jax.ShapeDtypeStruct((listed, 16, size), jnp.bfloat16)
    rows, own_r, own_l = pl.pallas_call(
        interleave_kernel,
        out_shape=(jax.ShapeDtypeStruct((256, 16, size), jnp.bfloat16), piece, piece),
        in_specs=[SMEM, SMEM, VMEM, ANY],
        out_specs=(VMEM,) * 3,
        compiler_params=PARAMS,
    )(meta, lists, rows, w)
    across, own_f, across_f, across_r, across_l, own = pl.pallas_call(
        select_kernel,
        out_shape=(piece,) * 6,
        in_specs=[SMEM, SMEM, VMEM],
        out_specs=(VMEM,) * 6,
        compiler_params=PARAMS,
    )(meta, lists, rows)
    first = [own, send(own_r, RIGHT), send(own_l, LEFT), send(across, OTHER_CORE)]
    second = [send(own_f, FAR), send(across_f, FAR_ACROSS)]
    second += [send(across_r, RIGHT_ACROSS), send(across_l, LEFT_ACROSS)]

    both = jax.ShapeDtypeStruct((depth, nodes), jnp.bfloat16)
    first_both, first_pre = pl.pallas_call(
        first_half_kernel,
        out_shape=(both, jax.ShapeDtypeStruct((nodes, hidden), jnp.float32)),
        in_specs=[SMEM] + [VMEM] * 6,
        out_specs=(VMEM, VMEM),
        compiler_params=PARAMS,
    )(tile_count, *first, adjacency_tiles, w)
    hidden_out, grad = pl.pallas_call(
        second_half_kernel,
        out_shape=(
            jax.ShapeDtypeStruct((nodes, hidden), jnp.bfloat16),
            jax.ShapeDtypeStruct((depth, 2, hidden), jnp.float32),
        ),
        in_specs=[SMEM, SMEM] + [VMEM] * 9,
        out_specs=(VMEM, VMEM),
        scratch_shapes=[pltpu.VMEM(both.shape, both.dtype)],
        compiler_params=PARAMS,
    )(tile_count, place, *second, adjacency_tiles, w, first_both, first_pre, cotangent)
    parts = lax.all_to_all(grad, ALL, split_axis=0, concat_axis=0, tiled=True)
    mine = jnp.sum(parts, axis=0).astype(jnp.bfloat16)
    total = lax.all_to_all(
        jnp.broadcast_to(mine[None], (depth, 2, hidden)), ALL, split_axis=0, concat_axis=0, tiled=True
    )
    summed = jax.ShapeDtypeStruct((depth, hidden), jnp.float32)
    grad_self, grad_neigh = pl.pallas_call(
        finish_kernel,
        out_shape=(summed, summed),
        in_specs=[VMEM],
        out_specs=(VMEM, VMEM),
        compiler_params=PARAMS,
    )(total)
    return hidden_out, grad_self, grad_neigh


def solution(mesh):
    return jax.shard_map(
        per_device,
        mesh=mesh,
        in_specs=(
            P(ALL, None),
            P(),
            P(),
            P(ALL, None, None, None),
            P(ALL, None),
            P(ALL),
            P(ALL, None),
        ),
        out_specs=(P(ALL, None), P(), P()),
        check_vma=False,
    )
```

time: 86.3 us -> 83.6 us (0.969)
  waiting for transfers between devices: 16.1 us -> 13.6 us
  Pallas kernels: 7.74 us -> 9.04 us
    all_to_all x1, waiting for transfers between devices: 6.71 us -> 3.04 us  [per_device(): lax.all_to_all(out, ALL, split_axis=0, concat_axis=0, tiled=True, axis_in...]
    pallas_call x4 -> x6, Pallas kernels: 6.63 us -> 8.94 us  [the longest x1 2.62 us: per_device(): pl.pallas_call(second_half_kernel, out_shape=(jax.ShapeDtypeStruct((nodes...]
    ppermute x11, starting transfers between devices: 20.9 us -> 19.7 us  [send(): return lax.ppermute(array, ALL, pairs)]
    ppermute x11, waiting for transfers between devices: 9.43 us -> 10.5 us  [send(): return lax.ppermute(array, ALL, pairs)]
    pallas_call x1, Pallas kernels: 1.1 us -> 0.1 us  [per_device(): pl.pallas_call(spread_kernel, out_shape=jax.ShapeDtypeStruct((4, 4, 256,...]
    unnamed x20 -> x22, local copies, waits for them, and re-layouts: 2.41 us -> 2.07 us
  transfers between devices with their start and end apart: 12 -> 12, of which waited for: 6 -> 6; matrix products, arithmetic and copies ran while one was open for 1% -> 0% of each run, Pallas kernels for 2% -> 5%
where the time goes in v5:
time: 83.6 us; the launch traced here: 83.4 us
  blocking collectives  30 us (36%)
  starting transfers between devices  27.5 us (33%)
  waiting for transfers between devices  13.6 us (16%)
  Pallas kernels  9.04 us (11%)
  local copies, waits for them, and re-layouts  2.15 us (3%)
    ppermute x11, starting transfers between devices, send(): return lax.ppermute(array, ALL, pairs)  19.7 us
    all_to_all x1, blocking collectives, per_device(): parts = lax.all_to_all(grad, ALL, split_axis=0, concat_axis=0, tiled=True)  15.8 us
    all_to_all x1, blocking collectives, per_device(): lax.all_to_all(jnp.broadcast_to(mine[None], (depth, 2, hidden)), ALL, spl...  14.2 us
    ppermute x11, waiting for transfers between devices, send(): return lax.ppermute(array, ALL, pairs)  10.5 us
    all_to_all x1, starting transfers between devices, per_device(): lax.all_to_all(out, ALL, split_axis=0, concat_axis=0, tiled=True, axis_in...  7.72 us
    all_to_all x1, waiting for transfers between devices, per_device(): lax.all_to_all(out, ALL, split_axis=0, concat_axis=0, tiled=True, axis_in...  3.04 us
    pallas_call x1, Pallas kernels, per_device(): pl.pallas_call(second_half_kernel, out_shape=(jax.ShapeDtypeStruct((nodes...  2.62 us
    unnamed x22, local copies, waits for them, and re-layouts  2.07 us
  transfers between devices with their start and end apart: 12, of which 6 were waited for; matrix products, arithmetic and copies ran while one was open for 0% of the time, Pallas kernels for 5%

profile of v5, /device:TPU:1, one launch (start us, length us, event | category | flops | bytes accessed | tf_op | source)
XLA Modules:
  0.0 83.4 jit_solution(13783165115639615368)
XLA Ops:
  0.7 1.0 %copy-done.2 = bf16[1,131072]{1,0:T(2,128)(2,1)S(1)} copy-done((bf16[1,131072]{1,0:T(2,128)(2,1)S(1)}, bf16[1,131072]{1,0:T(2,128)(2,1)}, u32[]{:S(2)}) %copy-start.2) | copy-done | bytes 262168
  1.8 1.0 %copy-done.1 = bf16[4,4,256,128]{3,2,1,0:T(8,128)(2,1)} copy-done((bf16[4,4,256,128]{3,2,1,0:T(8,128)(2,1)}, bf16[4,4,256,128]{3,2,1,0:T(8,128)(2,1)S(1)}, u32[]{:S(2)}) %copy-start.1) | copy-done | bytes 1048600
  2.8 7.7 %all-to-all-start = ((bf16[16,256,128]{2,1,0:T(8,128)(2,1)}), bf16[16,256,128]{2,1,0:T(8,128)(2,1)S(1)}, u32[]{:S(2)}, u32[]{:S(2)}) async-start(bf16[16,256,128]{2,1,0:T(8,128)(2,1)} %bitcast.9), calls=%async_computation | async-start | bytes 2097152 | tf_op jit(solution)/shard_map/all_to_all | solution.py:175
  10.7 1.0 %shard_map.121 = (bf16[256,256]{1,0:T(8,128)(2,1)S(1)}, s32[8,8]{1,0:T(8,128)S(1)}) custom-call(s32[16]{0:T(128)S(1)} %pad_add_fusion.2.place, bf16[128,256]{1,0:T(8,128)(2,1)S(1)} %copy-done.4, bf16[128,256]{1,0:T(8,128)(2,1)S(1)} %copy-done.5, s32[8,8]{1,0:T(8,128)S(1)} %copy-done.6), custom_call_target="tpu_custom_call" | custom-call | tf_op jit(solution)/shard_map/pallas_call | solution.py:187
  11.7 1.9 %collective-permute-start = (s32[8,8]{1,0:T(8,128)S(1)}, s32[8,8]{1,0:T(8,128)S(1)}, u32[]{:S(2)}, u32[]{:S(2)}) collective-permute-start(s32[8,8]{1,0:T(8,128)S(1)} %get-tuple-element.20), channel_id=1, source_target_pairs={{0,16},{1,17},{2,18},{3,19},{4,20},{5,21},{6,22},{7,23},{8,24},{9,... | collective-permute-start | bytes 776 | tf_op jit(solution)/shard_map/ppermute | solution.py:157
  14.4 2.8 %collective-permute-start.2 = (s32[2,8,8]{2,1,0:T(8,128)S(1)}, s32[2,8,8]{2,1,0:T(8,128)S(1)}, u32[]{:S(2)}, u32[]{:S(2)}) collective-permute-start(s32[2,8,8]{2,1,0:T(8,128)S(1)} %get-tuple-element.38), channel_id=1, source_target_pairs={{0,12},{16,19},{1,13},{17,16},{2,14},{18,17},{3,15},{19,18},{4,0},... | collective-permute-start | bytes 1544 | tf_op jit(solution)/shard_map/ppermute | solution.py:157
  17.2 1.8 %collective-permute-start.3 = (s32[2,8,8]{2,1,0:T(8,128)S(1)}, s32[2,8,8]{2,1,0:T(8,128)S(1)}, u32[]{:S(2)}, u32[]{:S(2)}) collective-permute-start(s32[2,8,8]{2,1,0:T(8,128)S(1)} %get-tuple-element.38), channel_id=1, source_target_pairs={{0,8},{16,18},{1,9},{17,19},{2,10},{18,16},{3,11},{19,17},{4,12},{... | collective-permute-start | bytes 1544 | tf_op jit(solution)/shard_map/ppermute | solution.py:157
  19.0 3.0 %collective-permute-done.1 = s32[2,8,8]{2,1,0:T(8,128)S(1)} collective-permute-done((s32[2,8,8]{2,1,0:T(8,128)S(1)}, s32[2,8,8]{2,1,0:T(8,128)S(1)}, u32[]{:S(2)}, u32[]{:S(2)}) %collective-permute-start.1) | collective-permute-done | bytes 544 | tf_op jit(solution)/shard_map/ppermute | solution.py:157
  22.3 3.0 %all-to-all-done.in_ref = bf16[16,256,128]{2,1,0:T(8,128)(2,1)S(1)} async-done(((bf16[16,256,128]{2,1,0:T(8,128)(2,1)}), bf16[16,256,128]{2,1,0:T(8,128)(2,1)S(1)}, u32[]{:S(2)}, u32[]{:S(2)}) %all-to-all-start) | async-done | bytes 1048608 | tf_op jit(solution)/shard_map/all_to_all | solution.py:175
  25.4 1.5 %shard_map.123 = (bf16[256,16,128]{2,1,0:T(8,128)(2,1)S(1)}, bf16[72,16,128]{2,1,0:T(8,128)(2,1)S(1)}, bf16[72,16,128]{2,1,0:T(8,128)(2,1)S(1)}) custom-call(s32[5]{0:T(128)S(1)} %pad_add_fusion.3.meta, s32[4,2,8,8]{3,2,1,0:T(8,128)S(1)} %pad_add_fusion.lists, bf16[16,256,128]{2,1,0:T(8,128)(2,1)S(1)} %all-to-all-done.in_ref, ...), custom_call_target="tpu_custom_call" | custom-call | tf_op jit(solution)/shard_map/pallas_call | solution.py:203
  26.9 1.7 %collective-permute-start.8 = (bf16[72,16,128]{2,1,0:T(8,128)(2,1)S(1)}, bf16[72,16,128]{2,1,0:T(8,128)(2,1)S(1)}, u32[]{:S(2)}, u32[]{:S(2)}) collective-permute-start(bf16[72,16,128]{2,1,0:T(8,128)(2,1)S(1)} %get-tuple-element.28), channel_id=1, source_target_pairs={{0,4},{16,17},{1,5},{17,18},{2,6},{18,19},{3,7},{19,16},{4,8},{20,... | collective-permute-start | bytes 884744 | tf_op jit(solution)/shard_map/ppermute | solution.py:157
  28.6 2.2 %collective-permute-start.9 = (bf16[72,16,128]{2,1,0:T(8,128)(2,1)S(1)}, bf16[72,16,128]{2,1,0:T(8,128)(2,1)S(1)}, u32[]{:S(2)}, u32[]{:S(2)}) collective-permute-start(bf16[72,16,128]{2,1,0:T(8,128)(2,1)S(1)} %get-tuple-element.29), channel_id=1, source_target_pairs={{0,12},{16,19},{1,13},{17,16},{2,14},{18,17},{3,15},{19,18},{4,0},... | collective-permute-start | bytes 884744 | tf_op jit(solution)/shard_map/ppermute | solution.py:157
  30.8 1.4 %shard_map.124 = (bf16[72,16,128]{2,1,0:T(8,128)(2,1)S(1)}, bf16[72,16,128]{2,1,0:T(8,128)(2,1)S(1)}, bf16[72,16,128]{2,1,0:T(8,128)(2,1)S(1)}, bf16[72,16,128]{...) custom-call(s32[5]{0:T(128)S(1)} %pad_add_fusion.3.meta, ...), custom_call_target="tpu_custom_call" | custom-call | tf_op jit(solution)/shard_map/pallas_call | solution.py:210
  32.2 1.6 %collective-permute-start.4 = (bf16[72,16,128]{2,1,0:T(8,128)(2,1)S(1)}, bf16[72,16,128]{2,1,0:T(8,128)(2,1)S(1)}, u32[]{:S(2)}, u32[]{:S(2)}) collective-permute-start(bf16[72,16,128]{2,1,0:T(8,128)(2,1)S(1)} %get-tuple-element.23), channel_id=1, source_target_pairs={{0,8},{16,18},{1,9},{17,19},{2,10},{18,16},{3,11},{19,17},{4,12},{... | collective-permute-start | bytes 884744 | tf_op jit(solution)/shard_map/ppermute | solution.py:157
  33.7 4.0 %collective-permute-start.10 = (bf16[72,16,128]{2,1,0:T(8,128)(2,1)S(1)}, bf16[72,16,128]{2,1,0:T(8,128)(2,1)S(1)}, u32[]{:S(2)}, u32[]{:S(2)}) collective-permute-start(bf16[72,16,128]{2,1,0:T(8,128)(2,1)S(1)} %get-tuple-element.30), channel_id=1, source_target_pairs={{0,16},{1,17},{2,18},{3,19},{4,20},{5,21},{6,22},{7,23},{8,24},{9,... | collective-permute-start | bytes 884744 | tf_op jit(solution)/shard_map/ppermute | solution.py:157
  37.8 1.1 %collective-permute-start.5 = (bf16[72,16,128]{2,1,0:T(8,128)(2,1)S(1)}, bf16[72,16,128]{2,1,0:T(8,128)(2,1)S(1)}, u32[]{:S(2)}, u32[]{:S(2)}) collective-permute-start(bf16[72,16,128]{2,1,0:T(8,128)(2,1)S(1)} %get-tuple-element.24), channel_id=1, source_target_pairs={{0,24},{16,2},{1,25},{17,3},{2,26},{18,0},{3,27},{19,1},{4,28},{20... | collective-permute-start | bytes 884744 | tf_op jit(solution)/shard_map/ppermute | solution.py:157
  38.8 1.2 %collective-permute-start.6 = (bf16[72,16,128]{2,1,0:T(8,128)(2,1)S(1)}, bf16[72,16,128]{2,1,0:T(8,128)(2,1)S(1)}, u32[]{:S(2)}, u32[]{:S(2)}) collective-permute-start(bf16[72,16,128]{2,1,0:T(8,128)(2,1)S(1)} %get-tuple-element.25), channel_id=1, source_target_pairs={{0,20},{16,1},{1,21},{17,2},{2,22},{18,3},{3,23},{19,0},{4,24},{20... | collective-permute-start | bytes 884744 | tf_op jit(solution)/shard_map/ppermute | solution.py:157
  40.1 1.5 %collective-permute-start.7 = (bf16[72,16,128]{2,1,0:T(8,128)(2,1)S(1)}, bf16[72,16,128]{2,1,0:T(8,128)(2,1)S(1)}, u32[]{:S(2)}, u32[]{:S(2)}) collective-permute-start(bf16[72,16,128]{2,1,0:T(8,128)(2,1)S(1)} %get-tuple-element.26), channel_id=1, source_target_pairs={{0,28},{16,3},{1,29},{17,0},{2,30},{18,1},{3,31},{19,2},{4,16},{20... | collective-permute-start | bytes 884744 | tf_op jit(solution)/shard_map/ppermute | solution.py:157
  41.6 1.7 %shard_map.125 = (bf16[128,1024]{1,0:T(8,128)(2,1)S(1)}, f32[1024,256]{1,0:T(8,128)S(1)}) custom-call(s32[8]{0:T(128)S(1)} %copy-done.7, bf16[72,16,128]{2,1,0:T(8,128)(2,1)S(1)} %get-tuple-element.27.refs_0_, bf16[72,16,128]{2,1,0:T(8,128)(2,1)S(1)} %collective-permute-done.8.refs_1_, bf16[72,16,128]{2,1,0:T(8,128)(2,1)S(1)} %collective-permute-done.9.refs_2_, ...), custom_call_target="tpu_custom_call" | custom-call | tf_op jit(solution)/shard_map/pallas_call | solution.py:222
  43.2 3.4 %collective-permute-done.5.refs_1_ = bf16[72,16,128]{2,1,0:T(8,128)(2,1)S(1)} collective-permute-done((bf16[72,16,128]{2,1,0:T(8,128)(2,1)S(1)}, bf16[72,16,128]{2,1,0:T(8,128)(2,1)S(1)}, u32[]{:S(2)}, u32[]{:S(2)}) %collective-permute-start.5) | collective-permute-done | bytes 294944 | tf_op jit(solution)/shard_map/ppermute | solution.py:157
  46.6 3.1 %collective-permute-done.6.refs_2_ = bf16[72,16,128]{2,1,0:T(8,128)(2,1)S(1)} collective-permute-done((bf16[72,16,128]{2,1,0:T(8,128)(2,1)S(1)}, bf16[72,16,128]{2,1,0:T(8,128)(2,1)S(1)}, u32[]{:S(2)}, u32[]{:S(2)}) %collective-permute-start.6) | collective-permute-done | bytes 294944 | tf_op jit(solution)/shard_map/ppermute | solution.py:157
  49.7 2.6 %shard_map.126 = (bf16[1024,256]{1,0:T(8,128)(2,1)}, f32[128,2,256]{2,1,0:T(2,128)S(1)}) custom-call(s32[8]{0:T(128)S(1)} %copy-done.7, s32[16]{0:T(128)S(1)} %pad_add_fusion.2.place, bf16[72,16,128]{2,1,0:T(8,128)(2,1)S(1)} %collective-permute-done.4.refs_0_, bf16[72,16,128]{2,1,0:T(8,128)(2,1)S(1)} %collective-permute-done.5.refs_1_, ...), custom_call_target="tpu_custom_call" | custom-call | tf_op jit(solution)/shard_map/pallas_call | solution.py:229
  52.3 15.8 %all_to_all.15 = f32[128,2,256]{2,1,0:T(2,128)S(1)} all-to-all(f32[128,2,256]{2,1,0:T(2,128)S(1)} %get-tuple-element.34), channel_id=1, replica_groups=mesh['blk'=8,'feat'=16] {'blk','feat'}, dimensions={0} | all-to-all | bytes 524288 | tf_op jit(solution)/shard_map/all_to_all | solution.py:240
  68.3 14.2 %all_to_all.16.total_ref = bf16[128,2,256]{2,1,0:T(2,128)(2,1)S(1)} all-to-all(bf16[128,2,256]{2,1,0:T(2,128)(2,1)S(1)} %broadcast_in_dim.29), channel_id=1, replica_groups=mesh['blk'=8,'feat'=16] {'blk','feat'}, dimensions={0} | all-to-all | bytes 262144 | tf_op jit(solution)/shard_map/all_to_all | solution.py:242
  (39 shorter events, 2.5 us)
Async XLA Ops:
  0.6 9.9 %copy-start.8 = (s32[8]{0:T(128)S(1)}, s32[8]{0:T(128)}, u32[]{:S(2)}) copy-start(s32[8]{0:T(128)} %constant.78.clone) | copy-start | bytes 100
  0.6 9.9 %copy-start.9 = (s32[8]{0:T(128)S(1)}, s32[8]{0:T(128)}, u32[]{:S(2)}) copy-start(s32[8]{0:T(128)} %constant.77.clone) | copy-start | bytes 100
  0.7 12.9 %copy-start.10 = (s32[4]{0:T(128)S(1)}, s32[4]{0:T(128)}, u32[]{:S(2)}) copy-start(s32[4]{0:T(128)} %constant.76.clone) | copy-start | bytes 52
  0.7 1.1 %copy-start.2 = (bf16[1,131072]{1,0:T(2,128)(2,1)S(1)}, bf16[1,131072]{1,0:T(2,128)(2,1)}, u32[]{:S(2)}) copy-start(bf16[1,131072]{1,0:T(2,128)(2,1)} %in_ref.1) | copy-start | bytes 786436
  1.7 9.0 %copy-start.4 = (bf16[128,256]{1,0:T(8,128)(2,1)S(1)}, bf16[128,256]{1,0:T(8,128)(2,1)}, u32[]{:S(2)}) copy-start(bf16[128,256]{1,0:T(8,128)(2,1)} %w_self_ref.1) | copy-start | bytes 196612
  1.7 9.0 %copy-start.5 = (bf16[128,256]{1,0:T(8,128)(2,1)S(1)}, bf16[128,256]{1,0:T(8,128)(2,1)}, u32[]{:S(2)}) copy-start(bf16[128,256]{1,0:T(8,128)(2,1)} %w_neigh_ref.1) | copy-start | bytes 196612
  1.7 9.0 %copy-start.6 = (s32[8,8]{1,0:T(8,128)S(1)}, s32[8,8]{1,0:T(8,128)}, u32[]{:S(2)}) copy-start(s32[8,8]{1,0:T(8,128)} %columns_ref.1) | copy-start | bytes 772
  1.8 1.0 %copy-start.1 = (bf16[4,4,256,128]{3,2,1,0:T(8,128)(2,1)}, bf16[4,4,256,128]{3,2,1,0:T(8,128)(2,1)S(1)}, u32[]{:S(2)}) copy-start(bf16[4,4,256,128]{3,2,1,0:T(8,128)(2,1)S(1)} %shard_map.122) | copy-start | bytes 3145732
  2.8 38.7 %copy-start = (bf16[8,8,128,128]{3,2,1,0:T(8,128)(2,1)S(1)}, bf16[8,8,128,128]{3,2,1,0:T(8,128)(2,1)}, u32[]{:S(2)}) copy-start(bf16[8,8,128,128]{3,2,1,0:T(8,128)(2,1)} %refs_4_.3) | copy-start | bytes 6291460
  2.8 38.7 %copy-start.7 = (s32[8]{0:T(128)S(1)}, s32[8]{0:T(128)}, u32[]{:S(2)}) copy-start(s32[8]{0:T(128)} %counts.3) | copy-start | bytes 100
  2.8 22.5 %all-to-all-start = ((bf16[16,256,128]{2,1,0:T(8,128)(2,1)}), bf16[16,256,128]{2,1,0:T(8,128)(2,1)S(1)}, u32[]{:S(2)}, u32[]{:S(2)}) async-start(bf16[16,256,128]{2,1,0:T(8,128)(2,1)} %bitcast.9), calls=%async_computation | async-start | bytes 2097152 | tf_op jit(solution)/shard_map/all_to_all | solution.py:175
  11.7 2.7 %collective-permute-start = (s32[8,8]{1,0:T(8,128)S(1)}, s32[8,8]{1,0:T(8,128)S(1)}, u32[]{:S(2)}, u32[]{:S(2)}) collective-permute-start(s32[8,8]{1,0:T(8,128)S(1)} %get-tuple-element.20), channel_id=1, source_target_pairs={{0,16},{1,17},{2,18},{3,19},{4,20},{5,21},{6,22},{7,23},{8,24},{9,... | collective-permute-start | bytes 776 | tf_op jit(solution)/shard_map/ppermute | solution.py:157
  14.4 4.7 %collective-permute-start.2 = (s32[2,8,8]{2,1,0:T(8,128)S(1)}, s32[2,8,8]{2,1,0:T(8,128)S(1)}, u32[]{:S(2)}, u32[]{:S(2)}) collective-permute-start(s32[2,8,8]{2,1,0:T(8,128)S(1)} %get-tuple-element.38), channel_id=1, source_target_pairs={{0,12},{16,19},{1,13},{17,16},{2,14},{18,17},{3,15},{19,18},{4,0},... | collective-permute-start | bytes 1544 | tf_op jit(solution)/shard_map/ppermute | solution.py:157
  17.2 4.8 %collective-permute-start.1 = (s32[2,8,8]{2,1,0:T(8,128)S(1)}, s32[2,8,8]{2,1,0:T(8,128)S(1)}, u32[]{:S(2)}, u32[]{:S(2)}) collective-permute-start(s32[2,8,8]{2,1,0:T(8,128)S(1)} %get-tuple-element.38), channel_id=1, source_target_pairs={{0,4},{16,17},{1,5},{17,18},{2,6},{18,19},{3,7},{19,16},{4,8},{20,... | collective-permute-start | bytes 1544 | tf_op jit(solution)/shard_map/ppermute | solution.py:157
  17.2 5.1 %collective-permute-start.3 = (s32[2,8,8]{2,1,0:T(8,128)S(1)}, s32[2,8,8]{2,1,0:T(8,128)S(1)}, u32[]{:S(2)}, u32[]{:S(2)}) collective-permute-start(s32[2,8,8]{2,1,0:T(8,128)S(1)} %get-tuple-element.38), channel_id=1, source_target_pairs={{0,8},{16,18},{1,9},{17,19},{2,10},{18,16},{3,11},{19,17},{4,12},{... | collective-permute-start | bytes 1544 | tf_op jit(solution)/shard_map/ppermute | solution.py:157
  26.9 12.0 %collective-permute-start.8 = (bf16[72,16,128]{2,1,0:T(8,128)(2,1)S(1)}, bf16[72,16,128]{2,1,0:T(8,128)(2,1)S(1)}, u32[]{:S(2)}, u32[]{:S(2)}) collective-permute-start(bf16[72,16,128]{2,1,0:T(8,128)(2,1)S(1)} %get-tuple-element.28), channel_id=1, source_target_pairs={{0,4},{16,17},{1,5},{17,18},{2,6},{18,19},{3,7},{19,16},{4,8},{20,... | collective-permute-start | bytes 884744 | tf_op jit(solution)/shard_map/ppermute | solution.py:157
  28.6 11.5 %collective-permute-start.9 = (bf16[72,16,128]{2,1,0:T(8,128)(2,1)S(1)}, bf16[72,16,128]{2,1,0:T(8,128)(2,1)S(1)}, u32[]{:S(2)}, u32[]{:S(2)}) collective-permute-start(bf16[72,16,128]{2,1,0:T(8,128)(2,1)S(1)} %get-tuple-element.29), channel_id=1, source_target_pairs={{0,12},{16,19},{1,13},{17,16},{2,14},{18,17},{3,15},{19,18},{4,0},... | collective-permute-start | bytes 884744 | tf_op jit(solution)/shard_map/ppermute | solution.py:157
  30.8 18.9 %copy-start.3 = (bf16[1024,256]{1,0:T(8,128)(2,1)S(1)}, bf16[1024,256]{1,0:T(8,128)(2,1)}, u32[]{:S(2)}) copy-start(bf16[1024,256]{1,0:T(8,128)(2,1)} %refs_8_.1) | copy-start | bytes 1572868
  32.2 11.1 %collective-permute-start.4 = (bf16[72,16,128]{2,1,0:T(8,128)(2,1)S(1)}, bf16[72,16,128]{2,1,0:T(8,128)(2,1)S(1)}, u32[]{:S(2)}, u32[]{:S(2)}) collective-permute-start(bf16[72,16,128]{2,1,0:T(8,128)(2,1)S(1)} %get-tuple-element.23), channel_id=1, source_target_pairs={{0,8},{16,18},{1,9},{17,19},{2,10},{18,16},{3,11},{19,17},{4,12},{... | collective-permute-start | bytes 884744 | tf_op jit(solution)/shard_map/ppermute | solution.py:157
  33.7 7.8 %collective-permute-start.10 = (bf16[72,16,128]{2,1,0:T(8,128)(2,1)S(1)}, bf16[72,16,128]{2,1,0:T(8,128)(2,1)S(1)}, u32[]{:S(2)}, u32[]{:S(2)}) collective-permute-start(bf16[72,16,128]{2,1,0:T(8,128)(2,1)S(1)} %get-tuple-element.30), channel_id=1, source_target_pairs={{0,16},{1,17},{2,18},{3,19},{4,20},{5,21},{6,22},{7,23},{8,24},{9,... | collective-permute-start | bytes 884744 | tf_op jit(solution)/shard_map/ppermute | solution.py:157
  37.8 8.8 %collective-permute-start.5 = (bf16[72,16,128]{2,1,0:T(8,128)(2,1)S(1)}, bf16[72,16,128]{2,1,0:T(8,128)(2,1)S(1)}, u32[]{:S(2)}, u32[]{:S(2)}) collective-permute-start(bf16[72,16,128]{2,1,0:T(8,128)(2,1)S(1)} %get-tuple-element.24), channel_id=1, source_target_pairs={{0,24},{16,2},{1,25},{17,3},{2,26},{18,0},{3,27},{19,1},{4,28},{20... | collective-permute-start | bytes 884744 | tf_op jit(solution)/shard_map/ppermute | solution.py:157
  38.8 10.8 %collective-permute-start.6 = (bf16[72,16,128]{2,1,0:T(8,128)(2,1)S(1)}, bf16[72,16,128]{2,1,0:T(8,128)(2,1)S(1)}, u32[]{:S(2)}, u32[]{:S(2)}) collective-permute-start(bf16[72,16,128]{2,1,0:T(8,128)(2,1)S(1)} %get-tuple-element.25), channel_id=1, source_target_pairs={{0,20},{16,1},{1,21},{17,2},{2,22},{18,3},{3,23},{19,0},{4,24},{20... | collective-permute-start | bytes 884744 | tf_op jit(solution)/shard_map/ppermute | solution.py:157
  40.1 9.6 %collective-permute-start.7 = (bf16[72,16,128]{2,1,0:T(8,128)(2,1)S(1)}, bf16[72,16,128]{2,1,0:T(8,128)(2,1)S(1)}, u32[]{:S(2)}, u32[]{:S(2)}) collective-permute-start(bf16[72,16,128]{2,1,0:T(8,128)(2,1)S(1)} %get-tuple-element.26), channel_id=1, source_target_pairs={{0,28},{16,3},{1,29},{17,0},{2,30},{18,1},{3,31},{19,2},{4,16},{20... | collective-permute-start | bytes 884744 | tf_op jit(solution)/shard_map/ppermute | solution.py:157

commit v6 on v5

--- a/solution.py
+++ b/solution.py
@@ -45,6 +45,15 @@
             out_ref[x, copy, first : first + step] = block
 
 
+def turn_kernel(counts, tiles_ref, turned_ref):
+    blocks, slots, size, _ = tiles_ref.shape
+    for b in range(blocks):
+        for t in range(slots):
+            tile = tiles_ref[b, t]
+            tile = jnp.where(t < counts[b], tile, jnp.zeros_like(tile))
+            turned_ref[b, t * size : (t + 1) * size] = tile.T
+
+
 def arrange_kernel(place, w_self_ref, w_neigh_ref, columns_ref, out_ref, columns_out_ref, wide_ref, placed_ref):
     columns_out_ref[...] = columns_ref[...]
     depth = w_self_ref.shape[0]
@@ -65,7 +74,8 @@
             yield 1, at + 64, row
 
 
-def interleave_kernel(meta, lists, in_ref, w_ref, rows_ref, *out_refs):
+def select_kernel(meta, lists, in_ref, w_ref, turned_ref, *refs):
+    out_refs, rows_ref = refs[:-1], refs[-1]
     half = rows_ref.shape[0] // 2
     step = 16
     for part in range(2):
@@ -75,29 +85,21 @@
             rows_ref[pl.ds(part * half + k * step, step)] = jnp.swapaxes(
                 in_ref[:, pl.ds(start, step), :], 0, 1
             )
-    select(meta, lists, rows_ref, out_refs, EARLY)
-
-
-def select_kernel(meta, lists, rows_ref, *out_refs):
-    select(meta, lists, rows_ref, out_refs, LATE)
-
-
-def select(meta, lists, rows_ref, out_refs, messages):
-    half = rows_ref.shape[0] // 2
     blocks, slots = lists.shape[2:]
-    for (place, part), out_ref in zip(messages, out_refs):
+    listed = blocks * slots
+    for (place, part), out_ref in zip(MESSAGES, out_refs):
         for b in range(blocks):
             for t in range(slots):
                 out_ref[b * slots + t] = rows_ref[part * half + lists[place, part, b, t]]
-            out_ref[blocks * slots + b] = rows_ref[part * half + meta[1 + place] * blocks + b]
-
-
-EARLY = ((2, 0), (1, 0))
-LATE = ((0, 1), (3, 0), (3, 1), (2, 1), (1, 1), (0, 0))
-
-
-def aggregate(counts, pieces, tiles_ref, both_ref):
-    blocks, slots, size, _ = tiles_ref.shape
+            out_ref[listed + b] = rows_ref[part * half + meta[1 + place] * blocks + b]
+
+
+MESSAGES = ((2, 0), (1, 0), (0, 1), (3, 0), (3, 1), (2, 1), (1, 1), (0, 0))
+
+
+def aggregate(pieces, turned_ref, both_ref):
+    blocks, width, size = turned_ref.shape
+    slots = width // size
     depth = both_ref.shape[0] // 2
 
     def features_of(k):
@@ -107,38 +109,43 @@
         nodes = slice(b * size, (b + 1) * size)
         both_ref[:depth, nodes] = features_of(blocks * slots + b)
         x = jnp.concatenate([features_of(b * slots + t) for t in range(slots)], axis=1)
-        tiles = []
-        for t in range(slots):
-            tile = tiles_ref[b, t]
-            tiles.append(jnp.where(t < counts[b], tile, jnp.zeros_like(tile)))
-        gathered = lax.dot_general(
-            x, jnp.concatenate(tiles, axis=1), CONTRACT_LAST, preferred_element_type=jnp.float32
-        )
+        gathered = jnp.dot(x, turned_ref[b], preferred_element_type=jnp.float32)
         both_ref[depth:, nodes] = gathered.astype(jnp.bfloat16)
 
 
-def first_half_kernel(counts, *refs):
+def first_half_kernel(*refs):
     tiles_ref, w_ref, both_ref, pre_ref = refs[4:]
-    aggregate(counts, refs[:4], tiles_ref, both_ref)
+    aggregate(refs[:4], tiles_ref, both_ref)
     pre_ref[...] = lax.dot_general(
         both_ref[...], w_ref[:128], CONTRACT_FIRST, preferred_element_type=jnp.float32
     )
 
 
-def second_half_kernel(counts, place, *refs):
-    tiles_ref, w_ref, first_ref, pre_ref, cot_ref, hidden_ref, grad_ref, both_ref = refs[4:]
-    aggregate(counts, refs[:4], tiles_ref, both_ref)
-    pre = pre_ref[...] + lax.dot_general(
-        both_ref[...], w_ref[128:], CONTRACT_FIRST, preferred_element_type=jnp.float32
-    )
-    s = jax.nn.sigmoid(pre)
-    hidden = pre * s
-    hidden_ref[...] = hidden.astype(jnp.bfloat16)
-    grad_pre = (cot_ref[...].astype(jnp.float32) * (s + hidden * (1.0 - s))).astype(jnp.bfloat16)
-    both = jnp.concatenate([first_ref[...], both_ref[...]], axis=0)
-    grad = jnp.dot(both, grad_pre, preferred_element_type=jnp.float32)
+def second_half_kernel(place, *refs):
+    tiles_ref, w_ref, first_ref, pre_ref, cot_ref, hidden_hbm, grad_ref, both_ref, hidden_ref, sems = refs[4:]
+    aggregate(refs[:4], tiles_ref, both_ref)
+    nodes = both_ref.shape[1]
+    step = nodes // sems.shape[0]
+    grad = jnp.zeros((2 * both_ref.shape[0], grad_ref.shape[2]), jnp.float32)
+    stores = []
+    for k in range(sems.shape[0]):
+        rows = pl.ds(k * step, step)
+        both = jnp.concatenate([first_ref[:, rows], both_ref[:, rows]], axis=0)
+        pre = pre_ref[rows, :] + lax.dot_general(
+            both_ref[:, rows], w_ref[128:], CONTRACT_FIRST, preferred_element_type=jnp.float32
+        )
+        s = jax.nn.sigmoid(pre)
+        hidden = pre * s
+        hidden_ref[rows, :] = hidden.astype(jnp.bfloat16)
+        stores.append(pltpu.make_async_copy(hidden_ref.at[rows, :], hidden_hbm.at[rows, :], sems.at[k]))
+        stores[-1].start()
+        slope = s + hidden * (1.0 - s)
+        grad_pre = (cot_ref[rows, :].astype(jnp.float32) * slope).astype(jnp.bfloat16)
+        grad += jnp.dot(both, grad_pre, preferred_element_type=jnp.float32)
     for s, at, row in feature_rows(place):
         grad_ref[row, s : s + 1] = grad[at : at + 1]
+    for store in stores:
+        store.wait()
 
 
 def finish_kernel(total_ref, grad_self_ref, grad_neigh_ref):
@@ -180,10 +187,17 @@
     chip = jnp.where(core == 0, ring_at % 4 * 4 + z, y * 4 + ring_at % 4)
     meta = jnp.concatenate([core[None], chip]).astype(jnp.int32)
     piece_core = jnp.array([0, 0, 0, 1, 0, 1, 1, 1], jnp.int32) ^ core
-    piece_at = jnp.where(piece_core == 0, y, z) + jnp.array([0, 3, 1, 0, 2, 2, 3, 1], jnp.int32)
+    piece_at = jnp.where(piece_core == 0, y, z) + jnp.array([0, 3, 1, 3, 2, 2, 1, 0], jnp.int32)
     strides = jnp.where(piece_core == 0, 1, 4)
     first_rows = piece_core * 16 + piece_at % 4 * jnp.where(piece_core == 0, 4, 1)
     place = jnp.concatenate([first_rows, strides]).astype(jnp.int32)
+    turned = pl.pallas_call(
+        turn_kernel,
+        out_shape=jax.ShapeDtypeStruct((blocks, slots * size, size), jnp.bfloat16),
+        in_specs=[SMEM, VMEM],
+        out_specs=VMEM,
+        compiler_params=PARAMS,
+    )(tile_count, adjacency_tiles)
     w, columns = pl.pallas_call(
         arrange_kernel,
         out_shape=(
@@ -200,43 +214,42 @@
     lists = jnp.stack([here, send(here, RIGHT), send(here, LEFT), send(here, FAR)])
     listed = blocks * slots + blocks
     piece = jax.ShapeDtypeStruct((listed, 16, size), jnp.bfloat16)
-    rows, own_r, own_l = pl.pallas_call(
-        interleave_kernel,
-        out_shape=(jax.ShapeDtypeStruct((256, 16, size), jnp.bfloat16), piece, piece),
-        in_specs=[SMEM, SMEM, VMEM, ANY],
-        out_specs=(VMEM,) * 3,
-        compiler_params=PARAMS,
-    )(meta, lists, rows, w)
-    across, own_f, across_f, across_r, across_l, own = pl.pallas_call(
+    own_r, own_l, across, own_f, across_f, across_r, across_l, own = pl.pallas_call(
         select_kernel,
-        out_shape=(piece,) * 6,
-        in_specs=[SMEM, SMEM, VMEM],
-        out_specs=(VMEM,) * 6,
-        compiler_params=PARAMS,
-    )(meta, lists, rows)
-    first = [own, send(own_r, RIGHT), send(own_l, LEFT), send(across, OTHER_CORE)]
+        out_shape=(piece,) * 8,
+        in_specs=[SMEM, SMEM, VMEM, ANY, ANY],
+        out_specs=(VMEM,) * 8,
+        scratch_shapes=[pltpu.VMEM((256, 16, size), jnp.bfloat16)],
+        compiler_params=PARAMS,
+    )(meta, lists, rows, w, turned)
+    first = [own, send(own_r, RIGHT)]
+    first += [send(own_l, LEFT), send(across_r, RIGHT_ACROSS)]
     second = [send(own_f, FAR), send(across_f, FAR_ACROSS)]
-    second += [send(across_r, RIGHT_ACROSS), send(across_l, LEFT_ACROSS)]
+    second += [send(across_l, LEFT_ACROSS), send(across, OTHER_CORE)]
 
     both = jax.ShapeDtypeStruct((depth, nodes), jnp.bfloat16)
     first_both, first_pre = pl.pallas_call(
         first_half_kernel,
         out_shape=(both, jax.ShapeDtypeStruct((nodes, hidden), jnp.float32)),
-        in_specs=[SMEM] + [VMEM] * 6,
+        in_specs=[VMEM] * 6,
         out_specs=(VMEM, VMEM),
         compiler_params=PARAMS,
-    )(tile_count, *first, adjacency_tiles, w)
+    )(*first, turned, w)
     hidden_out, grad = pl.pallas_call(
         second_half_kernel,
         out_shape=(
             jax.ShapeDtypeStruct((nodes, hidden), jnp.bfloat16),
             jax.ShapeDtypeStruct((depth, 2, hidden), jnp.float32),
         ),
-        in_specs=[SMEM, SMEM] + [VMEM] * 9,
-        out_specs=(VMEM, VMEM),
-        scratch_shapes=[pltpu.VMEM(both.shape, both.dtype)],
-        compiler_params=PARAMS,
-    )(tile_count, place, *second, adjacency_tiles, w, first_both, first_pre, cotangent)
+        in_specs=[SMEM] + [VMEM] * 9,
+        out_specs=(ANY, VMEM),
+        scratch_shapes=[
+            pltpu.VMEM(both.shape, both.dtype),
+            pltpu.VMEM((nodes, hidden), jnp.bfloat16),
+            pltpu.SemaphoreType.DMA((2,)),
+        ],
+        compiler_params=PARAMS,
+    )(place, *second, turned, w, first_both, first_pre, cotangent)
     parts = lax.all_to_all(grad, ALL, split_axis=0, concat_axis=0, tiled=True)
     mine = jnp.sum(parts, axis=0).astype(jnp.bfloat16)
     total = lax.all_to_all(

time: 83.6 us -> 83.2 us (level)
  waiting for transfers between devices: 13.6 us -> 8.99 us
  starting transfers between devices: 27.5 us -> 31.4 us
    ppermute x11, waiting for transfers between devices: 10.5 us -> 5.95 us  [send(): return lax.ppermute(array, ALL, pairs)]
    ppermute x11, starting transfers between devices: 19.7 us -> 23.8 us  [send(): return lax.ppermute(array, ALL, pairs)]
    pallas_call x1, Pallas kernels: 0.1 us -> 1.11 us  [per_device(): pl.pallas_call(spread_kernel, out_shape=jax.ShapeDtypeStruct((4, 4, 256,...]
    pallas_call x1, Pallas kernels: 1.66 us -> 0.79 us  [per_device(): pl.pallas_call(first_half_kernel, out_shape=(both, jax.ShapeDtypeStruct((...]
    unnamed x22 -> x20, local copies, waits for them, and re-layouts: 2.07 us -> 2.68 us
  transfers between devices with their start and end apart: 12 -> 12, of which waited for: 6 -> 6; matrix products, arithmetic and copies ran while one was open for 0% -> 0% of each run, Pallas kernels for 5% -> 3%
where the time goes in v6:
time: 83.2 us; the launch traced here: 82.9 us
  starting transfers between devices  31.4 us (38%)
  blocking collectives  29.6 us (36%)
  waiting for transfers between devices  8.99 us (11%)
  Pallas kernels  8.93 us (11%)
  local copies, waits for them, and re-layouts  2.75 us (3%)
    ppermute x11, starting transfers between devices, send(): return lax.ppermute(array, ALL, pairs)  23.8 us
    all_to_all x1, blocking collectives, per_device(): parts = lax.all_to_all(grad, ALL, split_axis=0, concat_axis=0, tiled=True)  15.4 us
    all_to_all x1, blocking collectives, per_device(): lax.all_to_all(jnp.broadcast_to(mine[None], (depth, 2, hidden)), ALL, spl...  14.2 us
    all_to_all x1, starting transfers between devices, per_device(): lax.all_to_all(out, ALL, split_axis=0, concat_axis=0, tiled=True, axis_in...  7.58 us
    ppermute x11, waiting for transfers between devices, send(): return lax.ppermute(array, ALL, pairs)  5.95 us
    all_to_all x1, waiting for transfers between devices, per_device(): lax.all_to_all(out, ALL, split_axis=0, concat_axis=0, tiled=True, axis_in...  3.04 us
    unnamed x20, local copies, waits for them, and re-layouts  2.68 us
    pallas_call x1, Pallas kernels, per_device(): pl.pallas_call(second_half_kernel, out_shape=(jax.ShapeDtypeStruct((nodes...  2.3 us
  transfers between devices with their start and end apart: 12, of which 6 were waited for; matrix products, arithmetic and copies ran while one was open for 0% of the time, Pallas kernels for 3%

profile of v6, /device:TPU:1, one launch (start us, length us, event | category | flops | bytes accessed | tf_op | source)
XLA Modules:
  0.0 82.9 jit_solution(8279259212696508923)
XLA Ops:
  0.7 1.0 %copy-done.1 = bf16[1,131072]{1,0:T(2,128)(2,1)S(1)} copy-done((bf16[1,131072]{1,0:T(2,128)(2,1)S(1)}, bf16[1,131072]{1,0:T(2,128)(2,1)}, u32[]{:S(2)}) %copy-start.1) | copy-done | bytes 262168
  1.7 1.1 %shard_map.122 = bf16[4,4,256,128]{3,2,1,0:T(8,128)(2,1)} custom-call(bf16[1,131072]{1,0:T(2,128)(2,1)S(1)} %copy-done.1), custom_call_target="tpu_custom_call" | custom-call | tf_op jit(solution)/shard_map/pallas_call | solution.py:175
  2.8 7.6 %all-to-all-start = ((bf16[16,256,128]{2,1,0:T(8,128)(2,1)}), bf16[16,256,128]{2,1,0:T(8,128)(2,1)S(1)}, u32[]{:S(2)}, u32[]{:S(2)}) async-start(bf16[16,256,128]{2,1,0:T(8,128)(2,1)} %bitcast.7), calls=%async_computation | async-start | bytes 2097152 | tf_op jit(solution)/shard_map/all_to_all | solution.py:182
  10.6 1.0 %shard_map.121 = (bf16[256,256]{1,0:T(8,128)(2,1)S(1)}, s32[8,8]{1,0:T(8,128)S(1)}) custom-call(s32[16]{0:T(128)S(1)} %pad_add_fusion.2.place, bf16[128,256]{1,0:T(8,128)(2,1)S(1)} %copy-done.3, bf16[128,256]{1,0:T(8,128)(2,1)S(1)} %copy-done.4, s32[8,8]{1,0:T(8,128)S(1)} %copy-done.5), custom_call_target="tpu_custom_call" | custom-call | tf_op jit(solution)/shard_map/pallas_call | solution.py:201
  11.6 1.9 %collective-permute-start = (s32[8,8]{1,0:T(8,128)S(1)}, s32[8,8]{1,0:T(8,128)S(1)}, u32[]{:S(2)}, u32[]{:S(2)}) collective-permute-start(s32[8,8]{1,0:T(8,128)S(1)} %get-tuple-element.19), channel_id=1, source_target_pairs={{0,16},{1,17},{2,18},{3,19},{4,20},{5,21},{6,22},{7,23},{8,24},{9,... | collective-permute-start | bytes 776 | tf_op jit(solution)/shard_map/ppermute | solution.py:164
  13.5 0.8 collective-permute-done
  14.3 2.8 %collective-permute-start.2 = (s32[2,8,8]{2,1,0:T(8,128)S(1)}, s32[2,8,8]{2,1,0:T(8,128)S(1)}, u32[]{:S(2)}, u32[]{:S(2)}) collective-permute-start(s32[2,8,8]{2,1,0:T(8,128)S(1)} %get-tuple-element.36), channel_id=1, source_target_pairs={{0,12},{16,19},{1,13},{17,16},{2,14},{18,17},{3,15},{19,18},{4,0},... | collective-permute-start | bytes 1544 | tf_op jit(solution)/shard_map/ppermute | solution.py:164
  17.1 1.8 %collective-permute-start.3 = (s32[2,8,8]{2,1,0:T(8,128)S(1)}, s32[2,8,8]{2,1,0:T(8,128)S(1)}, u32[]{:S(2)}, u32[]{:S(2)}) collective-permute-start(s32[2,8,8]{2,1,0:T(8,128)S(1)} %get-tuple-element.36), channel_id=1, source_target_pairs={{0,8},{16,18},{1,9},{17,19},{2,10},{18,16},{3,11},{19,17},{4,12},{... | collective-permute-start | bytes 1544 | tf_op jit(solution)/shard_map/ppermute | solution.py:164
  18.9 1.6 %copy-done = bf16[8,8,128,128]{3,2,1,0:T(8,128)(2,1)S(1)} copy-done((bf16[8,8,128,128]{3,2,1,0:T(8,128)(2,1)S(1)}, bf16[8,8,128,128]{3,2,1,0:T(8,128)(2,1)}, u32[]{:S(2)}) %copy-start) | copy-done | bytes 2097176
  20.5 1.1 %shard_map.123.turned_ref.refs_4_ = bf16[8,1024,128]{2,1,0:T(8,128)(2,1)S(1)} custom-call(s32[8]{0:T(128)S(1)} %copy-done.6, bf16[8,8,128,128]{3,2,1,0:T(8,128)(2,1)S(1)} %copy-done), custom_call_target="tpu_custom_call" | custom-call | tf_op jit(solution)/shard_map/pallas_call | solution.py:194
  22.2 3.0 %all-to-all-done.in_ref = bf16[16,256,128]{2,1,0:T(8,128)(2,1)S(1)} async-done(((bf16[16,256,128]{2,1,0:T(8,128)(2,1)}), bf16[16,256,128]{2,1,0:T(8,128)(2,1)S(1)}, u32[]{:S(2)}, u32[]{:S(2)}) %all-to-all-start) | async-done | bytes 1048608 | tf_op jit(solution)/shard_map/all_to_all | solution.py:182
  25.2 1.8 %shard_map.124 = (bf16[72,16,128]{2,1,0:T(8,128)(2,1)S(1)}, bf16[72,16,128]{2,1,0:T(8,128)(2,1)S(1)}, bf16[72,16,128]{2,1,0:T(8,128)(2,1)S(1)}, bf16[72,16,128]{...) custom-call(s32[5]{0:T(128)S(1)} %pad_add_fusion.3.meta, ...), custom_call_target="tpu_custom_call" | custom-call | tf_op jit(solution)/shard_map/pallas_call | solution.py:217
  27.1 1.7 %collective-permute-start.8 = (bf16[72,16,128]{2,1,0:T(8,128)(2,1)S(1)}, bf16[72,16,128]{2,1,0:T(8,128)(2,1)S(1)}, u32[]{:S(2)}, u32[]{:S(2)}) collective-permute-start(bf16[72,16,128]{2,1,0:T(8,128)(2,1)S(1)} %get-tuple-element.26), channel_id=1, source_target_pairs={{0,4},{16,17},{1,5},{17,18},{2,6},{18,19},{3,7},{19,16},{4,8},{20,... | collective-permute-start | bytes 884744 | tf_op jit(solution)/shard_map/ppermute | solution.py:164
  28.8 2.2 %collective-permute-start.9 = (bf16[72,16,128]{2,1,0:T(8,128)(2,1)S(1)}, bf16[72,16,128]{2,1,0:T(8,128)(2,1)S(1)}, u32[]{:S(2)}, u32[]{:S(2)}) collective-permute-start(bf16[72,16,128]{2,1,0:T(8,128)(2,1)S(1)} %get-tuple-element.27), channel_id=1, source_target_pairs={{0,12},{16,19},{1,13},{17,16},{2,14},{18,17},{3,15},{19,18},{4,0},... | collective-permute-start | bytes 884744 | tf_op jit(solution)/shard_map/ppermute | solution.py:164
  31.0 1.5 %collective-permute-start.4 = (bf16[72,16,128]{2,1,0:T(8,128)(2,1)S(1)}, bf16[72,16,128]{2,1,0:T(8,128)(2,1)S(1)}, u32[]{:S(2)}, u32[]{:S(2)}) collective-permute-start(bf16[72,16,128]{2,1,0:T(8,128)(2,1)S(1)} %get-tuple-element.21), channel_id=1, source_target_pairs={{0,8},{16,18},{1,9},{17,19},{2,10},{18,16},{3,11},{19,17},{4,12},{... | collective-permute-start | bytes 884744 | tf_op jit(solution)/shard_map/ppermute | solution.py:164
  32.5 5.1 %collective-permute-start.5 = (bf16[72,16,128]{2,1,0:T(8,128)(2,1)S(1)}, bf16[72,16,128]{2,1,0:T(8,128)(2,1)S(1)}, u32[]{:S(2)}, u32[]{:S(2)}) collective-permute-start(bf16[72,16,128]{2,1,0:T(8,128)(2,1)S(1)} %get-tuple-element.22), channel_id=1, source_target_pairs={{0,24},{16,2},{1,25},{17,3},{2,26},{18,0},{3,27},{19,1},{4,28},{20... | collective-permute-start | bytes 884744 | tf_op jit(solution)/shard_map/ppermute | solution.py:164
  37.6 2.7 %collective-permute-start.6 = (bf16[72,16,128]{2,1,0:T(8,128)(2,1)S(1)}, bf16[72,16,128]{2,1,0:T(8,128)(2,1)S(1)}, u32[]{:S(2)}, u32[]{:S(2)}) collective-permute-start(bf16[72,16,128]{2,1,0:T(8,128)(2,1)S(1)} %get-tuple-element.23), channel_id=1, source_target_pairs={{0,28},{16,3},{1,29},{17,0},{2,30},{18,1},{3,31},{19,2},{4,16},{20... | collective-permute-start | bytes 884744 | tf_op jit(solution)/shard_map/ppermute | solution.py:164
  41.0 4.2 %collective-permute-start.7 = (bf16[72,16,128]{2,1,0:T(8,128)(2,1)S(1)}, bf16[72,16,128]{2,1,0:T(8,128)(2,1)S(1)}, u32[]{:S(2)}, u32[]{:S(2)}) collective-permute-start(bf16[72,16,128]{2,1,0:T(8,128)(2,1)S(1)} %get-tuple-element.24), channel_id=1, source_target_pairs={{0,16},{1,17},{2,18},{3,19},{4,20},{5,21},{6,22},{7,23},{8,24},{9,... | collective-permute-start | bytes 884744 | tf_op jit(solution)/shard_map/ppermute | solution.py:164
  45.1 3.9 %collective-permute-done.10.refs_3_ = bf16[72,16,128]{2,1,0:T(8,128)(2,1)S(1)} collective-permute-done((bf16[72,16,128]{2,1,0:T(8,128)(2,1)S(1)}, bf16[72,16,128]{2,1,0:T(8,128)(2,1)S(1)}, u32[]{:S(2)}, u32[]{:S(2)}) %collective-permute-start.10) | collective-permute-done | bytes 294944 | tf_op jit(solution)/shard_map/ppermute | solution.py:164
  49.1 0.8 shard_map.125
  49.9 2.3 %shard_map.126 = (bf16[1024,256]{1,0:T(8,128)(2,1)}, f32[128,2,256]{2,1,0:T(2,128)S(1)}) custom-call(s32[16]{0:T(128)S(1)} %pad_add_fusion.2.place, bf16[72,16,128]{2,1,0:T(8,128)(2,1)S(1)} %collective-permute-done.4.refs_0_, bf16[72,16,128]{2,1,0:T(8,128)(2,1)S(1)} %collective-permute-done.5.refs_1_, ...), custom_call_target="tpu_custom_call" | custom-call | tf_op jit(solution)/shard_map/pallas_call | solution.py:238
  52.2 15.4 %all_to_all.15 = f32[128,2,256]{2,1,0:T(2,128)S(1)} all-to-all(f32[128,2,256]{2,1,0:T(2,128)S(1)} %get-tuple-element.32), channel_id=1, replica_groups=mesh['blk'=8,'feat'=16] {'blk','feat'}, dimensions={0} | all-to-all | bytes 524288 | tf_op jit(solution)/shard_map/all_to_all | solution.py:253
  67.9 14.2 %all_to_all.16.total_ref = bf16[128,2,256]{2,1,0:T(2,128)(2,1)S(1)} all-to-all(bf16[128,2,256]{2,1,0:T(2,128)(2,1)S(1)} %broadcast_in_dim.29), channel_id=1, replica_groups=mesh['blk'=8,'feat'=16] {'blk','feat'}, dimensions={0} | all-to-all | bytes 262144 | tf_op jit(solution)/shard_map/all_to_all | solution.py:255
  82.1 0.8 shard_map.127
  (37 shorter events, 1.7 us)
Async XLA Ops:
  0.6 9.8 %copy-start.7 = (s32[8]{0:T(128)S(1)}, s32[8]{0:T(128)}, u32[]{:S(2)}) copy-start(s32[8]{0:T(128)} %constant.78.clone) | copy-start | bytes 100
  0.6 9.8 %copy-start.8 = (s32[8]{0:T(128)S(1)}, s32[8]{0:T(128)}, u32[]{:S(2)}) copy-start(s32[8]{0:T(128)} %constant.77.clone) | copy-start | bytes 100
  0.7 12.8 %copy-start.9 = (s32[4]{0:T(128)S(1)}, s32[4]{0:T(128)}, u32[]{:S(2)}) copy-start(s32[4]{0:T(128)} %constant.76.clone) | copy-start | bytes 52
  0.7 1.1 %copy-start.1 = (bf16[1,131072]{1,0:T(2,128)(2,1)S(1)}, bf16[1,131072]{1,0:T(2,128)(2,1)}, u32[]{:S(2)}) copy-start(bf16[1,131072]{1,0:T(2,128)(2,1)} %in_ref.1) | copy-start | bytes 786436
  1.7 8.9 %copy-start.3 = (bf16[128,256]{1,0:T(8,128)(2,1)S(1)}, bf16[128,256]{1,0:T(8,128)(2,1)}, u32[]{:S(2)}) copy-start(bf16[128,256]{1,0:T(8,128)(2,1)} %w_self_ref.1) | copy-start | bytes 196612
  1.7 8.9 %copy-start.4 = (bf16[128,256]{1,0:T(8,128)(2,1)S(1)}, bf16[128,256]{1,0:T(8,128)(2,1)}, u32[]{:S(2)}) copy-start(bf16[128,256]{1,0:T(8,128)(2,1)} %w_neigh_ref.1) | copy-start | bytes 196612
  1.7 8.9 %copy-start.5 = (s32[8,8]{1,0:T(8,128)S(1)}, s32[8,8]{1,0:T(8,128)}, u32[]{:S(2)}) copy-start(s32[8,8]{1,0:T(8,128)} %columns_ref.1) | copy-start | bytes 772
  1.7 17.2 %copy-start.6 = (s32[8]{0:T(128)S(1)}, s32[8]{0:T(128)}, u32[]{:S(2)}) copy-start(s32[8]{0:T(128)} %counts.1) | copy-start | bytes 100
  2.8 22.4 %all-to-all-start = ((bf16[16,256,128]{2,1,0:T(8,128)(2,1)}), bf16[16,256,128]{2,1,0:T(8,128)(2,1)S(1)}, u32[]{:S(2)}, u32[]{:S(2)}) async-start(bf16[16,256,128]{2,1,0:T(8,128)(2,1)} %bitcast.7), calls=%async_computation | async-start | bytes 2097152 | tf_op jit(solution)/shard_map/all_to_all | solution.py:182
  11.6 2.7 %collective-permute-start = (s32[8,8]{1,0:T(8,128)S(1)}, s32[8,8]{1,0:T(8,128)S(1)}, u32[]{:S(2)}, u32[]{:S(2)}) collective-permute-start(s32[8,8]{1,0:T(8,128)S(1)} %get-tuple-element.19), channel_id=1, source_target_pairs={{0,16},{1,17},{2,18},{3,19},{4,20},{5,21},{6,22},{7,23},{8,24},{9,... | collective-permute-start | bytes 776 | tf_op jit(solution)/shard_map/ppermute | solution.py:164
  14.3 7.4 %collective-permute-start.2 = (s32[2,8,8]{2,1,0:T(8,128)S(1)}, s32[2,8,8]{2,1,0:T(8,128)S(1)}, u32[]{:S(2)}, u32[]{:S(2)}) collective-permute-start(s32[2,8,8]{2,1,0:T(8,128)S(1)} %get-tuple-element.36), channel_id=1, source_target_pairs={{0,12},{16,19},{1,13},{17,16},{2,14},{18,17},{3,15},{19,18},{4,0},... | collective-permute-start | bytes 1544 | tf_op jit(solution)/shard_map/ppermute | solution.py:164
  17.1 4.8 %collective-permute-start.1 = (s32[2,8,8]{2,1,0:T(8,128)S(1)}, s32[2,8,8]{2,1,0:T(8,128)S(1)}, u32[]{:S(2)}, u32[]{:S(2)}) collective-permute-start(s32[2,8,8]{2,1,0:T(8,128)S(1)} %get-tuple-element.36), channel_id=1, source_target_pairs={{0,4},{16,17},{1,5},{17,18},{2,6},{18,19},{3,7},{19,16},{4,8},{20,... | collective-permute-start | bytes 1544 | tf_op jit(solution)/shard_map/ppermute | solution.py:164
  17.1 5.1 %collective-permute-start.3 = (s32[2,8,8]{2,1,0:T(8,128)S(1)}, s32[2,8,8]{2,1,0:T(8,128)S(1)}, u32[]{:S(2)}, u32[]{:S(2)}) collective-permute-start(s32[2,8,8]{2,1,0:T(8,128)S(1)} %get-tuple-element.36), channel_id=1, source_target_pairs={{0,8},{16,18},{1,9},{17,19},{2,10},{18,16},{3,11},{19,17},{4,12},{... | collective-permute-start | bytes 1544 | tf_op jit(solution)/shard_map/ppermute | solution.py:164
  18.9 1.6 %copy-start = (bf16[8,8,128,128]{3,2,1,0:T(8,128)(2,1)S(1)}, bf16[8,8,128,128]{3,2,1,0:T(8,128)(2,1)}, u32[]{:S(2)}) copy-start(bf16[8,8,128,128]{3,2,1,0:T(8,128)(2,1)} %tiles_ref.1) | copy-start | bytes 6291460
  27.1 22.8 %copy-start.2 = (bf16[1024,256]{1,0:T(8,128)(2,1)S(1)}, bf16[1024,256]{1,0:T(8,128)(2,1)}, u32[]{:S(2)}) copy-start(bf16[1024,256]{1,0:T(8,128)(2,1)} %refs_8_.1) | copy-start | bytes 1572868
  27.1 10.5 %collective-permute-start.8 = (bf16[72,16,128]{2,1,0:T(8,128)(2,1)S(1)}, bf16[72,16,128]{2,1,0:T(8,128)(2,1)S(1)}, u32[]{:S(2)}, u32[]{:S(2)}) collective-permute-start(bf16[72,16,128]{2,1,0:T(8,128)(2,1)S(1)} %get-tuple-element.26), channel_id=1, source_target_pairs={{0,4},{16,17},{1,5},{17,18},{2,6},{18,19},{3,7},{19,16},{4,8},{20,... | collective-permute-start | bytes 884744 | tf_op jit(solution)/shard_map/ppermute | solution.py:164
  28.8 12.2 %collective-permute-start.9 = (bf16[72,16,128]{2,1,0:T(8,128)(2,1)S(1)}, bf16[72,16,128]{2,1,0:T(8,128)(2,1)S(1)}, u32[]{:S(2)}, u32[]{:S(2)}) collective-permute-start(bf16[72,16,128]{2,1,0:T(8,128)(2,1)S(1)} %get-tuple-element.27), channel_id=1, source_target_pairs={{0,12},{16,19},{1,13},{17,16},{2,14},{18,17},{3,15},{19,18},{4,0},... | collective-permute-start | bytes 884744 | tf_op jit(solution)/shard_map/ppermute | solution.py:164
  31.0 18.9 %collective-permute-start.4 = (bf16[72,16,128]{2,1,0:T(8,128)(2,1)S(1)}, bf16[72,16,128]{2,1,0:T(8,128)(2,1)S(1)}, u32[]{:S(2)}, u32[]{:S(2)}) collective-permute-start(bf16[72,16,128]{2,1,0:T(8,128)(2,1)S(1)} %get-tuple-element.21), channel_id=1, source_target_pairs={{0,8},{16,18},{1,9},{17,19},{2,10},{18,16},{3,11},{19,17},{4,12},{... | collective-permute-start | bytes 884744 | tf_op jit(solution)/shard_map/ppermute | solution.py:164
  32.5 17.4 %collective-permute-start.5 = (bf16[72,16,128]{2,1,0:T(8,128)(2,1)S(1)}, bf16[72,16,128]{2,1,0:T(8,128)(2,1)S(1)}, u32[]{:S(2)}, u32[]{:S(2)}) collective-permute-start(bf16[72,16,128]{2,1,0:T(8,128)(2,1)S(1)} %get-tuple-element.22), channel_id=1, source_target_pairs={{0,24},{16,2},{1,25},{17,3},{2,26},{18,0},{3,27},{19,1},{4,28},{20... | collective-permute-start | bytes 884744 | tf_op jit(solution)/shard_map/ppermute | solution.py:164
  37.6 11.5 %collective-permute-start.10 = (bf16[72,16,128]{2,1,0:T(8,128)(2,1)S(1)}, bf16[72,16,128]{2,1,0:T(8,128)(2,1)S(1)}, u32[]{:S(2)}, u32[]{:S(2)}) collective-permute-start(bf16[72,16,128]{2,1,0:T(8,128)(2,1)S(1)} %get-tuple-element.28), channel_id=1, source_target_pairs={{0,20},{16,1},{1,21},{17,2},{2,22},{18,3},{3,23},{19,0},{4,24},{20... | collective-permute-start | bytes 884744 | tf_op jit(solution)/shard_map/ppermute | solution.py:164
  37.6 12.3 %collective-permute-start.6 = (bf16[72,16,128]{2,1,0:T(8,128)(2,1)S(1)}, bf16[72,16,128]{2,1,0:T(8,128)(2,1)S(1)}, u32[]{:S(2)}, u32[]{:S(2)}) collective-permute-start(bf16[72,16,128]{2,1,0:T(8,128)(2,1)S(1)} %get-tuple-element.23), channel_id=1, source_target_pairs={{0,28},{16,3},{1,29},{17,0},{2,30},{18,1},{3,31},{19,2},{4,16},{20... | collective-permute-start | bytes 884744 | tf_op jit(solution)/shard_map/ppermute | solution.py:164
  41.0 8.9 %collective-permute-start.7 = (bf16[72,16,128]{2,1,0:T(8,128)(2,1)S(1)}, bf16[72,16,128]{2,1,0:T(8,128)(2,1)S(1)}, u32[]{:S(2)}, u32[]{:S(2)}) collective-permute-start(bf16[72,16,128]{2,1,0:T(8,128)(2,1)S(1)} %get-tuple-element.24), channel_id=1, source_target_pairs={{0,16},{1,17},{2,18},{3,19},{4,20},{5,21},{6,22},{7,23},{8,24},{9,... | collective-permute-start | bytes 884744 | tf_op jit(solution)/shard_map/ppermute | solution.py:164

commit v7 on v6

--- a/solution.py
+++ b/solution.py
@@ -15,8 +15,8 @@
     return (x * 2 + c) * 16 + y * 4 + z
 
 
-PLANES = [[device(x, 0, y, z) for x in RANGE for z in RANGE] for y in RANGE]
-PLANES += [[device(x, 1, y, z) for x in RANGE for y in RANGE] for z in RANGE]
+PLANES = [[device(x, 0, y, z) for z in RANGE for x in RANGE] for y in RANGE]
+PLANES += [[device(x, 1, y, z) for y in RANGE for x in RANGE] for z in RANGE]
 
 
 def ring(step, to_other_core=0):
@@ -35,14 +35,14 @@
 
 
 def spread_kernel(in_ref, out_ref):
-    copies, rows, size = out_ref.shape[1:]
+    copies, _, rows, size = out_ref.shape
     step = 16
     for k in range(in_ref.shape[1] // (step * size)):
         flat = in_ref[0:1, k * step * size : (k + 1) * step * size]
         block = flat.astype(jnp.float32).reshape(step, size).astype(jnp.bfloat16)
         x, first = divmod(k * step, rows)
         for copy in range(copies):
-            out_ref[x, copy, first : first + step] = block
+            out_ref[copy, x, first : first + step] = block
 
 
 def turn_kernel(counts, tiles_ref, turned_ref):
@@ -69,7 +69,7 @@
         first, stride = place[k], place[8 + k]
         for i in range(16):
             at = k // 4 * 128 + k % 4 * 16 + i
-            row = first + (i // 4) * 32 + (i % 4) * stride
+            row = first + (i % 4) * 32 + (i // 4) * stride
             yield 0, at, row
             yield 1, at + 64, row
 

time: 83.2 us -> 82.1 us (0.987)
  waiting for transfers between devices: 8.99 us -> 10.9 us
  starting transfers between devices: 31.4 us -> 29.8 us
  blocking collectives: 29.6 us -> 28.3 us
    ppermute x11, starting transfers between devices: 23.8 us -> 22.2 us  [send(): return lax.ppermute(array, ALL, pairs)]
    ppermute x11, waiting for transfers between devices: 5.95 us -> 7.43 us  [send(): return lax.ppermute(array, ALL, pairs)]
    all_to_all x1, blocking collectives: 15.4 us -> 14.1 us  [per_device(): parts = lax.all_to_all(grad, ALL, split_axis=0, concat_axis=0, tiled=True)]
  transfers between devices with their start and end apart: 12 -> 12, of which waited for: 6 -> 5; matrix products, arithmetic and copies ran while one was open for 0% -> 0% of each run, Pallas kernels for 3% -> 4%
where the time goes in v7:
time: 82.1 us; the launch traced here: 81.8 us
  starting transfers between devices  29.8 us (36%)
  blocking collectives  28.3 us (34%)
  waiting for transfers between devices  10.9 us (13%)
  Pallas kernels  8.8 us (11%)
  local copies, waits for them, and re-layouts  2.75 us (3%)
  between operations  0.85 us (1%)
    ppermute x11, starting transfers between devices, send(): return lax.ppermute(array, ALL, pairs)  22.2 us
    all_to_all x1, blocking collectives, per_device(): lax.all_to_all(jnp.broadcast_to(mine[None], (depth, 2, hidden)), ALL, spl...  14.2 us
    all_to_all x1, blocking collectives, per_device(): parts = lax.all_to_all(grad, ALL, split_axis=0, concat_axis=0, tiled=True)  14.1 us
    all_to_all x1, starting transfers between devices, per_device(): lax.all_to_all(out, ALL, split_axis=0, concat_axis=0, tiled=True, axis_in...  7.58 us
    ppermute x11, waiting for transfers between devices, send(): return lax.ppermute(array, ALL, pairs)  7.43 us
    all_to_all x1, waiting for transfers between devices, per_device(): lax.all_to_all(out, ALL, split_axis=0, concat_axis=0, tiled=True, axis_in...  3.52 us
    unnamed x20, local copies, waits for them, and re-layouts  2.68 us
    pallas_call x1, Pallas kernels, per_device(): pl.pallas_call(second_half_kernel, out_shape=(jax.ShapeDtypeStruct((nodes...  2.17 us
  transfers between devices with their start and end apart: 12, of which 5 were waited for; matrix products, arithmetic and copies ran while one was open for 0% of the time, Pallas kernels for 4%

profile of v7, /device:TPU:1, one launch (start us, length us, event | category | flops | bytes accessed | tf_op | source)
XLA Modules:
  0.0 81.8 jit_solution(12280285244410635732)
XLA Ops:
  0.7 1.0 %copy-done.1 = bf16[1,131072]{1,0:T(2,128)(2,1)S(1)} copy-done((bf16[1,131072]{1,0:T(2,128)(2,1)S(1)}, bf16[1,131072]{1,0:T(2,128)(2,1)}, u32[]{:S(2)}) %copy-start.1) | copy-done | bytes 262168
  1.7 1.1 %shard_map.122 = bf16[4,4,256,128]{3,2,1,0:T(8,128)(2,1)} custom-call(bf16[1,131072]{1,0:T(2,128)(2,1)S(1)} %copy-done.1), custom_call_target="tpu_custom_call" | custom-call | tf_op jit(solution)/shard_map/pallas_call | solution.py:175
  2.8 7.6 %all-to-all-start = ((bf16[16,256,128]{2,1,0:T(8,128)(2,1)}), bf16[16,256,128]{2,1,0:T(8,128)(2,1)S(1)}, u32[]{:S(2)}, u32[]{:S(2)}) async-start(bf16[16,256,128]{2,1,0:T(8,128)(2,1)} %bitcast.7), calls=%async_computation | async-start | bytes 2097152 | tf_op jit(solution)/shard_map/all_to_all | solution.py:182
  10.6 1.0 %shard_map.121 = (bf16[256,256]{1,0:T(8,128)(2,1)S(1)}, s32[8,8]{1,0:T(8,128)S(1)}) custom-call(s32[16]{0:T(128)S(1)} %pad_add_fusion.2.place, bf16[128,256]{1,0:T(8,128)(2,1)S(1)} %copy-done.3, bf16[128,256]{1,0:T(8,128)(2,1)S(1)} %copy-done.4, s32[8,8]{1,0:T(8,128)S(1)} %copy-done.5), custom_call_target="tpu_custom_call" | custom-call | tf_op jit(solution)/shard_map/pallas_call | solution.py:201
  11.6 1.9 %collective-permute-start = (s32[8,8]{1,0:T(8,128)S(1)}, s32[8,8]{1,0:T(8,128)S(1)}, u32[]{:S(2)}, u32[]{:S(2)}) collective-permute-start(s32[8,8]{1,0:T(8,128)S(1)} %get-tuple-element.19), channel_id=1, source_target_pairs={{0,16},{1,17},{2,18},{3,19},{4,20},{5,21},{6,22},{7,23},{8,24},{9,... | collective-permute-start | bytes 776 | tf_op jit(solution)/shard_map/ppermute | solution.py:164
  13.5 0.8 collective-permute-done
  14.3 2.8 %collective-permute-start.2 = (s32[2,8,8]{2,1,0:T(8,128)S(1)}, s32[2,8,8]{2,1,0:T(8,128)S(1)}, u32[]{:S(2)}, u32[]{:S(2)}) collective-permute-start(s32[2,8,8]{2,1,0:T(8,128)S(1)} %get-tuple-element.36), channel_id=1, source_target_pairs={{0,12},{16,19},{1,13},{17,16},{2,14},{18,17},{3,15},{19,18},{4,0},... | collective-permute-start | bytes 1544 | tf_op jit(solution)/shard_map/ppermute | solution.py:164
  17.1 1.8 %collective-permute-start.3 = (s32[2,8,8]{2,1,0:T(8,128)S(1)}, s32[2,8,8]{2,1,0:T(8,128)S(1)}, u32[]{:S(2)}, u32[]{:S(2)}) collective-permute-start(s32[2,8,8]{2,1,0:T(8,128)S(1)} %get-tuple-element.36), channel_id=1, source_target_pairs={{0,8},{16,18},{1,9},{17,19},{2,10},{18,16},{3,11},{19,17},{4,12},{... | collective-permute-start | bytes 1544 | tf_op jit(solution)/shard_map/ppermute | solution.py:164
  18.9 1.6 %copy-done = bf16[8,8,128,128]{3,2,1,0:T(8,128)(2,1)S(1)} copy-done((bf16[8,8,128,128]{3,2,1,0:T(8,128)(2,1)S(1)}, bf16[8,8,128,128]{3,2,1,0:T(8,128)(2,1)}, u32[]{:S(2)}) %copy-start) | copy-done | bytes 2097176
  20.5 1.1 %shard_map.123.turned_ref.refs_4_ = bf16[8,1024,128]{2,1,0:T(8,128)(2,1)S(1)} custom-call(s32[8]{0:T(128)S(1)} %copy-done.6, bf16[8,8,128,128]{3,2,1,0:T(8,128)(2,1)S(1)} %copy-done), custom_call_target="tpu_custom_call" | custom-call | tf_op jit(solution)/shard_map/pallas_call | solution.py:194
  21.7 3.5 %all-to-all-done.in_ref = bf16[16,256,128]{2,1,0:T(8,128)(2,1)S(1)} async-done(((bf16[16,256,128]{2,1,0:T(8,128)(2,1)}), bf16[16,256,128]{2,1,0:T(8,128)(2,1)S(1)}, u32[]{:S(2)}, u32[]{:S(2)}) %all-to-all-start) | async-done | bytes 1048608 | tf_op jit(solution)/shard_map/all_to_all | solution.py:182
  25.2 1.8 %shard_map.124 = (bf16[72,16,128]{2,1,0:T(8,128)(2,1)S(1)}, bf16[72,16,128]{2,1,0:T(8,128)(2,1)S(1)}, bf16[72,16,128]{2,1,0:T(8,128)(2,1)S(1)}, bf16[72,16,128]{...) custom-call(s32[5]{0:T(128)S(1)} %pad_add_fusion.3.meta, ...), custom_call_target="tpu_custom_call" | custom-call | tf_op jit(solution)/shard_map/pallas_call | solution.py:217
  27.1 2.2 %collective-permute-start.8 = (bf16[72,16,128]{2,1,0:T(8,128)(2,1)S(1)}, bf16[72,16,128]{2,1,0:T(8,128)(2,1)S(1)}, u32[]{:S(2)}, u32[]{:S(2)}) collective-permute-start(bf16[72,16,128]{2,1,0:T(8,128)(2,1)S(1)} %get-tuple-element.26), channel_id=1, source_target_pairs={{0,4},{16,17},{1,5},{17,18},{2,6},{18,19},{3,7},{19,16},{4,8},{20,... | collective-permute-start | bytes 884744 | tf_op jit(solution)/shard_map/ppermute | solution.py:164
  29.2 3.1 %collective-permute-start.9 = (bf16[72,16,128]{2,1,0:T(8,128)(2,1)S(1)}, bf16[72,16,128]{2,1,0:T(8,128)(2,1)S(1)}, u32[]{:S(2)}, u32[]{:S(2)}) collective-permute-start(bf16[72,16,128]{2,1,0:T(8,128)(2,1)S(1)} %get-tuple-element.27), channel_id=1, source_target_pairs={{0,12},{16,19},{1,13},{17,16},{2,14},{18,17},{3,15},{19,18},{4,0},... | collective-permute-start | bytes 884744 | tf_op jit(solution)/shard_map/ppermute | solution.py:164
  32.4 1.1 %collective-permute-start.4 = (bf16[72,16,128]{2,1,0:T(8,128)(2,1)S(1)}, bf16[72,16,128]{2,1,0:T(8,128)(2,1)S(1)}, u32[]{:S(2)}, u32[]{:S(2)}) collective-permute-start(bf16[72,16,128]{2,1,0:T(8,128)(2,1)S(1)} %get-tuple-element.21), channel_id=1, source_target_pairs={{0,8},{16,18},{1,9},{17,19},{2,10},{18,16},{3,11},{19,17},{4,12},{... | collective-permute-start | bytes 884744 | tf_op jit(solution)/shard_map/ppermute | solution.py:164
  33.5 3.0 %collective-permute-start.5 = (bf16[72,16,128]{2,1,0:T(8,128)(2,1)S(1)}, bf16[72,16,128]{2,1,0:T(8,128)(2,1)S(1)}, u32[]{:S(2)}, u32[]{:S(2)}) collective-permute-start(bf16[72,16,128]{2,1,0:T(8,128)(2,1)S(1)} %get-tuple-element.22), channel_id=1, source_target_pairs={{0,24},{16,2},{1,25},{17,3},{2,26},{18,0},{3,27},{19,1},{4,28},{20... | collective-permute-start | bytes 884744 | tf_op jit(solution)/shard_map/ppermute | solution.py:164
  36.7 3.1 %collective-permute-start.6 = (bf16[72,16,128]{2,1,0:T(8,128)(2,1)S(1)}, bf16[72,16,128]{2,1,0:T(8,128)(2,1)S(1)}, u32[]{:S(2)}, u32[]{:S(2)}) collective-permute-start(bf16[72,16,128]{2,1,0:T(8,128)(2,1)S(1)} %get-tuple-element.23), channel_id=1, source_target_pairs={{0,28},{16,3},{1,29},{17,0},{2,30},{18,1},{3,31},{19,2},{4,16},{20... | collective-permute-start | bytes 884744 | tf_op jit(solution)/shard_map/ppermute | solution.py:164
  39.7 2.6 %collective-permute-done.9.refs_2_ = bf16[72,16,128]{2,1,0:T(8,128)(2,1)S(1)} collective-permute-done((bf16[72,16,128]{2,1,0:T(8,128)(2,1)S(1)}, bf16[72,16,128]{2,1,0:T(8,128)(2,1)S(1)}, u32[]{:S(2)}, u32[]{:S(2)}) %collective-permute-start.9) | collective-permute-done | bytes 294944 | tf_op jit(solution)/shard_map/ppermute | solution.py:164
  42.4 3.3 %collective-permute-start.7 = (bf16[72,16,128]{2,1,0:T(8,128)(2,1)S(1)}, bf16[72,16,128]{2,1,0:T(8,128)(2,1)S(1)}, u32[]{:S(2)}, u32[]{:S(2)}) collective-permute-start(bf16[72,16,128]{2,1,0:T(8,128)(2,1)S(1)} %get-tuple-element.24), channel_id=1, source_target_pairs={{0,16},{1,17},{2,18},{3,19},{4,20},{5,21},{6,22},{7,23},{8,24},{9,... | collective-permute-start | bytes 884744 | tf_op jit(solution)/shard_map/ppermute | solution.py:164
  45.6 3.8 %collective-permute-done.10.refs_3_ = bf16[72,16,128]{2,1,0:T(8,128)(2,1)S(1)} collective-permute-done((bf16[72,16,128]{2,1,0:T(8,128)(2,1)S(1)}, bf16[72,16,128]{2,1,0:T(8,128)(2,1)S(1)}, u32[]{:S(2)}, u32[]{:S(2)}) %collective-permute-start.10) | collective-permute-done | bytes 294944 | tf_op jit(solution)/shard_map/ppermute | solution.py:164
  50.3 2.2 %shard_map.126 = (bf16[1024,256]{1,0:T(8,128)(2,1)}, f32[128,2,256]{2,1,0:T(2,128)S(1)}) custom-call(s32[16]{0:T(128)S(1)} %pad_add_fusion.2.place, bf16[72,16,128]{2,1,0:T(8,128)(2,1)S(1)} %collective-permute-done.4.refs_0_, bf16[72,16,128]{2,1,0:T(8,128)(2,1)S(1)} %collective-permute-done.5.refs_1_, ...), custom_call_target="tpu_custom_call" | custom-call | tf_op jit(solution)/shard_map/pallas_call | solution.py:238
  52.5 14.1 %all_to_all.15 = f32[128,2,256]{2,1,0:T(2,128)S(1)} all-to-all(f32[128,2,256]{2,1,0:T(2,128)S(1)} %get-tuple-element.32), channel_id=1, replica_groups=mesh['blk'=8,'feat'=16] {'blk','feat'}, dimensions={0} | all-to-all | bytes 524288 | tf_op jit(solution)/shard_map/all_to_all | solution.py:253
  66.8 14.2 %all_to_all.16.total_ref = bf16[128,2,256]{2,1,0:T(2,128)(2,1)S(1)} all-to-all(bf16[128,2,256]{2,1,0:T(2,128)(2,1)S(1)} %broadcast_in_dim.29), channel_id=1, replica_groups=mesh['blk'=8,'feat'=16] {'blk','feat'}, dimensions={0} | all-to-all | bytes 262144 | tf_op jit(solution)/shard_map/all_to_all | solution.py:255
  81.0 0.8 shard_map.127
  (37 shorter events, 1.5 us)
Async XLA Ops:
  0.6 9.8 %copy-start.7 = (s32[8]{0:T(128)S(1)}, s32[8]{0:T(128)}, u32[]{:S(2)}) copy-start(s32[8]{0:T(128)} %constant.78.clone) | copy-start | bytes 100
  0.6 9.8 %copy-start.8 = (s32[8]{0:T(128)S(1)}, s32[8]{0:T(128)}, u32[]{:S(2)}) copy-start(s32[8]{0:T(128)} %constant.77.clone) | copy-start | bytes 100
  0.7 12.8 %copy-start.9 = (s32[4]{0:T(128)S(1)}, s32[4]{0:T(128)}, u32[]{:S(2)}) copy-start(s32[4]{0:T(128)} %constant.76.clone) | copy-start | bytes 52
  0.7 1.1 %copy-start.1 = (bf16[1,131072]{1,0:T(2,128)(2,1)S(1)}, bf16[1,131072]{1,0:T(2,128)(2,1)}, u32[]{:S(2)}) copy-start(bf16[1,131072]{1,0:T(2,128)(2,1)} %in_ref.1) | copy-start | bytes 786436
  1.7 8.9 %copy-start.3 = (bf16[128,256]{1,0:T(8,128)(2,1)S(1)}, bf16[128,256]{1,0:T(8,128)(2,1)}, u32[]{:S(2)}) copy-start(bf16[128,256]{1,0:T(8,128)(2,1)} %w_self_ref.1) | copy-start | bytes 196612
  1.7 8.9 %copy-start.4 = (bf16[128,256]{1,0:T(8,128)(2,1)S(1)}, bf16[128,256]{1,0:T(8,128)(2,1)}, u32[]{:S(2)}) copy-start(bf16[128,256]{1,0:T(8,128)(2,1)} %w_neigh_ref.1) | copy-start | bytes 196612
  1.7 8.9 %copy-start.5 = (s32[8,8]{1,0:T(8,128)S(1)}, s32[8,8]{1,0:T(8,128)}, u32[]{:S(2)}) copy-start(s32[8,8]{1,0:T(8,128)} %columns_ref.1) | copy-start | bytes 772
  1.7 17.2 %copy-start.6 = (s32[8]{0:T(128)S(1)}, s32[8]{0:T(128)}, u32[]{:S(2)}) copy-start(s32[8]{0:T(128)} %counts.1) | copy-start | bytes 100
  2.8 22.4 %all-to-all-start = ((bf16[16,256,128]{2,1,0:T(8,128)(2,1)}), bf16[16,256,128]{2,1,0:T(8,128)(2,1)S(1)}, u32[]{:S(2)}, u32[]{:S(2)}) async-start(bf16[16,256,128]{2,1,0:T(8,128)(2,1)} %bitcast.7), calls=%async_computation | async-start | bytes 2097152 | tf_op jit(solution)/shard_map/all_to_all | solution.py:182
  11.6 2.7 %collective-permute-start = (s32[8,8]{1,0:T(8,128)S(1)}, s32[8,8]{1,0:T(8,128)S(1)}, u32[]{:S(2)}, u32[]{:S(2)}) collective-permute-start(s32[8,8]{1,0:T(8,128)S(1)} %get-tuple-element.19), channel_id=1, source_target_pairs={{0,16},{1,17},{2,18},{3,19},{4,20},{5,21},{6,22},{7,23},{8,24},{9,... | collective-permute-start | bytes 776 | tf_op jit(solution)/shard_map/ppermute | solution.py:164
  14.3 7.4 %collective-permute-start.2 = (s32[2,8,8]{2,1,0:T(8,128)S(1)}, s32[2,8,8]{2,1,0:T(8,128)S(1)}, u32[]{:S(2)}, u32[]{:S(2)}) collective-permute-start(s32[2,8,8]{2,1,0:T(8,128)S(1)} %get-tuple-element.36), channel_id=1, source_target_pairs={{0,12},{16,19},{1,13},{17,16},{2,14},{18,17},{3,15},{19,18},{4,0},... | collective-permute-start | bytes 1544 | tf_op jit(solution)/shard_map/ppermute | solution.py:164
  17.1 4.6 %collective-permute-start.1 = (s32[2,8,8]{2,1,0:T(8,128)S(1)}, s32[2,8,8]{2,1,0:T(8,128)S(1)}, u32[]{:S(2)}, u32[]{:S(2)}) collective-permute-start(s32[2,8,8]{2,1,0:T(8,128)S(1)} %get-tuple-element.36), channel_id=1, source_target_pairs={{0,4},{16,17},{1,5},{17,18},{2,6},{18,19},{3,7},{19,16},{4,8},{20,... | collective-permute-start | bytes 1544 | tf_op jit(solution)/shard_map/ppermute | solution.py:164
  17.1 4.6 %collective-permute-start.3 = (s32[2,8,8]{2,1,0:T(8,128)S(1)}, s32[2,8,8]{2,1,0:T(8,128)S(1)}, u32[]{:S(2)}, u32[]{:S(2)}) collective-permute-start(s32[2,8,8]{2,1,0:T(8,128)S(1)} %get-tuple-element.36), channel_id=1, source_target_pairs={{0,8},{16,18},{1,9},{17,19},{2,10},{18,16},{3,11},{19,17},{4,12},{... | collective-permute-start | bytes 1544 | tf_op jit(solution)/shard_map/ppermute | solution.py:164
  18.9 1.6 %copy-start = (bf16[8,8,128,128]{3,2,1,0:T(8,128)(2,1)S(1)}, bf16[8,8,128,128]{3,2,1,0:T(8,128)(2,1)}, u32[]{:S(2)}) copy-start(bf16[8,8,128,128]{3,2,1,0:T(8,128)(2,1)} %tiles_ref.1) | copy-start | bytes 6291460
  27.1 23.2 %copy-start.2 = (bf16[1024,256]{1,0:T(8,128)(2,1)S(1)}, bf16[1024,256]{1,0:T(8,128)(2,1)}, u32[]{:S(2)}) copy-start(bf16[1024,256]{1,0:T(8,128)(2,1)} %refs_8_.1) | copy-start | bytes 1572868
  27.1 9.6 %collective-permute-start.8 = (bf16[72,16,128]{2,1,0:T(8,128)(2,1)S(1)}, bf16[72,16,128]{2,1,0:T(8,128)(2,1)S(1)}, u32[]{:S(2)}, u32[]{:S(2)}) collective-permute-start(bf16[72,16,128]{2,1,0:T(8,128)(2,1)S(1)} %get-tuple-element.26), channel_id=1, source_target_pairs={{0,4},{16,17},{1,5},{17,18},{2,6},{18,19},{3,7},{19,16},{4,8},{20,... | collective-permute-start | bytes 884744 | tf_op jit(solution)/shard_map/ppermute | solution.py:164
  29.2 13.1 %collective-permute-start.9 = (bf16[72,16,128]{2,1,0:T(8,128)(2,1)S(1)}, bf16[72,16,128]{2,1,0:T(8,128)(2,1)S(1)}, u32[]{:S(2)}, u32[]{:S(2)}) collective-permute-start(bf16[72,16,128]{2,1,0:T(8,128)(2,1)S(1)} %get-tuple-element.27), channel_id=1, source_target_pairs={{0,12},{16,19},{1,13},{17,16},{2,14},{18,17},{3,15},{19,18},{4,0},... | collective-permute-start | bytes 884744 | tf_op jit(solution)/shard_map/ppermute | solution.py:164
  32.4 17.9 %collective-permute-start.4 = (bf16[72,16,128]{2,1,0:T(8,128)(2,1)S(1)}, bf16[72,16,128]{2,1,0:T(8,128)(2,1)S(1)}, u32[]{:S(2)}, u32[]{:S(2)}) collective-permute-start(bf16[72,16,128]{2,1,0:T(8,128)(2,1)S(1)} %get-tuple-element.21), channel_id=1, source_target_pairs={{0,8},{16,18},{1,9},{17,19},{2,10},{18,16},{3,11},{19,17},{4,12},{... | collective-permute-start | bytes 884744 | tf_op jit(solution)/shard_map/ppermute | solution.py:164
  33.5 16.8 %collective-permute-start.5 = (bf16[72,16,128]{2,1,0:T(8,128)(2,1)S(1)}, bf16[72,16,128]{2,1,0:T(8,128)(2,1)S(1)}, u32[]{:S(2)}, u32[]{:S(2)}) collective-permute-start(bf16[72,16,128]{2,1,0:T(8,128)(2,1)S(1)} %get-tuple-element.22), channel_id=1, source_target_pairs={{0,24},{16,2},{1,25},{17,3},{2,26},{18,0},{3,27},{19,1},{4,28},{20... | collective-permute-start | bytes 884744 | tf_op jit(solution)/shard_map/ppermute | solution.py:164
  36.5 12.9 %collective-permute-start.10 = (bf16[72,16,128]{2,1,0:T(8,128)(2,1)S(1)}, bf16[72,16,128]{2,1,0:T(8,128)(2,1)S(1)}, u32[]{:S(2)}, u32[]{:S(2)}) collective-permute-start(bf16[72,16,128]{2,1,0:T(8,128)(2,1)S(1)} %get-tuple-element.28), channel_id=1, source_target_pairs={{0,20},{16,1},{1,21},{17,2},{2,22},{18,3},{3,23},{19,0},{4,24},{20... | collective-permute-start | bytes 884744 | tf_op jit(solution)/shard_map/ppermute | solution.py:164
  36.7 13.6 %collective-permute-start.6 = (bf16[72,16,128]{2,1,0:T(8,128)(2,1)S(1)}, bf16[72,16,128]{2,1,0:T(8,128)(2,1)S(1)}, u32[]{:S(2)}, u32[]{:S(2)}) collective-permute-start(bf16[72,16,128]{2,1,0:T(8,128)(2,1)S(1)} %get-tuple-element.23), channel_id=1, source_target_pairs={{0,28},{16,3},{1,29},{17,0},{2,30},{18,1},{3,31},{19,2},{4,16},{20... | collective-permute-start | bytes 884744 | tf_op jit(solution)/shard_map/ppermute | solution.py:164
  42.4 7.9 %collective-permute-start.7 = (bf16[72,16,128]{2,1,0:T(8,128)(2,1)S(1)}, bf16[72,16,128]{2,1,0:T(8,128)(2,1)S(1)}, u32[]{:S(2)}, u32[]{:S(2)}) collective-permute-start(bf16[72,16,128]{2,1,0:T(8,128)(2,1)S(1)} %get-tuple-element.24), channel_id=1, source_target_pairs={{0,16},{1,17},{2,18},{3,19},{4,20},{5,21},{6,22},{7,23},{8,24},{9,... | collective-permute-start | bytes 884744 | tf_op jit(solution)/shard_map/ppermute | solution.py:164

commit v8 on v7

--- a/solution.py
+++ b/solution.py
@@ -17,6 +17,8 @@
 
 PLANES = [[device(x, 0, y, z) for z in RANGE for x in RANGE] for y in RANGE]
 PLANES += [[device(x, 1, y, z) for y in RANGE for x in RANGE] for z in RANGE]
+
+EVERYONE = [[device(x, c, y, z) for y in RANGE for z in RANGE for x in RANGE for c in range(2)]]
 
 
 def ring(step, to_other_core=0):
@@ -250,10 +252,13 @@
         ],
         compiler_params=PARAMS,
     )(place, *second, turned, w, first_both, first_pre, cotangent)
-    parts = lax.all_to_all(grad, ALL, split_axis=0, concat_axis=0, tiled=True)
+    parts = lax.all_to_all(
+        grad, ALL, split_axis=0, concat_axis=0, tiled=True, axis_index_groups=EVERYONE
+    )
     mine = jnp.sum(parts, axis=0).astype(jnp.bfloat16)
     total = lax.all_to_all(
-        jnp.broadcast_to(mine[None], (depth, 2, hidden)), ALL, split_axis=0, concat_axis=0, tiled=True
+        jnp.broadcast_to(mine[None], (depth, 2, hidden)), ALL, split_axis=0, concat_axis=0, tiled=True,
+        axis_index_groups=EVERYONE,
     )
     summed = jax.ShapeDtypeStruct((depth, hidden), jnp.float32)
     grad_self, grad_neigh = pl.pallas_call(

time: 82.1 us -> 82 us (level)
  no operation moved by 1% of the time
where the time goes in v8:
time: 82 us; the launch traced here: 81.8 us
  starting transfers between devices  29.8 us (36%)
  blocking collectives  28.3 us (35%)
  waiting for transfers between devices  10.9 us (13%)
  Pallas kernels  8.8 us (11%)
  local copies, waits for them, and re-layouts  2.75 us (3%)
  between operations  0.85 us (1%)
    ppermute x11, starting transfers between devices, send(): return lax.ppermute(array, ALL, pairs)  22.2 us
    all_to_all x1, blocking collectives, per_device(): lax.all_to_all(jnp.broadcast_to(mine[None], (depth, 2, hidden)), ALL, spl...  14.5 us
    all_to_all x1, blocking collectives, per_device(): lax.all_to_all(grad, ALL, split_axis=0, concat_axis=0, tiled=True, axis_i...  13.8 us
    all_to_all x1, starting transfers between devices, per_device(): lax.all_to_all(out, ALL, split_axis=0, concat_axis=0, tiled=True, axis_in...  7.58 us
    ppermute x11, waiting for transfers between devices, send(): return lax.ppermute(array, ALL, pairs)  7.43 us
    all_to_all x1, waiting for transfers between devices, per_device(): lax.all_to_all(out, ALL, split_axis=0, concat_axis=0, tiled=True, axis_in...  3.52 us
    unnamed x20, local copies, waits for them, and re-layouts  2.68 us
    pallas_call x1, Pallas kernels, per_device(): pl.pallas_call(second_half_kernel, out_shape=(jax.ShapeDtypeStruct((nodes...  2.17 us
  transfers between devices with their start and end apart: 12, of which 5 were waited for; matrix products, arithmetic and copies ran while one was open for 0% of the time, Pallas kernels for 4%

profile of v8, /device:TPU:1, one launch (start us, length us, event | category | flops | bytes accessed | tf_op | source)
XLA Modules:
  0.0 81.8 jit_solution(18096711962821932320)
XLA Ops:
  0.7 1.0 %copy-done.1 = bf16[1,131072]{1,0:T(2,128)(2,1)S(1)} copy-done((bf16[1,131072]{1,0:T(2,128)(2,1)S(1)}, bf16[1,131072]{1,0:T(2,128)(2,1)}, u32[]{:S(2)}) %copy-start.1) | copy-done | bytes 262168
  1.7 1.1 %shard_map.122 = bf16[4,4,256,128]{3,2,1,0:T(8,128)(2,1)} custom-call(bf16[1,131072]{1,0:T(2,128)(2,1)S(1)} %copy-done.1), custom_call_target="tpu_custom_call" | custom-call | tf_op jit(solution)/shard_map/pallas_call | solution.py:177
  2.8 7.6 %all-to-all-start = ((bf16[16,256,128]{2,1,0:T(8,128)(2,1)}), bf16[16,256,128]{2,1,0:T(8,128)(2,1)S(1)}, u32[]{:S(2)}, u32[]{:S(2)}) async-start(bf16[16,256,128]{2,1,0:T(8,128)(2,1)} %bitcast.7), calls=%async_computation | async-start | bytes 2097152 | tf_op jit(solution)/shard_map/all_to_all | solution.py:184
  10.6 1.0 %shard_map.121 = (bf16[256,256]{1,0:T(8,128)(2,1)S(1)}, s32[8,8]{1,0:T(8,128)S(1)}) custom-call(s32[16]{0:T(128)S(1)} %pad_add_fusion.2.place, bf16[128,256]{1,0:T(8,128)(2,1)S(1)} %copy-done.3, bf16[128,256]{1,0:T(8,128)(2,1)S(1)} %copy-done.4, s32[8,8]{1,0:T(8,128)S(1)} %copy-done.5), custom_call_target="tpu_custom_call" | custom-call | tf_op jit(solution)/shard_map/pallas_call | solution.py:203
  11.6 1.9 %collective-permute-start = (s32[8,8]{1,0:T(8,128)S(1)}, s32[8,8]{1,0:T(8,128)S(1)}, u32[]{:S(2)}, u32[]{:S(2)}) collective-permute-start(s32[8,8]{1,0:T(8,128)S(1)} %get-tuple-element.19), channel_id=1, source_target_pairs={{0,16},{1,17},{2,18},{3,19},{4,20},{5,21},{6,22},{7,23},{8,24},{9,... | collective-permute-start | bytes 776 | tf_op jit(solution)/shard_map/ppermute | solution.py:166
  13.5 0.8 collective-permute-done
  14.3 2.8 %collective-permute-start.2 = (s32[2,8,8]{2,1,0:T(8,128)S(1)}, s32[2,8,8]{2,1,0:T(8,128)S(1)}, u32[]{:S(2)}, u32[]{:S(2)}) collective-permute-start(s32[2,8,8]{2,1,0:T(8,128)S(1)} %get-tuple-element.36), channel_id=1, source_target_pairs={{0,12},{16,19},{1,13},{17,16},{2,14},{18,17},{3,15},{19,18},{4,0},... | collective-permute-start | bytes 1544 | tf_op jit(solution)/shard_map/ppermute | solution.py:166
  17.1 1.8 %collective-permute-start.3 = (s32[2,8,8]{2,1,0:T(8,128)S(1)}, s32[2,8,8]{2,1,0:T(8,128)S(1)}, u32[]{:S(2)}, u32[]{:S(2)}) collective-permute-start(s32[2,8,8]{2,1,0:T(8,128)S(1)} %get-tuple-element.36), channel_id=1, source_target_pairs={{0,8},{16,18},{1,9},{17,19},{2,10},{18,16},{3,11},{19,17},{4,12},{... | collective-permute-start | bytes 1544 | tf_op jit(solution)/shard_map/ppermute | solution.py:166
  18.9 1.6 %copy-done = bf16[8,8,128,128]{3,2,1,0:T(8,128)(2,1)S(1)} copy-done((bf16[8,8,128,128]{3,2,1,0:T(8,128)(2,1)S(1)}, bf16[8,8,128,128]{3,2,1,0:T(8,128)(2,1)}, u32[]{:S(2)}) %copy-start) | copy-done | bytes 2097176
  20.5 1.1 %shard_map.123.turned_ref.refs_4_ = bf16[8,1024,128]{2,1,0:T(8,128)(2,1)S(1)} custom-call(s32[8]{0:T(128)S(1)} %copy-done.6, bf16[8,8,128,128]{3,2,1,0:T(8,128)(2,1)S(1)} %copy-done), custom_call_target="tpu_custom_call" | custom-call | tf_op jit(solution)/shard_map/pallas_call | solution.py:196
  21.7 3.5 %all-to-all-done.in_ref = bf16[16,256,128]{2,1,0:T(8,128)(2,1)S(1)} async-done(((bf16[16,256,128]{2,1,0:T(8,128)(2,1)}), bf16[16,256,128]{2,1,0:T(8,128)(2,1)S(1)}, u32[]{:S(2)}, u32[]{:S(2)}) %all-to-all-start) | async-done | bytes 1048608 | tf_op jit(solution)/shard_map/all_to_all | solution.py:184
  25.2 1.8 %shard_map.124 = (bf16[72,16,128]{2,1,0:T(8,128)(2,1)S(1)}, bf16[72,16,128]{2,1,0:T(8,128)(2,1)S(1)}, bf16[72,16,128]{2,1,0:T(8,128)(2,1)S(1)}, bf16[72,16,128]{...) custom-call(s32[5]{0:T(128)S(1)} %pad_add_fusion.3.meta, ...), custom_call_target="tpu_custom_call" | custom-call | tf_op jit(solution)/shard_map/pallas_call | solution.py:219
  27.1 2.2 %collective-permute-start.8 = (bf16[72,16,128]{2,1,0:T(8,128)(2,1)S(1)}, bf16[72,16,128]{2,1,0:T(8,128)(2,1)S(1)}, u32[]{:S(2)}, u32[]{:S(2)}) collective-permute-start(bf16[72,16,128]{2,1,0:T(8,128)(2,1)S(1)} %get-tuple-element.26), channel_id=1, source_target_pairs={{0,4},{16,17},{1,5},{17,18},{2,6},{18,19},{3,7},{19,16},{4,8},{20,... | collective-permute-start | bytes 884744 | tf_op jit(solution)/shard_map/ppermute | solution.py:166
  29.2 3.1 %collective-permute-start.9 = (bf16[72,16,128]{2,1,0:T(8,128)(2,1)S(1)}, bf16[72,16,128]{2,1,0:T(8,128)(2,1)S(1)}, u32[]{:S(2)}, u32[]{:S(2)}) collective-permute-start(bf16[72,16,128]{2,1,0:T(8,128)(2,1)S(1)} %get-tuple-element.27), channel_id=1, source_target_pairs={{0,12},{16,19},{1,13},{17,16},{2,14},{18,17},{3,15},{19,18},{4,0},... | collective-permute-start | bytes 884744 | tf_op jit(solution)/shard_map/ppermute | solution.py:166
  32.4 1.1 %collective-permute-start.4 = (bf16[72,16,128]{2,1,0:T(8,128)(2,1)S(1)}, bf16[72,16,128]{2,1,0:T(8,128)(2,1)S(1)}, u32[]{:S(2)}, u32[]{:S(2)}) collective-permute-start(bf16[72,16,128]{2,1,0:T(8,128)(2,1)S(1)} %get-tuple-element.21), channel_id=1, source_target_pairs={{0,8},{16,18},{1,9},{17,19},{2,10},{18,16},{3,11},{19,17},{4,12},{... | collective-permute-start | bytes 884744 | tf_op jit(solution)/shard_map/ppermute | solution.py:166
  33.5 3.0 %collective-permute-start.5 = (bf16[72,16,128]{2,1,0:T(8,128)(2,1)S(1)}, bf16[72,16,128]{2,1,0:T(8,128)(2,1)S(1)}, u32[]{:S(2)}, u32[]{:S(2)}) collective-permute-start(bf16[72,16,128]{2,1,0:T(8,128)(2,1)S(1)} %get-tuple-element.22), channel_id=1, source_target_pairs={{0,24},{16,2},{1,25},{17,3},{2,26},{18,0},{3,27},{19,1},{4,28},{20... | collective-permute-start | bytes 884744 | tf_op jit(solution)/shard_map/ppermute | solution.py:166
  36.7 3.1 %collective-permute-start.6 = (bf16[72,16,128]{2,1,0:T(8,128)(2,1)S(1)}, bf16[72,16,128]{2,1,0:T(8,128)(2,1)S(1)}, u32[]{:S(2)}, u32[]{:S(2)}) collective-permute-start(bf16[72,16,128]{2,1,0:T(8,128)(2,1)S(1)} %get-tuple-element.23), channel_id=1, source_target_pairs={{0,28},{16,3},{1,29},{17,0},{2,30},{18,1},{3,31},{19,2},{4,16},{20... | collective-permute-start | bytes 884744 | tf_op jit(solution)/shard_map/ppermute | solution.py:166
  39.7 2.6 %collective-permute-done.9.refs_2_ = bf16[72,16,128]{2,1,0:T(8,128)(2,1)S(1)} collective-permute-done((bf16[72,16,128]{2,1,0:T(8,128)(2,1)S(1)}, bf16[72,16,128]{2,1,0:T(8,128)(2,1)S(1)}, u32[]{:S(2)}, u32[]{:S(2)}) %collective-permute-start.9) | collective-permute-done | bytes 294944 | tf_op jit(solution)/shard_map/ppermute | solution.py:166
  42.4 3.3 %collective-permute-start.7 = (bf16[72,16,128]{2,1,0:T(8,128)(2,1)S(1)}, bf16[72,16,128]{2,1,0:T(8,128)(2,1)S(1)}, u32[]{:S(2)}, u32[]{:S(2)}) collective-permute-start(bf16[72,16,128]{2,1,0:T(8,128)(2,1)S(1)} %get-tuple-element.24), channel_id=1, source_target_pairs={{0,16},{1,17},{2,18},{3,19},{4,20},{5,21},{6,22},{7,23},{8,24},{9,... | collective-permute-start | bytes 884744 | tf_op jit(solution)/shard_map/ppermute | solution.py:166
  45.6 3.8 %collective-permute-done.10.refs_3_ = bf16[72,16,128]{2,1,0:T(8,128)(2,1)S(1)} collective-permute-done((bf16[72,16,128]{2,1,0:T(8,128)(2,1)S(1)}, bf16[72,16,128]{2,1,0:T(8,128)(2,1)S(1)}, u32[]{:S(2)}, u32[]{:S(2)}) %collective-permute-start.10) | collective-permute-done | bytes 294944 | tf_op jit(solution)/shard_map/ppermute | solution.py:166
  50.3 2.2 %shard_map.126 = (bf16[1024,256]{1,0:T(8,128)(2,1)}, f32[128,2,256]{2,1,0:T(2,128)S(1)}) custom-call(s32[16]{0:T(128)S(1)} %pad_add_fusion.2.place, bf16[72,16,128]{2,1,0:T(8,128)(2,1)S(1)} %collective-permute-done.4.refs_0_, bf16[72,16,128]{2,1,0:T(8,128)(2,1)S(1)} %collective-permute-done.5.refs_1_, ...), custom_call_target="tpu_custom_call" | custom-call | tf_op jit(solution)/shard_map/pallas_call | solution.py:240
  52.5 13.8 %all_to_all.15 = f32[128,2,256]{2,1,0:T(2,128)S(1)} all-to-all(f32[128,2,256]{2,1,0:T(2,128)S(1)} %get-tuple-element.32), channel_id=1, replica_groups={{0,16,32,48,64,80,96,112,1,17,33,49,65,81,97,113,2,18,34,50,66,82,98,11..., dimensions={0} | all-to-all | bytes 524288 | tf_op jit(solution)/shard_map/all_to_all | solution.py:255
  66.5 14.5 %all_to_all.16.total_ref = bf16[128,2,256]{2,1,0:T(2,128)(2,1)S(1)} all-to-all(bf16[128,2,256]{2,1,0:T(2,128)(2,1)S(1)} %broadcast_in_dim.29), channel_id=1, replica_groups={{0,16,32,48,64,80,96,112,1,17,33,49,65,81,97,113,2,18,34,50,66,82,98,11..., dimensions={0} | all-to-all | bytes 262144 | tf_op jit(solution)/shard_map/all_to_all | solution.py:259
  81.0 0.8 shard_map.127
  (37 shorter events, 1.5 us)
Async XLA Ops:
  0.6 9.8 %copy-start.7 = (s32[8]{0:T(128)S(1)}, s32[8]{0:T(128)}, u32[]{:S(2)}) copy-start(s32[8]{0:T(128)} %constant.78.clone) | copy-start | bytes 100
  0.6 9.8 %copy-start.8 = (s32[8]{0:T(128)S(1)}, s32[8]{0:T(128)}, u32[]{:S(2)}) copy-start(s32[8]{0:T(128)} %constant.77.clone) | copy-start | bytes 100
  0.7 12.8 %copy-start.9 = (s32[4]{0:T(128)S(1)}, s32[4]{0:T(128)}, u32[]{:S(2)}) copy-start(s32[4]{0:T(128)} %constant.76.clone) | copy-start | bytes 52
  0.7 1.1 %copy-start.1 = (bf16[1,131072]{1,0:T(2,128)(2,1)S(1)}, bf16[1,131072]{1,0:T(2,128)(2,1)}, u32[]{:S(2)}) copy-start(bf16[1,131072]{1,0:T(2,128)(2,1)} %in_ref.1) | copy-start | bytes 786436
  1.7 8.9 %copy-start.3 = (bf16[128,256]{1,0:T(8,128)(2,1)S(1)}, bf16[128,256]{1,0:T(8,128)(2,1)}, u32[]{:S(2)}) copy-start(bf16[128,256]{1,0:T(8,128)(2,1)} %w_self_ref.1) | copy-start | bytes 196612
  1.7 8.9 %copy-start.4 = (bf16[128,256]{1,0:T(8,128)(2,1)S(1)}, bf16[128,256]{1,0:T(8,128)(2,1)}, u32[]{:S(2)}) copy-start(bf16[128,256]{1,0:T(8,128)(2,1)} %w_neigh_ref.1) | copy-start | bytes 196612
  1.7 8.9 %copy-start.5 = (s32[8,8]{1,0:T(8,128)S(1)}, s32[8,8]{1,0:T(8,128)}, u32[]{:S(2)}) copy-start(s32[8,8]{1,0:T(8,128)} %columns_ref.1) | copy-start | bytes 772
  1.7 17.2 %copy-start.6 = (s32[8]{0:T(128)S(1)}, s32[8]{0:T(128)}, u32[]{:S(2)}) copy-start(s32[8]{0:T(128)} %counts.1) | copy-start | bytes 100
  2.8 22.4 %all-to-all-start = ((bf16[16,256,128]{2,1,0:T(8,128)(2,1)}), bf16[16,256,128]{2,1,0:T(8,128)(2,1)S(1)}, u32[]{:S(2)}, u32[]{:S(2)}) async-start(bf16[16,256,128]{2,1,0:T(8,128)(2,1)} %bitcast.7), calls=%async_computation | async-start | bytes 2097152 | tf_op jit(solution)/shard_map/all_to_all | solution.py:184
  11.6 2.7 %collective-permute-start = (s32[8,8]{1,0:T(8,128)S(1)}, s32[8,8]{1,0:T(8,128)S(1)}, u32[]{:S(2)}, u32[]{:S(2)}) collective-permute-start(s32[8,8]{1,0:T(8,128)S(1)} %get-tuple-element.19), channel_id=1, source_target_pairs={{0,16},{1,17},{2,18},{3,19},{4,20},{5,21},{6,22},{7,23},{8,24},{9,... | collective-permute-start | bytes 776 | tf_op jit(solution)/shard_map/ppermute | solution.py:166
  14.3 7.4 %collective-permute-start.2 = (s32[2,8,8]{2,1,0:T(8,128)S(1)}, s32[2,8,8]{2,1,0:T(8,128)S(1)}, u32[]{:S(2)}, u32[]{:S(2)}) collective-permute-start(s32[2,8,8]{2,1,0:T(8,128)S(1)} %get-tuple-element.36), channel_id=1, source_target_pairs={{0,12},{16,19},{1,13},{17,16},{2,14},{18,17},{3,15},{19,18},{4,0},... | collective-permute-start | bytes 1544 | tf_op jit(solution)/shard_map/ppermute | solution.py:166
  17.1 4.6 %collective-permute-start.1 = (s32[2,8,8]{2,1,0:T(8,128)S(1)}, s32[2,8,8]{2,1,0:T(8,128)S(1)}, u32[]{:S(2)}, u32[]{:S(2)}) collective-permute-start(s32[2,8,8]{2,1,0:T(8,128)S(1)} %get-tuple-element.36), channel_id=1, source_target_pairs={{0,4},{16,17},{1,5},{17,18},{2,6},{18,19},{3,7},{19,16},{4,8},{20,... | collective-permute-start | bytes 1544 | tf_op jit(solution)/shard_map/ppermute | solution.py:166
  17.1 4.6 %collective-permute-start.3 = (s32[2,8,8]{2,1,0:T(8,128)S(1)}, s32[2,8,8]{2,1,0:T(8,128)S(1)}, u32[]{:S(2)}, u32[]{:S(2)}) collective-permute-start(s32[2,8,8]{2,1,0:T(8,128)S(1)} %get-tuple-element.36), channel_id=1, source_target_pairs={{0,8},{16,18},{1,9},{17,19},{2,10},{18,16},{3,11},{19,17},{4,12},{... | collective-permute-start | bytes 1544 | tf_op jit(solution)/shard_map/ppermute | solution.py:166
  18.9 1.6 %copy-start = (bf16[8,8,128,128]{3,2,1,0:T(8,128)(2,1)S(1)}, bf16[8,8,128,128]{3,2,1,0:T(8,128)(2,1)}, u32[]{:S(2)}) copy-start(bf16[8,8,128,128]{3,2,1,0:T(8,128)(2,1)} %tiles_ref.1) | copy-start | bytes 6291460
  27.1 23.2 %copy-start.2 = (bf16[1024,256]{1,0:T(8,128)(2,1)S(1)}, bf16[1024,256]{1,0:T(8,128)(2,1)}, u32[]{:S(2)}) copy-start(bf16[1024,256]{1,0:T(8,128)(2,1)} %refs_8_.1) | copy-start | bytes 1572868
  27.1 9.6 %collective-permute-start.8 = (bf16[72,16,128]{2,1,0:T(8,128)(2,1)S(1)}, bf16[72,16,128]{2,1,0:T(8,128)(2,1)S(1)}, u32[]{:S(2)}, u32[]{:S(2)}) collective-permute-start(bf16[72,16,128]{2,1,0:T(8,128)(2,1)S(1)} %get-tuple-element.26), channel_id=1, source_target_pairs={{0,4},{16,17},{1,5},{17,18},{2,6},{18,19},{3,7},{19,16},{4,8},{20,... | collective-permute-start | bytes 884744 | tf_op jit(solution)/shard_map/ppermute | solution.py:166
  29.2 13.1 %collective-permute-start.9 = (bf16[72,16,128]{2,1,0:T(8,128)(2,1)S(1)}, bf16[72,16,128]{2,1,0:T(8,128)(2,1)S(1)}, u32[]{:S(2)}, u32[]{:S(2)}) collective-permute-start(bf16[72,16,128]{2,1,0:T(8,128)(2,1)S(1)} %get-tuple-element.27), channel_id=1, source_target_pairs={{0,12},{16,19},{1,13},{17,16},{2,14},{18,17},{3,15},{19,18},{4,0},... | collective-permute-start | bytes 884744 | tf_op jit(solution)/shard_map/ppermute | solution.py:166
  32.4 17.9 %collective-permute-start.4 = (bf16[72,16,128]{2,1,0:T(8,128)(2,1)S(1)}, bf16[72,16,128]{2,1,0:T(8,128)(2,1)S(1)}, u32[]{:S(2)}, u32[]{:S(2)}) collective-permute-start(bf16[72,16,128]{2,1,0:T(8,128)(2,1)S(1)} %get-tuple-element.21), channel_id=1, source_target_pairs={{0,8},{16,18},{1,9},{17,19},{2,10},{18,16},{3,11},{19,17},{4,12},{... | collective-permute-start | bytes 884744 | tf_op jit(solution)/shard_map/ppermute | solution.py:166
  33.5 16.8 %collective-permute-start.5 = (bf16[72,16,128]{2,1,0:T(8,128)(2,1)S(1)}, bf16[72,16,128]{2,1,0:T(8,128)(2,1)S(1)}, u32[]{:S(2)}, u32[]{:S(2)}) collective-permute-start(bf16[72,16,128]{2,1,0:T(8,128)(2,1)S(1)} %get-tuple-element.22), channel_id=1, source_target_pairs={{0,24},{16,2},{1,25},{17,3},{2,26},{18,0},{3,27},{19,1},{4,28},{20... | collective-permute-start | bytes 884744 | tf_op jit(solution)/shard_map/ppermute | solution.py:166
  36.5 12.9 %collective-permute-start.10 = (bf16[72,16,128]{2,1,0:T(8,128)(2,1)S(1)}, bf16[72,16,128]{2,1,0:T(8,128)(2,1)S(1)}, u32[]{:S(2)}, u32[]{:S(2)}) collective-permute-start(bf16[72,16,128]{2,1,0:T(8,128)(2,1)S(1)} %get-tuple-element.28), channel_id=1, source_target_pairs={{0,20},{16,1},{1,21},{17,2},{2,22},{18,3},{3,23},{19,0},{4,24},{20... | collective-permute-start | bytes 884744 | tf_op jit(solution)/shard_map/ppermute | solution.py:166
  36.7 13.6 %collective-permute-start.6 = (bf16[72,16,128]{2,1,0:T(8,128)(2,1)S(1)}, bf16[72,16,128]{2,1,0:T(8,128)(2,1)S(1)}, u32[]{:S(2)}, u32[]{:S(2)}) collective-permute-start(bf16[72,16,128]{2,1,0:T(8,128)(2,1)S(1)} %get-tuple-element.23), channel_id=1, source_target_pairs={{0,28},{16,3},{1,29},{17,0},{2,30},{18,1},{3,31},{19,2},{4,16},{20... | collective-permute-start | bytes 884744 | tf_op jit(solution)/shard_map/ppermute | solution.py:166
  42.4 7.9 %collective-permute-start.7 = (bf16[72,16,128]{2,1,0:T(8,128)(2,1)S(1)}, bf16[72,16,128]{2,1,0:T(8,128)(2,1)S(1)}, u32[]{:S(2)}, u32[]{:S(2)}) collective-permute-start(bf16[72,16,128]{2,1,0:T(8,128)(2,1)S(1)} %get-tuple-element.24), channel_id=1, source_target_pairs={{0,16},{1,17},{2,18},{3,19},{4,20},{5,21},{6,22},{7,23},{8,24},{9,... | collective-permute-start | bytes 884744 | tf_op jit(solution)/shard_map/ppermute | solution.py:166
